TPU v7x, 32 devices: a whole 2x2x4 slice. The times are simulated.
32 devices in a mesh: req: 16 (over z, y, core), tp: 2 (over x).
Axes of the slice: x: 2, y: 2, z: 4, core: 2. Of those that a mesh axis runs over, the one named last changes fastest.
Arguments:
- queries: bfloat16 [4096, 5120], P('req', 'tp')
- new_keys: bfloat16 [4096, 5120], P('req', 'tp')
- new_values: bfloat16 [4096, 5120], P('req', 'tp'), may hold values from -6 to 6
- query_gain: float32 [5120], P('tp'), may hold values from 0.1 to 1.9
- key_gain: float32 [5120], P('tp'), may hold values from 0.4 to 2.5
- cache_keys: bfloat16 [1024, 8, 5120], P('req', None, 'tp')
- cache_values: bfloat16 [1024, 8, 5120], P('req', None, 'tp'), may hold values from -6 to 6
- page_table: int32 [16, 48], P('req'), may hold values from 0 to 63, as said below
- cache_lens: int32 [16], P('req'), may hold values from 48 to 384, as said below
- mig_pages: int32 [16, 16], P('req'), may hold values from 0 to 63, as said below
- mig_dest: int32 [256, 1], P('req'), may hold values from 0 to 15; in each aligned block of 16 rows (0 to 15, 16 to 31, ...) at most 2 rows name the same one
- cross_queries: bfloat16 [4096, 5120], P('req', 'tp')
- text_keys: bfloat16 [2048, 5120], P('req', 'tp')
- text_values: bfloat16 [2048, 5120], P('req', 'tp'), may hold values from -6 to 6
- out_weight: bfloat16 [5120, 5120], P('tp', 'req'), may hold values from -0.5 to 0.5
- residual: bfloat16 [4096, 5120], P('req', 'tp')
- gate: bfloat16 [16, 5120], P('req', 'tp'), may hold values from -6 to 6
- shift: bfloat16 [16, 5120], P('req', 'tp'), may hold values from -3 to 3
- scale: bfloat16 [16, 5120], P('req', 'tp'), may hold values from -3 to 3
Outputs:
- stream: bfloat16 [4096, 5120], P('req', 'tp')
- normed: bfloat16 [4096, 5120], P('req', 'tp')
- cross_out: bfloat16 [4096, 5120], P('req', 'tp')
Inputs may be any that keep to these rules, and one draw needn't show every extreme that they name: Row r of page_table and row r of mig_pages together name every one of the 64 pages of row r's pool exactly once. `mig_pages`: see page_table. `cache_lens`: at least 48; the largest is exactly 384. `mig_dest`: among the 16 pages of one request row (the rows of one device) no destination is named more than 2 times.
All inputs are finite; a program needn't handle non-finite values.
Results may differ from a plain program's by a relative error of at most 0.014.
Values may be sent and summed in bfloat16 or wider, within the bound.
No kernel may reach another device: no remote copies, remote signals or barrier semaphores. Data moves between devices by JAX's collectives and lax.ppermute only.
A program may use at most 128 MiB of HBM per device.

v0:
```python
import math

import jax
import jax.numpy as jnp
from jax import lax
from jax.sharding import PartitionSpec as P

HD = 128
CAP = 2


EPS = 1e-06


def attend(query_rows, key_rows, value_rows, usable, head_count):
    row_count = query_rows.shape[0]
    head_width = query_rows.shape[1] // head_count
    query_heads = query_rows.reshape(row_count, head_count, head_width)
    key_heads = key_rows.reshape(key_rows.shape[0], head_count, head_width)
    value_heads = value_rows.reshape(value_rows.shape[0], head_count, head_width)
    scores = jnp.einsum(
        "qhd,khd->hqk", query_heads, key_heads, preferred_element_type=jnp.float32
    ) * (1.0 / math.sqrt(head_width))
    if usable is not None:
        scores = jnp.where(usable[None, None, :], scores, -jnp.inf)
    row_max = jnp.max(scores, axis=2, keepdims=True)
    exponent = jnp.exp(scores - row_max)
    denominator = jnp.sum(exponent, axis=2)
    weights = exponent.astype(jnp.bfloat16)
    mixed = jnp.einsum("hqk,khd->qhd", weights, value_heads, preferred_element_type=jnp.float32)
    mixed = mixed / jnp.transpose(denominator)[:, :, None]
    return mixed.reshape(row_count, head_count * head_width).astype(jnp.bfloat16)


def shards(
    queries,
    new_keys,
    new_values,
    query_gain,
    key_gain,
    cache_keys,
    cache_values,
    page_table,
    cache_lens,
    mig_pages,
    mig_dest,
    cross_queries,
    text_keys,
    text_values,
    out_weight,
    residual,
    gate,
    shift,
    scale,
):
    token_count, local_width = queries.shape
    head_count = local_width // HD
    full_width = local_width * lax.axis_size("tp")
    query_float = queries.astype(jnp.float32)
    key_float = new_keys.astype(jnp.float32)
    query_squares, key_squares = lax.psum(
        (jnp.sum(query_float * query_float, axis=1), jnp.sum(key_float * key_float, axis=1)), "tp"
    )
    query_normed = (
        query_float * lax.rsqrt(query_squares / full_width + EPS)[:, None] * query_gain
    ).astype(jnp.bfloat16)
    key_normed = (key_float * lax.rsqrt(key_squares / full_width + EPS)[:, None] * key_gain).astype(
        jnp.bfloat16
    )
    peer_count = lax.axis_size("req")
    page_len = cache_keys.shape[1]
    destination = mig_dest[:, 0]
    slot_match = (destination[:, None] == jnp.arange(peer_count, dtype=jnp.int32)[None, :]).astype(
        jnp.int32
    )
    position = jnp.sum(jnp.cumsum(slot_match, axis=0) * slot_match, axis=1) - 1
    target_slot = destination * CAP + position
    selection = (
        jnp.arange(peer_count * CAP, dtype=jnp.int32)[:, None] == target_slot[None, :]
    ).astype(jnp.bfloat16)
    moving = mig_pages[0]
    moving_keys = cache_keys[moving].reshape(moving.shape[0], -1)
    moving_values = cache_values[moving].reshape(moving.shape[0], -1)
    sent_keys = (
        jnp.dot(selection, moving_keys, preferred_element_type=jnp.float32)
        .astype(jnp.bfloat16)
        .reshape(peer_count * CAP, page_len, local_width)
    )
    sent_values = (
        jnp.dot(selection, moving_values, preferred_element_type=jnp.float32)
        .astype(jnp.bfloat16)
        .reshape(peer_count * CAP, page_len, local_width)
    )
    slot_filled = jnp.sum(selection.astype(jnp.float32), axis=1)
    sent_flags = jnp.broadcast_to(slot_filled[:, None], (peer_count * CAP, page_len)).astype(
        jnp.bfloat16
    )
    arrived_keys, arrived_values, arrived_flags = (
        lax.all_to_all(sent_keys, "req", split_axis=0, concat_axis=0, tiled=True),
        lax.all_to_all(sent_values, "req", split_axis=0, concat_axis=0, tiled=True),
        lax.all_to_all(sent_flags, "req", split_axis=0, concat_axis=0, tiled=True),
    )
    own_pages = page_table[0]
    resident_keys = cache_keys[own_pages].reshape(-1, local_width)
    resident_values = cache_values[own_pages].reshape(-1, local_width)
    resident_usable = jnp.arange(resident_keys.shape[0], dtype=jnp.int32) < cache_lens[0]
    all_keys = jnp.concatenate(
        [resident_keys, arrived_keys.reshape(-1, local_width), key_normed], axis=0
    )
    all_values = jnp.concatenate(
        [resident_values, arrived_values.reshape(-1, local_width), new_values], axis=0
    )
    usable = jnp.concatenate(
        [resident_usable, arrived_flags.reshape(-1) > 0, jnp.ones((token_count,), bool)]
    )
    attended = attend(query_normed, all_keys, all_values, usable, head_count)
    cross_out = attend(cross_queries, text_keys, text_values, None, head_count)
    partial_rows = jnp.dot(
        attended,
        lax.all_gather(out_weight, "req", axis=1, tiled=True),
        preferred_element_type=jnp.float32,
    )
    projected = lax.psum(partial_rows.astype(jnp.bfloat16), "tp").astype(jnp.float32)
    stream_all, gate_all = (
        lax.all_gather(residual, "tp", axis=1, tiled=True),
        lax.all_gather(gate, "tp", axis=1, tiled=True),
    )
    updated_all = stream_all.astype(jnp.float32) + gate_all.astype(jnp.float32) * projected
    row_mean = jnp.mean(updated_all, axis=1, keepdims=True)
    row_var = jnp.mean(jnp.square(updated_all - row_mean), axis=1, keepdims=True)
    column = lax.axis_index("tp") * local_width
    updated = lax.dynamic_slice_in_dim(updated_all, column, local_width, 1)
    stream = updated.astype(jnp.bfloat16)
    normed = (
        (updated - row_mean) * lax.rsqrt(row_var + EPS) * (1.0 + scale.astype(jnp.float32))
        + shift.astype(jnp.float32)
    ).astype(jnp.bfloat16)
    return (stream, normed, cross_out)


def solution(mesh):
    in_specs = (
        P("req", "tp"),
        P("req", "tp"),
        P("req", "tp"),
        P("tp"),
        P("tp"),
        P("req", None, "tp"),
        P("req", None, "tp"),
        P("req", None),
        P("req"),
        P("req", None),
        P("req", None),
        P("req", "tp"),
        P("req", "tp"),
        P("req", "tp"),
        P("tp", "req"),
        P("req", "tp"),
        P("req", "tp"),
        P("req", "tp"),
        P("req", "tp"),
    )
    out_specs = (P("req", "tp"), P("req", "tp"), P("req", "tp"))
    return jax.shard_map(shards, mesh=mesh, in_specs=in_specs, out_specs=out_specs, check_vma=False)
```

profile of v0, /device:TPU:0, one launch (start us, length us, event | category | flops | bytes accessed | tf_op | source)
XLA Modules:
  0.0 332.1 jit_solution(8869672953466806260)
XLA Ops:
  11.1 7.4 %all-to-all-start.1 = ((bf16[16,2,8]{2,1,0:T(2,128)(2,1)}), bf16[16,2,8]{2,1,0:T(2,128)(2,1)S(1)}, u32[]{:S(2)}, u32[]{:S(2)}) async-start(bf16[16,2,8]{2,1,0:T(2,128)(2,1)} %broadcast_in_dim.15), calls=%async_computation.1 | async-start | bytes 16384 | tf_op jit(solution)/shard_map/all_to_all | solution.py:101
  22.0 2.8 all-to-all-done.1
  24.8 4.4 %all-to-all-start.2 = ((bf16[32,8,2560]{2,1,0:T(8,128)(2,1)}), bf16[32,8,2560]{2,1,0:T(8,128)(2,1)}, u32[]{:S(2)}, u32[]{:S(2)}) async-start(bf16[32,8,2560]{2,1,0:T(8,128)(2,1)} %bitcast.48), calls=%async_computation.2 | async-start | bytes 2621440 | tf_op jit(solution)/shard_map/all_to_all | solution.py:99
  30.0 2.4 copy.50
  37.4 40.1 %all-to-all-done.2 = bf16[32,8,2560]{2,1,0:T(8,128)(2,1)} async-done(((bf16[32,8,2560]{2,1,0:T(8,128)(2,1)}), bf16[32,8,2560]{2,1,0:T(8,128)(2,1)}, u32[]{:S(2)}, u32[]{:S(2)}) %all-to-all-start.2) | async-done | bytes 1310752 | tf_op jit(solution)/shard_map/all_to_all | solution.py:99
  77.5 4.4 %all-to-all-start = ((bf16[32,8,2560]{2,1,0:T(8,128)(2,1)}), bf16[32,8,2560]{2,1,0:T(8,128)(2,1)}, u32[]{:S(2)}, u32[]{:S(2)}) async-start(bf16[32,8,2560]{2,1,0:T(8,128)(2,1)} %bitcast.47), calls=%async_computation | async-start | bytes 2621440 | tf_op jit(solution)/shard_map/all_to_all | solution.py:100
  84.0 4.0 %gather_fusion = bf16[48,8,2560]{2,1,0:T(8,128)(2,1)} fusion(bf16[64,8,2560]{2,1,0:T(8,128)(2,1)} %param.25, s32[1024]{0:T(1024)S(1)} %pad_clamp_fusion.1), kind=kCustom, calls=%fused_computation | custom fusion | bytes 3932352 | tf_op jit(solution)/shard_map/gather | solution.py:105
  89.0 5.1 %all-reduce = (f32[256]{0:T(256)S(1)}, f32[256]{0:T(256)S(1)}) all-reduce(f32[256]{0:T(256)S(1)} %fusion.20, f32[256]{0:T(256)S(1)} %fusion.23), channel_id=1, replica_groups=mesh['req'=16,'tp'=2] {'tp'}, use_global_device_ids=true, to_apply=%region_4.0 | all-reduce | flops 512 | bytes 4096 | tf_op jit(solution)/shard_map/psum | solution.py:61
  96.6 3.0 concatenate.28
  101.4 4.4 %concatenate.23 = bf16[384,20,128]{2,1,0:T(8,128)(2,1)} reshape(bf16[48,8,2560]{2,1,0:T(8,128)(2,1)} %gather_fusion) | data formatting | bytes 3932160 | tf_op jit(solution)/shard_map/concatenate | solution.py:110
  105.7 4.5 %copy.48 = bf16[384,20,128]{0,2,1:T(8,128)(2,1)} copy(bf16[384,20,128]{2,1,0:T(8,128)(2,1)} %concatenate.23) | data formatting | bytes 3932160 | tf_op jit(solution)/shard_map/concatenate | solution.py:110
  113.3 2.6 concatenate.29
  117.2 13.0 %all-to-all-done = bf16[32,8,2560]{2,1,0:T(8,128)(2,1)} async-done(((bf16[32,8,2560]{2,1,0:T(8,128)(2,1)}), bf16[32,8,2560]{2,1,0:T(8,128)(2,1)}, u32[]{:S(2)}, u32[]{:S(2)}) %all-to-all-start) | async-done | bytes 1310752 | tf_op jit(solution)/shard_map/all_to_all | solution.py:100
  130.2 2.6 concatenate.24
  134.5 12.7 %fusion = (f32[20,256]{1,0:T(8,128)S(1)}, f32[20,256,896]{2,1,0:T(8,128)}) fusion(pred[896]{0:T(1024)(128)(4,1)S(1)} %pad_add_fusion, bf16[256,20,128]{0,2,1:T(8,128)(2,1)} %bitcast.59, bf16[256,20,128]{2,0,1:T(8,128)(2,1)} %copy.54, bf16[256,20,128]{2,0,1:T(8,128)(2,1)} %copy.53, bf16[384,20,128]{2,0,1:T(8,128)(2,1)} %copy.52), kind=kOutput, calls=%fused_computation.8 | convolution fusion | flops 1201925120 | bytes 24269696 | tf_op jit(solution)/shard_map/qhd,khd->hqk/dot_general | solution.py:21
  147.2 9.9 %fusion.1 = f32[20,256]{1,0:T(8,128)S(1)} fusion(f32[20,256,896]{2,1,0:T(8,128)} %get-tuple-element.17, f32[20,256]{1,0:T(8,128)S(1)} %get-tuple-element.16, pred[896]{0:T(1024)(128)(4,1)S(1)} %pad_add_fusion), kind=kLoop, calls=%fused_computation.9 | loop fusion | flops 18344960 | bytes 18391936 | tf_op jit(solution)/shard_map/reduce_sum | solution.py:28
  157.2 9.7 %fusion.27 = bf16[256,20,128]{0,2,1:T(8,128)(2,1)} fusion(f32[20,256,896]{2,1,0:T(8,128)} %get-tuple-element.17, f32[20,256]{1,0:T(8,128)S(1)} %get-tuple-element.16, pred[896]{0:T(1024)(128)(4,1)S(1)} %pad_add_fusion, bf16[256,20,128]{0,2,1:T(8,128)(2,1)S(1)} %bitcast.58, bf16[256,20,128]{0,2,1:T(8,128)(2,1)S(1)} %copy-done.9, ...), kind=kOutput, calls=%fused_computation.43 | convolution fusion | flops 1207828480 | bytes 24290176 | tf_op jit(solution)/shard_map/hqk,khd->qhd/dot_general | solution.py:30
  166.8 24.8 %all-gather.5.cloned.1.call-done = bf16[2560,5120]{0,1:T(8,128)(2,1)} async-done(((bf16[2560,320]{0,1:T(8,128)(2,1)}), bf16[2560,5120]{0,1:T(8,128)(2,1)}) %all-gather.5.cloned.1.call-update) | async-done | bytes 26214416 | tf_op jit(solution)/shard_map/all_gather | solution.py:120
  191.7 13.5 %convolution_convert_fusion.2 = bf16[256,5120]{1,0:T(8,128)(2,1)} fusion(bf16[256,2560]{0,1:T(8,128)(2,1)} %bitcast.67, bf16[2560,5120]{0,1:T(8,128)(2,1)} %all-gather.5.cloned.1.call-done), kind=kOutput, calls=%fused_computation.16 | convolution fusion | flops 6712197120 | bytes 30146560 | tf_op jit(solution)/shard_map/dot_general | solution.py:118
  205.9 4.5 %all_gather.10 = bf16[1,5120]{1,0:T(2,128)(2,1)S(1)} all-gather(bf16[1,2560]{1,0:T(2,128)(2,1)S(1)} %copy-done.15), channel_id=1, replica_groups=mesh['req'=16,'tp'=2] {'tp'}, dimensions={1}, use_global_device_ids=true | all-gather | bytes 15360 | tf_op jit(solution)/shard_map/all_gather | solution.py:126
  217.6 2.4 copy.62
  220.1 21.7 %all-gather.3.cloned.1.call-done = bf16[256,5120]{1,0:T(8,128)(2,1)} async-done(((bf16[256,2560]{1,0:T(8,128)(2,1)}), bf16[256,5120]{1,0:T(8,128)(2,1)}) %all-gather.3.cloned.1.call-update) | async-done | bytes 2621456 | tf_op jit(solution)/shard_map/all_gather | solution.py:125
  241.9 76.7 %all-reduce.3.cloned.1.call-done = bf16[256,5120]{1,0:T(8,128)(2,1)} async-done(((bf16[256,5120]{1,0:T(8,128)(2,1)}), bf16[256,5120]{1,0:T(8,128)(2,1)}) %all-reduce.3.cloned.1.call-update) | async-done | bytes 2621456 | tf_op jit(solution)/shard_map/psum | solution.py:123
  318.5 3.5 %fusion.49 = (f32[256]{0:T(256)S(1)}, f32[256,5120]{1,0:T(8,128)S(1)}) fusion(bf16[256,5120]{1,0:T(8,128)(2,1)} %all-reduce.3.cloned.1.call-done, f32[5120]{0:T(1024)S(1)} %bitcast.62, bf16[256,5120]{1,0:T(8,128)(2,1)} %all-gather.3.cloned.1.call-done), kind=kLoop, calls=%fused_computation.81 | loop fusion | flops 6553344 | bytes 10507264 | tf_op jit(solution)/shard_map/reduce_sum | solution.py:129
  (93 shorter events, 37.3 us)
Async XLA Ops:
  7.2 12.0 %copy-start = (bf16[64,8,2560]{2,1,0:T(8,128)(2,1)S(1)}, bf16[64,8,2560]{2,1,0:T(8,128)(2,1)}, u32[]{:S(2)}) copy-start(bf16[64,8,2560]{2,1,0:T(8,128)(2,1)} %param.24) | copy-start | bytes 7864324
  7.2 184.5 %all-gather.5.cloned.1.call-start = ((), (), s32[]{:S(2)}) async-start(), calls=%async_computation.4 | async-start | bytes 27852800 | tf_op jit(solution)/shard_map/all_gather | solution.py:120
  11.1 13.7 %all-to-all-start.1 = ((bf16[16,2,8]{2,1,0:T(2,128)(2,1)}), bf16[16,2,8]{2,1,0:T(2,128)(2,1)S(1)}, u32[]{:S(2)}, u32[]{:S(2)}) async-start(bf16[16,2,8]{2,1,0:T(2,128)(2,1)} %broadcast_in_dim.15), calls=%async_computation.1 | async-start | bytes 16384 | tf_op jit(solution)/shard_map/all_to_all | solution.py:101
  24.8 52.7 %all-to-all-start.2 = ((bf16[32,8,2560]{2,1,0:T(8,128)(2,1)}), bf16[32,8,2560]{2,1,0:T(8,128)(2,1)}, u32[]{:S(2)}, u32[]{:S(2)}) async-start(bf16[32,8,2560]{2,1,0:T(8,128)(2,1)} %bitcast.48), calls=%async_computation.2 | async-start | bytes 2621440 | tf_op jit(solution)/shard_map/all_to_all | solution.py:99
  29.2 212.6 %all-gather.3.cloned.1.call-start = ((), (), s32[]{:S(2)}) async-start(), calls=%async_computation.3 | async-start | bytes 3932160 | tf_op jit(solution)/shard_map/all_gather | solution.py:125
  35.0 2.1 copy-start.2
  35.0 2.5 copy-start.18
  77.5 52.7 %all-to-all-start = ((bf16[32,8,2560]{2,1,0:T(8,128)(2,1)}), bf16[32,8,2560]{2,1,0:T(8,128)(2,1)}, u32[]{:S(2)}, u32[]{:S(2)}) async-start(bf16[32,8,2560]{2,1,0:T(8,128)(2,1)} %bitcast.47), calls=%async_computation | async-start | bytes 2621440 | tf_op jit(solution)/shard_map/all_to_all | solution.py:100
  81.9 236.6 %all-reduce.3.cloned.1.call-start = ((), (), s32[]{:S(2)}) async-start(), calls=%async_computation.5 | async-start | bytes 5242880 | tf_op jit(solution)/shard_map/psum | solution.py:123
  84.0 4.0 %copy-start.5 = (bf16[256,2560]{1,0:T(8,128)(2,1)S(1)}, bf16[256,2560]{1,0:T(8,128)(2,1)}, u32[]{:S(2)}) copy-start(bf16[256,2560]{1,0:T(8,128)(2,1)} %param.20) | copy-start | bytes 3932164
  88.0 6.1 %copy-start.13 = (f32[2560]{0:T(1024)S(1)}, f32[2560]{0:T(1024)}, u32[]{:S(2)}) copy-start(f32[2560]{0:T(1024)} %param.23) | copy-start | bytes 30724
  105.7 4.5 %copy-start.6 = (bf16[256,2560]{1,0:T(8,128)(2,1)S(1)}, bf16[256,2560]{1,0:T(8,128)(2,1)}, u32[]{:S(2)}) copy-start(bf16[256,2560]{1,0:T(8,128)(2,1)} %param.21) | copy-start | bytes 3932164
  105.7 5.9 %copy-start.3 = (bf16[256,2560]{0,1:T(8,128)(2,1)S(1)}, bf16[256,2560]{0,1:T(8,128)(2,1)}, u32[]{:S(2)}) copy-start(bf16[256,2560]{0,1:T(8,128)(2,1)} %copy.50) | copy-start | bytes 3932164
  105.7 5.9 %copy-start.14 = (f32[2560]{0:T(1024)S(1)}, f32[2560]{0:T(1024)}, u32[]{:S(2)}) copy-start(f32[2560]{0:T(1024)} %param.22) | copy-start | bytes 30724
  147.2 9.9 %copy-start.4 = (bf16[384,20,128]{0,2,1:T(8,128)(2,1)S(1)}, bf16[384,20,128]{0,2,1:T(8,128)(2,1)}, u32[]{:S(2)}) copy-start(bf16[384,20,128]{0,2,1:T(8,128)(2,1)} %copy.48) | copy-start | bytes 5898244
  147.2 9.9 %copy-start.8 = (bf16[256,2560]{0,1:T(8,128)(2,1)S(1)}, bf16[256,2560]{0,1:T(8,128)(2,1)}, u32[]{:S(2)}) copy-start(bf16[256,2560]{0,1:T(8,128)(2,1)} %copy.47) | copy-start | bytes 3932164
  147.2 9.9 %copy-start.9 = (bf16[256,20,128]{0,2,1:T(8,128)(2,1)S(1)}, bf16[256,20,128]{0,2,1:T(8,128)(2,1)}, u32[]{:S(2)}) copy-start(bf16[256,20,128]{0,2,1:T(8,128)(2,1)} %copy.49) | copy-start | bytes 3932164
  205.2 5.2 %copy-start.7 = (bf16[256,2560]{1,0:T(8,128)(2,1)S(1)}, bf16[256,2560]{1,0:T(8,128)(2,1)}, u32[]{:S(2)}) copy-start(bf16[256,2560]{1,0:T(8,128)(2,1)} %param.30) | copy-start | bytes 3932164
  205.2 6.7 %copy-start.10 = (bf16[128,2560]{1,0:T(8,128)(2,1)S(1)}, bf16[128,2560]{1,0:T(8,128)(2,1)}, u32[]{:S(2)}) copy-start(bf16[128,2560]{1,0:T(8,128)(2,1)} %param.31) | copy-start | bytes 1966084
  205.2 7.0 %copy-start.11 = (bf16[128,2560]{1,0:T(8,128)(2,1)S(1)}, bf16[128,2560]{1,0:T(8,128)(2,1)}, u32[]{:S(2)}) copy-start(bf16[128,2560]{1,0:T(8,128)(2,1)} %param.32) | copy-start | bytes 1966084
  213.3 2.5 copy-start.12
  217.6 2.5 copy-start.16
  217.6 2.5 copy-start.17
  322.7 2.9 copy-start.1
  (1 other events, 0.7 us)
Sparse Core Ops, SparseCore 0:
  9.6 182.0 all-gather.4
  193.2 48.6 all-gather.2
  244.2 74.3 all-reduce.2
where the time goes:
time: 333 us; the launch traced here: 332 us
  waiting for transfers between devices  181 us (54%)
  local copies, waits for them, and re-layouts  48 us (14%)
  matrix products  40.9 us (12%)
  other arithmetic  22 us (7%)
  starting transfers between devices  16.3 us (5%)
  between operations  14.7 us (4%)
  blocking collectives  9.62 us (3%)
    psum x1, waiting for transfers between devices, shards(): lax.psum(partial_rows.astype(jnp.bfloat16), 'tp').astype(jnp.float32)  76.7 us
    all_to_all x1, waiting for transfers between devices, shards(): lax.all_to_all(sent_keys, 'req', split_axis=0, concat_axis=0, tiled=True)  40.1 us
    all_gather x1, waiting for transfers between devices, shards(): lax.all_gather(out_weight, 'req', axis=1, tiled=True)  24.8 us
    all_gather x1, waiting for transfers between devices, shards(): lax.all_gather(residual, 'tp', axis=1, tiled=True)  21.7 us
    dot_general x2, matrix products, attend(): jnp.einsum('qhd,khd->hqk', query_heads, key_heads, preferred_element_type...  14.7 us
    unnamed x49, local copies, waits for them, and re-layouts  13.8 us
    dot_general x1, matrix products, shards(): jnp.dot(attended, lax.all_gather(out_weight, 'req', axis=1, tiled=True),...  13.5 us
    concatenate x4, local copies, waits for them, and re-layouts, shards(): jnp.concatenate([resident_values, arrived_values.reshape(-1, local_width)...  13.1 us
  transfers between devices with their start and end apart: 6, of which 6 were waited for; matrix products, arithmetic and copies ran while one was open for 31% of the time, Pallas kernels for 0%

commit v1 on v0

v1 whole, which is shorter than its diff:
```python
import functools
import math

import jax
import jax.numpy as jnp
from jax import lax
from jax.experimental import pallas as pl
from jax.experimental.pallas import tpu as pltpu
from jax.sharding import PartitionSpec as P

HD = 128
CAP = 2
EPS = 1e-06
VMEM_LIMIT = 48 * 1024 * 1024


def pack_kernel(peers, me_ref, dest_ref, page_ref, keys_ref, values_ref, *refs):
    out_refs, (table, count, sems) = refs[:peers], refs[peers:]

    @pl.loop(0, peers)
    def _(r):
        count[r] = 0
        for c in range(CAP):
            table[r * CAP + c] = 0

    @pl.loop(0, dest_ref.shape[0])
    def _(i):
        r = dest_ref[i]
        c = jnp.minimum(count[r], CAP - 1)
        table[r * CAP + c] = page_ref[i]
        count[r] = c + 1

    copies = []
    for k in range(peers):
        r = jnp.bitwise_xor(me_ref[0], k)
        for c in range(CAP):
            page = table[r * CAP + c]
            for half, source in enumerate((keys_ref, values_ref)):
                copy = pltpu.make_async_copy(
                    source.at[page], out_refs[k].at[half, c], sems.at[(k * CAP + c) * 2 + half]
                )
                copy.start()
                copies.append(copy)
    for copy in copies:
        copy.wait()


def pack_pages(me, dest, pages, cache_keys, cache_values, peers):
    _, page_len, width = cache_keys.shape
    smem = pl.BlockSpec(memory_space=pltpu.SMEM)
    hbm = pl.BlockSpec(memory_space=pl.ANY)
    return pl.pallas_call(
        functools.partial(pack_kernel, peers),
        out_shape=[jax.ShapeDtypeStruct((2, CAP, page_len, width), cache_keys.dtype)] * peers,
        in_specs=[smem, smem, smem, hbm, hbm],
        out_specs=[hbm] * peers,
        scratch_shapes=[
            pltpu.SMEM((peers * CAP,), jnp.int32),
            pltpu.SMEM((peers,), jnp.int32),
            pltpu.SemaphoreType.DMA((peers * CAP * 2,)),
        ],
        name="pack_pages",
    )(me, dest, pages, cache_keys, cache_values)


def resident_kernel(table_ref, keys_ref, values_ref, out_keys, out_values, sems):
    copies = []
    for j in range(table_ref.shape[0]):
        page = table_ref[j]
        for half, (source, target) in enumerate(((keys_ref, out_keys), (values_ref, out_values))):
            copy = pltpu.make_async_copy(source.at[page], target.at[j], sems.at[j * 2 + half])
            copy.start()
            copies.append(copy)
    for copy in copies:
        copy.wait()


def resident_pages(table, cache_keys, cache_values):
    pages = table.shape[0]
    hbm = pl.BlockSpec(memory_space=pl.ANY)
    shape = jax.ShapeDtypeStruct((pages,) + cache_keys.shape[1:], cache_keys.dtype)
    return pl.pallas_call(
        resident_kernel,
        out_shape=[shape, shape],
        in_specs=[pl.BlockSpec(memory_space=pltpu.SMEM), hbm, hbm],
        out_specs=[hbm, hbm],
        scratch_shapes=[pltpu.SemaphoreType.DMA((pages * 2,))],
        name="resident_pages",
    )(table, cache_keys, cache_values)


def softmax_head(query, keys, values, bias):
    factor = math.log2(math.e) / math.sqrt(HD)
    scores = lax.dot_general(
        query, keys, (((1,), (1,)), ((), ())), preferred_element_type=jnp.float32
    )
    if bias is not None:
        scores = scores + bias
    row_max = jnp.max(scores, axis=1, keepdims=True)
    exponent = jnp.exp2((scores - row_max) * factor)
    denominator = jnp.sum(exponent, axis=1, keepdims=True)
    mixed = jnp.dot(exponent.astype(jnp.bfloat16), values, preferred_element_type=jnp.float32)
    return (mixed / denominator).astype(jnp.bfloat16)


def self_kernel(heads, bias_ref, q_ref, rk_ref, rv_ref, k_ref, v_ref, *refs):
    arrived, out_ref = refs[:-1], refs[-1]
    for h in range(heads):
        part = slice(h * HD, (h + 1) * HD)
        keys = [rk_ref[:, :, part].reshape(-1, HD)]
        values = [rv_ref[:, :, part].reshape(-1, HD)]
        for a in arrived:
            keys.append(a[0, :, :, part].reshape(-1, HD))
            values.append(a[1, :, :, part].reshape(-1, HD))
        keys.append(k_ref[:, part])
        values.append(v_ref[:, part])
        out_ref[:, part] = softmax_head(
            q_ref[:, part], jnp.concatenate(keys, axis=0), jnp.concatenate(values, axis=0), bias_ref[...]
        )


def cross_kernel(heads, q_ref, k_ref, v_ref, out_ref):
    for h in range(heads):
        part = slice(h * HD, (h + 1) * HD)
        out_ref[:, part] = softmax_head(q_ref[:, part], k_ref[:, part], v_ref[:, part], None)


def head_group(width):
    heads = width // HD
    for group in (5, 4, 2):
        if heads % group == 0:
            return group
    return 1


def self_attention(bias, query, res_keys, res_values, keys, values, arrived):
    tokens, width = query.shape
    group = head_group(width)
    block = group * HD
    flat = lambda rows: pl.BlockSpec((rows, block), lambda h: (0, h))
    paged = pl.BlockSpec(res_keys.shape[:2] + (block,), lambda h: (0, 0, h))
    moved = pl.BlockSpec(arrived[0].shape[:3] + (block,), lambda h: (0, 0, 0, h))
    count = bias.shape[1]
    return pl.pallas_call(
        functools.partial(self_kernel, group),
        out_shape=jax.ShapeDtypeStruct((tokens, width), query.dtype),
        grid=(width // block,),
        in_specs=[pl.BlockSpec(bias.shape, lambda h: (0, 0)), flat(tokens), paged, paged, flat(tokens), flat(tokens)]
        + [moved] * len(arrived),
        out_specs=flat(tokens),
        compiler_params=pltpu.CompilerParams(vmem_limit_bytes=VMEM_LIMIT),
        cost_estimate=pl.CostEstimate(
            flops=4 * tokens * count * width,
            bytes_accessed=2 * width * (2 * tokens + 2 * count),
            transcendentals=tokens * count * width // HD,
        ),
        name="self_attention",
    )(bias, query, res_keys, res_values, keys, values, *arrived)


def cross_attention(query, keys, values):
    tokens, width = query.shape
    group = head_group(width)
    block = group * HD
    flat = lambda rows: pl.BlockSpec((rows, block), lambda h: (0, h))
    count = keys.shape[0]
    return pl.pallas_call(
        functools.partial(cross_kernel, group),
        out_shape=jax.ShapeDtypeStruct((tokens, width), query.dtype),
        grid=(width // block,),
        in_specs=[flat(tokens), flat(count), flat(count)],
        out_specs=flat(tokens),
        compiler_params=pltpu.CompilerParams(vmem_limit_bytes=VMEM_LIMIT),
        cost_estimate=pl.CostEstimate(
            flops=4 * tokens * count * width,
            bytes_accessed=2 * width * (2 * tokens + 2 * count),
            transcendentals=tokens * count * width // HD,
        ),
        name="cross_attention",
    )(query, keys, values)


def tp_sum(x):
    if lax.axis_size("tp") == 2:
        return x + lax.ppermute(x, "tp", [(0, 1), (1, 0)])
    return lax.psum(x, "tp")


def after(x, *earlier):
    return lax.optimization_barrier((x,) + earlier)[0]


def swap(x, bits):
    size = lax.axis_size("req")
    return lax.ppermute(x, "req", [(i, i ^ bits) for i in range(size)])


def partial_product(rows, weights):
    return jnp.dot(rows, weights, preferred_element_type=jnp.float32)


def projection_gathered(attended, out_weight):
    width = attended.shape[1]
    weights = lax.all_gather(out_weight, "req", axis=1, tiled=True)
    partial = partial_product(attended, weights).astype(jnp.bfloat16)
    column = lax.axis_index("tp") * width
    if lax.axis_size("tp") == 2:
        other = (lax.axis_size("tp") - 1) * width - column
        own = lax.dynamic_slice_in_dim(partial, column, width, 1)
        sent = lax.dynamic_slice_in_dim(partial, other, width, 1)
        received = lax.ppermute(sent, "tp", [(0, 1), (1, 0)])
        return own.astype(jnp.float32) + received.astype(jnp.float32)
    summed = lax.psum(partial, "tp").astype(jnp.float32)
    return lax.dynamic_slice_in_dim(summed, column, width, 1)


CORE, Y, Z1, Z2 = 1, 2, 4, 8
CHUNKS = 5


def projection_planes(attended, out_weight, pages_in):
    tokens, width = attended.shape
    shard = out_weight.shape[1]
    me, x = lax.axis_index("req"), lax.axis_index("tp")
    core, z_low, z_high = me % 2, (me // 4) % 2, me // 8
    half = width // 2

    mine = lax.dynamic_slice_in_dim(out_weight, core * half, half, 0)
    other = lax.dynamic_slice_in_dim(out_weight, (1 - core) * half, half, 0)
    got = swap(other, CORE)
    block = jnp.where(
        core == 0, jnp.concatenate([mine, got], axis=1), jnp.concatenate([got, mine], axis=1)
    )
    block_y = swap(block, Y)

    early_mine = jnp.concatenate([block, block_y], axis=1)
    early_other = swap(early_mine, CORE)

    step = 2 * shard // CHUNKS
    late = []
    gate_on = list(pages_in)
    for j in range(CHUNKS):
        piece = lax.slice_in_dim(block, j * step, (j + 1) * step, axis=1)
        piece = swap(after(piece, *gate_on), Z2)
        late_mine = jnp.concatenate([piece, swap(piece, Y)], axis=1)
        late.append((late_mine, swap(late_mine, CORE)))
        gate_on = [late[-2][0]] if j >= 1 else gate_on

    both = jnp.concatenate([attended, swap(attended, Z1)], axis=0)
    rows_mine = lax.dynamic_slice_in_dim(both, core * half, half, 1)
    rows_other = lax.dynamic_slice_in_dim(both, (1 - core) * half, half, 1)

    def product(w_mine, w_other):
        return (partial_product(rows_mine, w_mine) + partial_product(rows_other, w_other)).astype(jnp.bfloat16)

    ids = [(r, t) for r in range(16) for t in range(2)]
    flat = lambda r, t: r * 2 + t

    def deliver(partial, late_half):
        owners = [(r, t) for r, t in ids if t == ((r // 8) ^ late_half)]
        others = [(r, t) for r, t in ids if t != ((r // 8) ^ late_half)]
        axes = ("req", "tp")
        own, neighbour = partial[:tokens], partial[tokens:]
        from_x = lax.ppermute(own, axes, [(flat(r, t), flat(r, 1 - t)) for r, t in others])
        from_z = lax.ppermute(neighbour, axes, [(flat(r, t), flat(r ^ Z1, t)) for r, t in owners])
        from_xz = lax.ppermute(neighbour, axes, [(flat(r, t), flat(r ^ Z1, 1 - t)) for r, t in others])
        own_sum = own.astype(jnp.float32) + from_x.astype(jnp.float32)
        other_sum = from_z.astype(jnp.float32) + from_xz.astype(jnp.float32)
        return own_sum, other_sum

    early_own, early_neigh = deliver(product(early_mine, early_other), 0)
    late_parts = [deliver(product(a, b), 1) for a, b in late]
    block_width = 2 * shard

    def late_columns(i):
        first = [p[i][:, :step] for p in late_parts]
        second = [p[i][:, step:] for p in late_parts]
        return jnp.concatenate(first + second, axis=1)

    def ordered(a):
        y = (me // 2) % 2
        a0, a1 = a[:, :block_width], a[:, block_width:]
        return jnp.where(y == 0, jnp.concatenate([a0, a1], axis=1), jnp.concatenate([a1, a0], axis=1))

    is_early = x == z_high
    own_cols = ordered(jnp.where(is_early, early_own, late_columns(0)))
    neigh_cols = ordered(jnp.where(is_early, early_neigh, late_columns(1)))
    return jnp.where(
        z_low == 0,
        jnp.concatenate([own_cols, neigh_cols], axis=1),
        jnp.concatenate([neigh_cols, own_cols], axis=1),
    )


def shards(
    queries,
    new_keys,
    new_values,
    query_gain,
    key_gain,
    cache_keys,
    cache_values,
    page_table,
    cache_lens,
    mig_pages,
    mig_dest,
    cross_queries,
    text_keys,
    text_values,
    out_weight,
    residual,
    gate,
    shift,
    scale,
):
    tokens, width = queries.shape
    tp, peers = lax.axis_size("tp"), lax.axis_size("req")
    full_width = width * tp
    me = lax.axis_index("req")
    page_len = cache_keys.shape[1]

    packed = pack_pages(
        me.reshape(1).astype(jnp.int32), mig_dest[:, 0], mig_pages[0], cache_keys, cache_values, peers
    )
    arrived = [packed[0]] + [swap(packed[k], k) for k in range(1, peers)]
    all_dest = lax.all_gather(mig_dest[:, 0], "req", axis=0)
    filled = jnp.sum((all_dest == me).astype(jnp.int32), axis=1)
    filled = filled[jnp.bitwise_xor(jnp.arange(peers, dtype=jnp.int32), me)]
    slots = jnp.arange(CAP * page_len, dtype=jnp.int32) // page_len
    arrived_usable = (slots[None, :] < filled[:, None]).reshape(-1)

    query_float = queries.astype(jnp.float32)
    key_float = new_keys.astype(jnp.float32)
    squares = tp_sum(
        jnp.stack([jnp.sum(query_float * query_float, axis=1), jnp.sum(key_float * key_float, axis=1)])
    )
    inverse = lax.rsqrt(squares / full_width + EPS)
    query_normed = (query_float * inverse[0][:, None] * query_gain).astype(jnp.bfloat16)
    key_normed = (key_float * inverse[1][:, None] * key_gain).astype(jnp.bfloat16)

    res_keys, res_values = resident_pages(page_table[0], cache_keys, cache_values)
    resident_usable = jnp.arange(res_keys.shape[0] * page_len, dtype=jnp.int32) < cache_lens[0]
    usable = jnp.concatenate([resident_usable, arrived_usable, jnp.ones((tokens,), bool)])
    bias = jnp.where(usable, 0.0, -jnp.inf).astype(jnp.float32)[None, :]

    cross_out = cross_attention(cross_queries, text_keys, text_values)
    attended = self_attention(bias, query_normed, res_keys, res_values, key_normed, new_values, arrived)

    if peers == 16 and tp == 2:
        projected = projection_planes(attended, out_weight, arrived)
    else:
        projected = projection_gathered(attended, out_weight)

    updated = residual.astype(jnp.float32) + gate.astype(jnp.float32) * projected
    stream = updated.astype(jnp.bfloat16)
    local_mean = jnp.mean(updated, axis=1)
    local_square = jnp.sum(jnp.square(updated - local_mean[:, None]), axis=1)
    if tp == 2:
        theirs = lax.ppermute(jnp.stack([local_mean, local_square]), "tp", [(0, 1), (1, 0)])
        row_mean = (local_mean + theirs[0]) * 0.5
        gap = local_mean - theirs[0]
        row_var = (local_square + theirs[1] + gap * gap * (0.5 * width)) / full_width
    else:
        row_mean = lax.psum(local_mean, "tp") / tp
        offset = local_mean - row_mean
        row_var = lax.psum(local_square + width * offset * offset, "tp") / full_width
    normed = (
        (updated - row_mean[:, None]) * lax.rsqrt(row_var + EPS)[:, None] * (1.0 + scale.astype(jnp.float32))
        + shift.astype(jnp.float32)
    ).astype(jnp.bfloat16)
    return (stream, normed, cross_out)


def solution(mesh):
    in_specs = (
        P("req", "tp"),
        P("req", "tp"),
        P("req", "tp"),
        P("tp"),
        P("tp"),
        P("req", None, "tp"),
        P("req", None, "tp"),
        P("req", None),
        P("req"),
        P("req", None),
        P("req", None),
        P("req", "tp"),
        P("req", "tp"),
        P("req", "tp"),
        P("tp", "req"),
        P("req", "tp"),
        P("req", "tp"),
        P("req", "tp"),
        P("req", "tp"),
    )
    out_specs = (P("req", "tp"), P("req", "tp"), P("req", "tp"))
    return jax.shard_map(shards, mesh=mesh, in_specs=in_specs, out_specs=out_specs, check_vma=False)
```

time: 333 us -> 521 us (1.56)
  Pallas kernels: 0 us -> 220 us
  starting transfers between devices: 16.3 us -> 88.6 us
  local copies, waits for them, and re-layouts: 48 us -> 9.21 us
  matrix products: 40.9 us -> 9.19 us
  waiting for transfers between devices: 181 us -> 166 us
  between operations: 14.7 us -> 3.05 us
  other arithmetic: 22 us -> 10.9 us
    pallas_call x0 -> x4, Pallas kernels: none -> 220 us  [the longest x1 122 us: resident_pages(): pl.pallas_call(resident_kernel, out_shape=[shape, shape], in_specs=[pl.Bl...]
    ppermute x0 -> x54, waiting for transfers between devices: none -> 166 us  [the longest x34 129 us: swap(): return lax.ppermute(x, 'req', [(i, i ^ bits) for i in range(size)])]
    ppermute x0 -> x54, starting transfers between devices: none -> 88.6 us  [the longest x34 44.9 us: swap(): return lax.ppermute(x, 'req', [(i, i ^ bits) for i in range(size)])]
    psum x1 -> x0, waiting for transfers between devices: 76.7 us -> none  [shards(): lax.psum(partial_rows.astype(jnp.bfloat16), 'tp').astype(jnp.float32)]
    all_to_all x3 -> x0, waiting for transfers between devices: 55.9 us -> none  [the longest x1 40.1 us: shards(): lax.all_to_all(sent_keys, 'req', split_axis=0, concat_axis=0, tiled=True)]
    all_gather x2 -> x0, waiting for transfers between devices: 46.6 us -> none  [the longest x1 24.8 us: shards(): lax.all_gather(out_weight, 'req', axis=1, tiled=True)]
    dot_general x7 -> x12, matrix products: 40.9 us -> 9.19 us  [partial_product(): return jnp.dot(rows, weights, preferred_element_type=jnp.float32)]
    concatenate x9 -> x10, local copies, waits for them, and re-layouts: 23.2 us -> 0.24 us  [the longest x5 0.12 us: projection_planes(): late_mine = jnp.concatenate([piece, swap(piece, Y)], axis=1)]
  transfers between devices with their start and end apart: 6 -> 54, of which waited for: 6 -> 22; matrix products, arithmetic and copies ran while one was open for 31% -> 3% of each run, Pallas kernels for 0% -> 42%
where the time goes in v1:
time: 521 us
  Pallas kernels  220 us (42%)
  waiting for transfers between devices  166 us (32%)
  starting transfers between devices  88.6 us (17%)
  blocking collectives  13 us (2%)
  other arithmetic  10.9 us (2%)
  local copies, waits for them, and re-layouts  9.21 us (2%)
  matrix products  9.19 us (2%)
    ppermute x34, waiting for transfers between devices, swap(): return lax.ppermute(x, 'req', [(i, i ^ bits) for i in range(size)])  129 us
    pallas_call x1, Pallas kernels, resident_pages(): pl.pallas_call(resident_kernel, out_shape=[shape, shape], in_specs=[pl.Bl...  122 us
    pallas_call x1, Pallas kernels, pack_pages(): pl.pallas_call(functools.partial(pack_kernel, peers), out_shape=[jax.Shap...  82.2 us
    ppermute x34, starting transfers between devices, swap(): return lax.ppermute(x, 'req', [(i, i ^ bits) for i in range(size)])  44.9 us
    ppermute x6, waiting for transfers between devices, deliver(): lax.ppermute(own, axes, [(flat(r, t), flat(r, 1 - t)) for r, t in others])  34.4 us
    ppermute x6, starting transfers between devices, deliver(): lax.ppermute(own, axes, [(flat(r, t), flat(r, 1 - t)) for r, t in others])  20 us
    ppermute x6, starting transfers between devices, deliver(): lax.ppermute(neighbour, axes, [(flat(r, t), flat(r ^ Z1, 1 - t)) for r, t...  14.3 us
    unnamed x1, blocking collectives  13 us
  transfers between devices with their start and end apart: 54, of which 22 were waited for; matrix products, arithmetic and copies ran while one was open for 3% of the time, Pallas kernels for 42%

profile of v1, /device:TPU:0, one launch (start us, length us, event | category | flops | bytes accessed | tf_op | source)
XLA Modules:
  0.0 520.7 jit_solution(8495985141552953262)
XLA Ops:
  5.8 82.2 %pack_pages.1 = (bf16[2,2,8,2560]{3,2,1,0:T(8,128)(2,1)}, bf16[2,2,8,2560]{3,2,1,0:T(8,128)(2,1)}, bf16[2,2,8,2560]{3,2,1,0:T(8,128)(2,1)}, bf16[2,2,8,2560]{3,2...) custom-call(s32[1]{0:T(128)} %bitcast.9.me_ref, ...), custom_call_target="tpu_custom_call" | custom-call | tf_op jit(solution)/shard_map/pack_pages/pallas_call | solution.py:52
  92.8 13.0 %all-reduce = s32[256]{0:T(256)S(1)} all-reduce(s32[256]{0:T(256)S(1)} %bitcast_dynamic-update-slice_fusion), channel_id=2, replica_groups=mesh['req'=16,'tp'=2] {'req'}, use_global_device_ids=true, to_apply=%add | all-reduce | flops 256 | bytes 2048
  110.3 121.9 %resident_pages.1 = (bf16[48,8,2560]{2,1,0:T(8,128)(2,1)}, bf16[48,8,2560]{2,1,0:T(8,128)(2,1)}) custom-call(s32[48]{0:T(128)} %bitcast.53, bf16[64,8,2560]{2,1,0:T(8,128)(2,1)} %keys_ref.3, bf16[64,8,2560]{2,1,0:T(8,128)(2,1)} %values_ref.3), custom_call_target="tpu_custom_call" | custom-call | tf_op jit(solution)/shard_map/resident_pages/pallas_call | solution.py:82
  240.3 6.8 %collective-permute-done.6.refs_6_ = bf16[2,2,8,2560]{3,2,1,0:T(8,128)(2,1)S(1)} collective-permute-done((bf16[2,2,8,2560]{3,2,1,0:T(8,128)(2,1)}, bf16[2,2,8,2560]{3,2,1,0:T(8,128)(2,1)S(1)}, u32[]{:S(2)}, u32[]{:S(2)}) %collective-permute-start.6) | collective-permute-done | bytes 163872 | tf_op jit(solution)/shard_map/ppermute | solution.py:195
  251.6 4.3 collective-permute-start.12
  255.9 10.7 %collective-permute-done.9.refs_9_ = bf16[2,2,8,2560]{3,2,1,0:T(8,128)(2,1)S(1)} collective-permute-done((bf16[2,2,8,2560]{3,2,1,0:T(8,128)(2,1)}, bf16[2,2,8,2560]{3,2,1,0:T(8,128)(2,1)S(1)}, u32[]{:S(2)}, u32[]{:S(2)}) %collective-permute-start.9) | collective-permute-done | bytes 163872 | tf_op jit(solution)/shard_map/ppermute | solution.py:195
  266.7 5.7 %collective-permute-done.10.refs_10_ = bf16[2,2,8,2560]{3,2,1,0:T(8,128)(2,1)S(1)} collective-permute-done((bf16[2,2,8,2560]{3,2,1,0:T(8,128)(2,1)}, bf16[2,2,8,2560]{3,2,1,0:T(8,128)(2,1)S(1)}, u32[]{:S(2)}, u32[]{:S(2)}) %collective-permute-start.10) | collective-permute-done | bytes 163872 | tf_op jit(solution)/shard_map/ppermute | solution.py:195
  272.4 9.3 %collective-permute-done.11.refs_11_ = bf16[2,2,8,2560]{3,2,1,0:T(8,128)(2,1)S(1)} collective-permute-done((bf16[2,2,8,2560]{3,2,1,0:T(8,128)(2,1)}, bf16[2,2,8,2560]{3,2,1,0:T(8,128)(2,1)S(1)}, u32[]{:S(2)}, u32[]{:S(2)}) %collective-permute-start.11) | collective-permute-done | bytes 163872 | tf_op jit(solution)/shard_map/ppermute | solution.py:195
  284.4 12.3 %self_attention.1 = bf16[256,2560]{1,0:T(8,128)(2,1)S(1)} custom-call(f32[1,896]{1,0:T(1,128)S(1)} %fusion.16.bias_ref, bf16[256,2560]{1,0:T(8,128)(2,1)S(1)} %get-tuple-element.82.q_ref, bf16[48,8,2560]{2,1,0:T(8,128)(2,1)} %get-tuple-element.26.rk_ref, bf16[48,8,2560]{2,1,0:T(8,128)(2,1)} %get-tuple-element.27.rv_ref, ...), custom_call_target="tpu_custom_call" | custom-call | flops 2348810240 | bytes 11796480 | tf_op jit(solution)/shard_map/self_attention/pallas_call | solution.py:144
  296.7 11.9 %collective-permute-start.16 = (bf16[256,2560]{1,0:T(8,128)(2,1)S(1)}, bf16[256,2560]{1,0:T(8,128)(2,1)}, u32[]{:S(2)}, u32[]{:S(2)}) collective-permute-start(bf16[256,2560]{1,0:T(8,128)(2,1)S(1)} %self_attention.1), channel_id=1, source_target_pairs={{0,8},{2,10},{4,12},{6,14},{8,0},{10,2},{12,4},{14,6},{16,24},{18,... | collective-permute-start | bytes 3932168 | tf_op jit(solution)/shard_map/ppermute | solution.py:195
  314.1 30.8 %collective-permute-done.21 = bf16[1280,128]{0,1:T(8,128)(2,1)} collective-permute-done((bf16[1280,128]{0,1:T(8,128)(2,1)}, bf16[1280,128]{0,1:T(8,128)(2,1)}, u32[]{:S(2)}, u32[]{:S(2)}) %collective-permute-start.21) | collective-permute-done | bytes 327712 | tf_op jit(solution)/shard_map/ppermute | solution.py:195
  346.4 5.0 collective-permute-done.25
  352.0 7.3 %collective-permute-done.22 = bf16[1280,128]{0,1:T(8,128)(2,1)S(1)} collective-permute-done((bf16[1280,128]{0,1:T(8,128)(2,1)}, bf16[1280,128]{0,1:T(8,128)(2,1)S(1)}, u32[]{:S(2)}, u32[]{:S(2)}) %collective-permute-start.22) | collective-permute-done | bytes 327712 | tf_op jit(solution)/shard_map/ppermute | solution.py:195
  359.4 5.5 %collective-permute-done.26 = bf16[1280,128]{0,1:T(8,128)(2,1)S(1)} collective-permute-done((bf16[1280,128]{0,1:T(8,128)(2,1)S(1)}, bf16[1280,128]{0,1:T(8,128)(2,1)S(1)}, u32[]{:S(2)}, u32[]{:S(2)}) %collective-permute-start.26) | collective-permute-done | bytes 327712 | tf_op jit(solution)/shard_map/ppermute | solution.py:195
  369.5 20.4 %collective-permute-done.29 = bf16[1280,128]{0,1:T(8,128)(2,1)S(1)} collective-permute-done((bf16[1280,128]{0,1:T(8,128)(2,1)S(1)}, bf16[1280,128]{0,1:T(8,128)(2,1)S(1)}, u32[]{:S(2)}, u32[]{:S(2)}) %collective-permute-start.29) | collective-permute-done | bytes 327712 | tf_op jit(solution)/shard_map/ppermute | solution.py:195
  390.4 6.5 %collective-permute-done.33 = bf16[1280,128]{0,1:T(8,128)(2,1)S(1)} collective-permute-done((bf16[1280,128]{0,1:T(8,128)(2,1)S(1)}, bf16[1280,128]{0,1:T(8,128)(2,1)S(1)}, u32[]{:S(2)}, u32[]{:S(2)}) %collective-permute-start.33) | collective-permute-done | bytes 327712 | tf_op jit(solution)/shard_map/ppermute | solution.py:195
  401.8 4.8 collective-permute-done.34
  411.5 4.3 collective-permute-start.28
  427.6 13.3 %collective-permute-done.37 = bf16[1280,128]{0,1:T(8,128)(2,1)S(1)} collective-permute-done((bf16[1280,128]{0,1:T(8,128)(2,1)S(1)}, bf16[1280,128]{0,1:T(8,128)(2,1)S(1)}, u32[]{:S(2)}, u32[]{:S(2)}) %collective-permute-start.37) | collective-permute-done | bytes 327712 | tf_op jit(solution)/shard_map/ppermute | solution.py:195
  445.9 4.3 collective-permute-start.32
  454.1 5.3 %collective-permute-start.50 = (bf16[256,256]{1,0:T(8,128)(2,1)S(1)}, bf16[256,256]{1,0:T(8,128)(2,1)S(1)}, u32[]{:S(2)}, u32[]{:S(2)}) collective-permute-start(bf16[256,256]{1,0:T(8,128)(2,1)S(1)} %get-tuple-element.68), channel_id=1, source_target_pairs={{0,9},{2,11},{4,13},{6,15},{8,1},{10,3},{12,5},{14,7},{17,24},{19,... | collective-permute-start | bytes 393224 | tf_op jit(solution)/shard_map/ppermute | solution.py:266
  463.5 6.3 %collective-permute-start.40 = (bf16[256,256]{1,0:T(8,128)(2,1)S(1)}, bf16[256,256]{1,0:T(8,128)(2,1)S(1)}, u32[]{:S(2)}, u32[]{:S(2)}) collective-permute-start(bf16[256,256]{1,0:T(8,128)(2,1)S(1)} %get-tuple-element.67), channel_id=1, source_target_pairs={{0,1},{2,3},{4,5},{6,7},{8,9},{10,11},{12,13},{14,15},{17,16},{19,... | collective-permute-start | bytes 393224 | tf_op jit(solution)/shard_map/ppermute | solution.py:264
  484.8 25.1 %collective-permute-done.20 = bf16[256,1280]{1,0:T(8,128)(2,1)S(1)} collective-permute-done((bf16[256,1280]{1,0:T(8,128)(2,1)S(1)}, bf16[256,1280]{1,0:T(8,128)(2,1)S(1)}, u32[]{:S(2)}, u32[]{:S(2)}) %collective-permute-start.20) | collective-permute-done | bytes 655392 | tf_op jit(solution)/shard_map/ppermute | solution.py:264
  514.2 4.0 cross_attention.1
  (226 shorter events, 96.4 us)
Async XLA Ops:
  2.8 229.4 %collective-permute-start = (f32[2,256]{1,0:T(2,128)S(1)}, f32[2,256]{1,0:T(2,128)S(1)}, u32[]{:S(2)}, u32[]{:S(2)}) collective-permute-start(f32[2,256]{1,0:T(2,128)S(1)} %pad_maximum_fusion.1), channel_id=1, source_target_pairs={{0,1},{1,0},{2,3},{3,2},{4,5},{5,4},{6,7},{7,6},{8,9},{9,8},{10,11... | collective-permute-start | bytes 6152 | tf_op jit(solution)/shard_map/ppermute | solution.py:185
  88.0 144.3 %collective-permute-start.1 = (bf16[2,2,8,2560]{3,2,1,0:T(8,128)(2,1)}, bf16[2,2,8,2560]{3,2,1,0:T(8,128)(2,1)S(1)}, u32[]{:S(2)}, u32[]{:S(2)}) collective-permute-start(bf16[2,2,8,2560]{3,2,1,0:T(8,128)(2,1)} %get-tuple-element.29), channel_id=1, source_target_pairs={{0,2},{2,0},{4,6},{6,4},{8,10},{10,8},{12,14},{14,12},{16,18},{18,... | collective-permute-start | bytes 491528 | tf_op jit(solution)/shard_map/ppermute | solution.py:195
  88.0 145.8 %collective-permute-start.2 = (bf16[2,2,8,2560]{3,2,1,0:T(8,128)(2,1)}, bf16[2,2,8,2560]{3,2,1,0:T(8,128)(2,1)S(1)}, u32[]{:S(2)}, u32[]{:S(2)}) collective-permute-start(bf16[2,2,8,2560]{3,2,1,0:T(8,128)(2,1)} %get-tuple-element.30), channel_id=1, source_target_pairs={{0,4},{2,6},{4,0},{6,2},{8,12},{10,14},{12,8},{14,10},{16,20},{18,... | collective-permute-start | bytes 491528 | tf_op jit(solution)/shard_map/ppermute | solution.py:195
  89.6 145.6 %collective-permute-start.3 = (bf16[2,2,8,2560]{3,2,1,0:T(8,128)(2,1)}, bf16[2,2,8,2560]{3,2,1,0:T(8,128)(2,1)S(1)}, u32[]{:S(2)}, u32[]{:S(2)}) collective-permute-start(bf16[2,2,8,2560]{3,2,1,0:T(8,128)(2,1)} %get-tuple-element.31), channel_id=1, source_target_pairs={{0,6},{2,4},{4,2},{6,0},{8,14},{10,12},{12,10},{14,8},{16,22},{18,... | collective-permute-start | bytes 491528 | tf_op jit(solution)/shard_map/ppermute | solution.py:195
  89.9 145.6 %collective-permute-start.4 = (bf16[2,2,8,2560]{3,2,1,0:T(8,128)(2,1)}, bf16[2,2,8,2560]{3,2,1,0:T(8,128)(2,1)S(1)}, u32[]{:S(2)}, u32[]{:S(2)}) collective-permute-start(bf16[2,2,8,2560]{3,2,1,0:T(8,128)(2,1)} %get-tuple-element.32), channel_id=1, source_target_pairs={{0,8},{2,10},{4,12},{6,14},{8,0},{10,2},{12,4},{14,6},{16,24},{18,... | collective-permute-start | bytes 491528 | tf_op jit(solution)/shard_map/ppermute | solution.py:195
  235.5 31.2 %collective-permute-start.9 = (bf16[2,2,8,2560]{3,2,1,0:T(8,128)(2,1)}, bf16[2,2,8,2560]{3,2,1,0:T(8,128)(2,1)S(1)}, u32[]{:S(2)}, u32[]{:S(2)}) collective-permute-start(bf16[2,2,8,2560]{3,2,1,0:T(8,128)(2,1)} %get-tuple-element.37), channel_id=1, source_target_pairs={{0,18},{2,16},{4,22},{6,20},{8,26},{10,24},{12,30},{14,28},{16,2},... | collective-permute-start | bytes 491528 | tf_op jit(solution)/shard_map/ppermute | solution.py:195
  238.8 33.6 %collective-permute-start.10 = (bf16[2,2,8,2560]{3,2,1,0:T(8,128)(2,1)}, bf16[2,2,8,2560]{3,2,1,0:T(8,128)(2,1)S(1)}, u32[]{:S(2)}, u32[]{:S(2)}) collective-permute-start(bf16[2,2,8,2560]{3,2,1,0:T(8,128)(2,1)} %get-tuple-element.38), channel_id=1, source_target_pairs={{0,20},{2,22},{4,16},{6,18},{8,28},{10,30},{12,24},{14,26},{16,4},... | collective-permute-start | bytes 491528 | tf_op jit(solution)/shard_map/ppermute | solution.py:195
  247.1 34.6 %collective-permute-start.11 = (bf16[2,2,8,2560]{3,2,1,0:T(8,128)(2,1)}, bf16[2,2,8,2560]{3,2,1,0:T(8,128)(2,1)S(1)}, u32[]{:S(2)}, u32[]{:S(2)}) collective-permute-start(bf16[2,2,8,2560]{3,2,1,0:T(8,128)(2,1)} %get-tuple-element.39), channel_id=1, source_target_pairs={{0,22},{2,20},{4,18},{6,16},{8,30},{10,28},{12,26},{14,24},{16,6},... | collective-permute-start | bytes 491528 | tf_op jit(solution)/shard_map/ppermute | solution.py:195
  251.6 32.8 %collective-permute-start.12 = (bf16[2,2,8,2560]{3,2,1,0:T(8,128)(2,1)}, bf16[2,2,8,2560]{3,2,1,0:T(8,128)(2,1)S(1)}, u32[]{:S(2)}, u32[]{:S(2)}) collective-permute-start(bf16[2,2,8,2560]{3,2,1,0:T(8,128)(2,1)} %get-tuple-element.40), channel_id=1, source_target_pairs={{0,24},{2,26},{4,28},{6,30},{8,16},{10,18},{12,20},{14,22},{16,8},... | collective-permute-start | bytes 491528 | tf_op jit(solution)/shard_map/ppermute | solution.py:195
  255.9 28.4 %collective-permute-start.13 = (bf16[2,2,8,2560]{3,2,1,0:T(8,128)(2,1)}, bf16[2,2,8,2560]{3,2,1,0:T(8,128)(2,1)S(1)}, u32[]{:S(2)}, u32[]{:S(2)}) collective-permute-start(bf16[2,2,8,2560]{3,2,1,0:T(8,128)(2,1)} %get-tuple-element.41), channel_id=1, source_target_pairs={{0,26},{2,24},{4,30},{6,28},{8,18},{10,16},{12,22},{14,20},{16,10}... | collective-permute-start | bytes 491528 | tf_op jit(solution)/shard_map/ppermute | solution.py:195
  281.7 27.0 %collective-permute-start.17 = (bf16[1280,320]{0,1:T(8,128)(2,1)}, bf16[1280,320]{0,1:T(8,128)(2,1)S(1)}, u32[]{:S(2)}, u32[]{:S(2)}) collective-permute-start(bf16[1280,320]{0,1:T(8,128)(2,1)} %get-tuple-element.59), channel_id=1, source_target_pairs={{0,2},{2,0},{4,6},{6,4},{8,10},{10,8},{12,14},{14,12},{16,18},{18,... | collective-permute-start | bytes 2457608 | tf_op jit(solution)/shard_map/ppermute | solution.py:195
  296.7 68.7 %collective-permute-start.16 = (bf16[256,2560]{1,0:T(8,128)(2,1)S(1)}, bf16[256,2560]{1,0:T(8,128)(2,1)}, u32[]{:S(2)}, u32[]{:S(2)}) collective-permute-start(bf16[256,2560]{1,0:T(8,128)(2,1)S(1)} %self_attention.1), channel_id=1, source_target_pairs={{0,8},{2,10},{4,12},{6,14},{8,0},{10,2},{12,4},{14,6},{16,24},{18,... | collective-permute-start | bytes 3932168 | tf_op jit(solution)/shard_map/ppermute | solution.py:195
  310.4 34.5 %collective-permute-start.21 = (bf16[1280,128]{0,1:T(8,128)(2,1)}, bf16[1280,128]{0,1:T(8,128)(2,1)}, u32[]{:S(2)}, u32[]{:S(2)}) collective-permute-start(bf16[1280,128]{0,1:T(8,128)(2,1)} %get-tuple-element.44), channel_id=1, source_target_pairs={{0,16},{2,18},{4,20},{6,22},{8,24},{10,26},{12,28},{14,30},{16,0},... | collective-permute-start | bytes 983048 | tf_op jit(solution)/shard_map/ppermute | solution.py:195
  310.4 41.0 %collective-permute-start.25 = (bf16[1280,128]{0,1:T(8,128)(2,1)}, bf16[1280,128]{0,1:T(8,128)(2,1)S(1)}, u32[]{:S(2)}, u32[]{:S(2)}) collective-permute-start(bf16[1280,128]{0,1:T(8,128)(2,1)} %get-tuple-element.45), channel_id=1, source_target_pairs={{0,16},{2,18},{4,20},{6,22},{8,24},{10,26},{12,28},{14,30},{16,0},... | collective-permute-start | bytes 983048 | tf_op jit(solution)/shard_map/ppermute | solution.py:195
  313.5 128.9 %collective-permute-start.18 = (bf16[1280,640]{0,1:T(8,128)(2,1)S(1)}, bf16[1280,640]{0,1:T(8,128)(2,1)S(1)}, u32[]{:S(2)}, u32[]{:S(2)}) collective-permute-start(bf16[1280,640]{0,1:T(8,128)(2,1)S(1)} %maximum_select_fusion.1), channel_id=1, source_target_pairs={{0,4},{2,6},{4,0},{6,2},{8,12},{10,14},{12,8},{14,10},{16,20},{18,... | collective-permute-start | bytes 4915208 | tf_op jit(solution)/shard_map/ppermute | solution.py:195
  359.3 38.1 %collective-permute-start.23 = (bf16[1280,256]{0,1:T(8,128)(2,1)S(1)}, bf16[1280,256]{0,1:T(8,128)(2,1)S(1)}, u32[]{:S(2)}, u32[]{:S(2)}) collective-permute-start(bf16[1280,256]{0,1:T(8,128)(2,1)S(1)} %constant_dynamic-update-slice_fusion), channel_id=1, source_target_pairs={{0,2},{2,0},{4,6},{6,4},{8,10},{10,8},{12,14},{14,12},{16,18},{18,... | collective-permute-start | bytes 1966088 | tf_op jit(solution)/shard_map/ppermute | solution.py:195
  364.9 35.6 %collective-permute-start.27 = (bf16[1280,256]{0,1:T(8,128)(2,1)S(1)}, bf16[1280,256]{0,1:T(8,128)(2,1)S(1)}, u32[]{:S(2)}, u32[]{:S(2)}) collective-permute-start(bf16[1280,256]{0,1:T(8,128)(2,1)S(1)} %constant_dynamic-update-slice_fusion.2), channel_id=1, source_target_pairs={{0,2},{2,0},{4,6},{6,4},{8,10},{10,8},{12,14},{14,12},{16,18},{18,... | collective-permute-start | bytes 1966088 | tf_op jit(solution)/shard_map/ppermute | solution.py:195
  365.0 24.9 %collective-permute-start.29 = (bf16[1280,128]{0,1:T(8,128)(2,1)S(1)}, bf16[1280,128]{0,1:T(8,128)(2,1)S(1)}, u32[]{:S(2)}, u32[]{:S(2)}) collective-permute-start(bf16[1280,128]{0,1:T(8,128)(2,1)S(1)} %copy-done.9), channel_id=1, source_target_pairs={{0,16},{2,18},{4,20},{6,22},{8,24},{10,26},{12,28},{14,30},{16,0},... | collective-permute-start | bytes 983048 | tf_op jit(solution)/shard_map/ppermute | solution.py:195
  365.4 31.5 %collective-permute-start.33 = (bf16[1280,128]{0,1:T(8,128)(2,1)S(1)}, bf16[1280,128]{0,1:T(8,128)(2,1)S(1)}, u32[]{:S(2)}, u32[]{:S(2)}) collective-permute-start(bf16[1280,128]{0,1:T(8,128)(2,1)S(1)} %copy-done.8), channel_id=1, source_target_pairs={{0,16},{2,18},{4,20},{6,22},{8,24},{10,26},{12,28},{14,30},{16,0},... | collective-permute-start | bytes 983048 | tf_op jit(solution)/shard_map/ppermute | solution.py:195
  400.6 42.1 %collective-permute-start.31 = (bf16[1280,256]{0,1:T(8,128)(2,1)S(1)}, bf16[1280,256]{0,1:T(8,128)(2,1)S(1)}, u32[]{:S(2)}, u32[]{:S(2)}) collective-permute-start(bf16[1280,256]{0,1:T(8,128)(2,1)S(1)} %constant_dynamic-update-slice_fusion.4), channel_id=1, source_target_pairs={{0,2},{2,0},{4,6},{6,4},{8,10},{10,8},{12,14},{14,12},{16,18},{18,... | collective-permute-start | bytes 1966088 | tf_op jit(solution)/shard_map/ppermute | solution.py:195
  442.7 32.7 %collective-permute-start.19 = (bf16[1280,1280]{0,1:T(8,128)(2,1)S(1)}, bf16[1280,1280]{0,1:T(8,128)(2,1)S(1)}, u32[]{:S(2)}, u32[]{:S(2)}) collective-permute-start(bf16[1280,1280]{0,1:T(8,128)(2,1)S(1)} %pad_maximum_fusion), channel_id=1, source_target_pairs={{0,2},{2,0},{4,6},{6,4},{8,10},{10,8},{12,14},{14,12},{16,18},{18,... | collective-permute-start | bytes 9830408 | tf_op jit(solution)/shard_map/ppermute | solution.py:195
  479.3 30.7 %collective-permute-start.20 = (bf16[256,1280]{1,0:T(8,128)(2,1)S(1)}, bf16[256,1280]{1,0:T(8,128)(2,1)S(1)}, u32[]{:S(2)}, u32[]{:S(2)}) collective-permute-start(bf16[256,1280]{1,0:T(8,128)(2,1)S(1)} %get-tuple-element.63), channel_id=1, source_target_pairs={{1,0},{3,2},{5,4},{7,6},{9,8},{11,10},{13,12},{15,14},{16,17},{18,... | collective-permute-start | bytes 1966088 | tf_op jit(solution)/shard_map/ppermute | solution.py:264
  480.6 29.6 %collective-permute-start.42 = (bf16[256,1280]{1,0:T(8,128)(2,1)S(1)}, bf16[256,1280]{1,0:T(8,128)(2,1)S(1)}, u32[]{:S(2)}, u32[]{:S(2)}) collective-permute-start(bf16[256,1280]{1,0:T(8,128)(2,1)S(1)} %get-tuple-element.62), channel_id=1, source_target_pairs={{1,8},{3,10},{5,12},{7,14},{9,0},{11,2},{13,4},{15,6},{16,25},{18,... | collective-permute-start | bytes 1966088 | tf_op jit(solution)/shard_map/ppermute | solution.py:266
  481.9 28.3 %collective-permute-start.41 = (bf16[256,1280]{1,0:T(8,128)(2,1)S(1)}, bf16[256,1280]{1,0:T(8,128)(2,1)S(1)}, u32[]{:S(2)}, u32[]{:S(2)}) collective-permute-start(bf16[256,1280]{1,0:T(8,128)(2,1)S(1)} %get-tuple-element.62), channel_id=1, source_target_pairs={{0,8},{2,10},{4,12},{6,14},{8,0},{10,2},{12,4},{14,6},{17,25},{19,... | collective-permute-start | bytes 1966088 | tf_op jit(solution)/shard_map/ppermute | solution.py:265
  (48 other events, 1338.7 us)

commit v2 on v1

v2 whole, which is shorter than its diff:
```python
import functools
import math

import jax
import jax.numpy as jnp
from jax import lax
from jax.experimental import pallas as pl
from jax.experimental.pallas import tpu as pltpu
from jax.sharding import PartitionSpec as P

HD = 128
CAP = 2
EPS = 1e-06
VMEM_LIMIT = 48 * 1024 * 1024
COST = pl.CostEstimate(flops=1, bytes_accessed=1, transcendentals=0)


def pack_kernel(dest_ref, page_ref, keys_ref, values_ref, out_ref, table, count, sems):
    peers = count.shape[0]

    @pl.loop(0, peers)
    def _(r):
        count[r] = 0

    @pl.loop(0, dest_ref.shape[0])
    def _(i):
        r = dest_ref[i, 0]
        c = jnp.minimum(count[r], CAP - 1)
        table[r * CAP + c] = page_ref[0, i]
        count[r] = c + 1

    def copies(slot, page):
        return [
            pltpu.make_async_copy(source.at[page], out_ref.at[slot, half], sems.at[slot * 2 + half])
            for half, source in enumerate((keys_ref, values_ref))
        ]

    for r in range(peers):
        for c in range(CAP):
            slot = r * CAP + c

            @pl.when(c < count[r])
            def _():
                for copy in copies(slot, table[slot]):
                    copy.start()

            @pl.when(c >= count[r])
            def _():
                out_ref[slot, 0] = jnp.full(out_ref.shape[2:], jnp.inf, out_ref.dtype)
                out_ref[slot, 1] = jnp.zeros(out_ref.shape[2:], out_ref.dtype)

    for r in range(peers):
        for c in range(CAP):
            slot = r * CAP + c

            @pl.when(c < count[r])
            def _():
                for copy in copies(slot, 0):
                    copy.wait()


def pack_pages(dest, pages, cache_keys, cache_values, peers):
    _, page_len, width = cache_keys.shape
    smem = pl.BlockSpec(memory_space=pltpu.SMEM)
    hbm = pl.BlockSpec(memory_space=pl.ANY)
    return pl.pallas_call(
        pack_kernel,
        out_shape=jax.ShapeDtypeStruct((peers * CAP, 2, page_len, width), cache_keys.dtype),
        in_specs=[smem, smem, hbm, hbm],
        out_specs=pl.BlockSpec(memory_space=pltpu.VMEM),
        scratch_shapes=[
            pltpu.SMEM((peers * CAP,), jnp.int32),
            pltpu.SMEM((peers,), jnp.int32),
            pltpu.SemaphoreType.DMA((peers * CAP * 2,)),
        ],
        compiler_params=pltpu.CompilerParams(vmem_limit_bytes=VMEM_LIMIT),
        cost_estimate=COST,
        name="pack_pages",
    )(dest, pages, cache_keys, cache_values)


def resident_kernel(table_ref, keys_ref, values_ref, out_keys, out_values, sems):
    copies = []
    for j in range(table_ref.shape[0]):
        page = table_ref[j]
        for half, (source, target) in enumerate(((keys_ref, out_keys), (values_ref, out_values))):
            copy = pltpu.make_async_copy(source.at[page], target.at[j], sems.at[j * 2 + half])
            copy.start()
            copies.append(copy)
    for copy in copies:
        copy.wait()


def resident_pages(table, cache_keys, cache_values):
    pages = table.shape[0]
    hbm = pl.BlockSpec(memory_space=pl.ANY)
    vmem = pl.BlockSpec(memory_space=pltpu.VMEM)
    shape = jax.ShapeDtypeStruct((pages,) + cache_keys.shape[1:], cache_keys.dtype)
    return pl.pallas_call(
        resident_kernel,
        out_shape=[shape, shape],
        in_specs=[pl.BlockSpec(memory_space=pltpu.SMEM), hbm, hbm],
        out_specs=[vmem, vmem],
        scratch_shapes=[pltpu.SemaphoreType.DMA((pages * 2,))],
        compiler_params=pltpu.CompilerParams(vmem_limit_bytes=VMEM_LIMIT),
        cost_estimate=COST,
        name="resident_pages",
    )(table, cache_keys, cache_values)


STAT_ROWS = 16
FACTOR = math.log2(math.e) / math.sqrt(HD)


def head_scores(query, keys):
    return lax.dot_general(keys, query, (((1,), (1,)), ((), ())), preferred_element_type=jnp.float32)


def weigh(scores, row_max, values):
    exponent = jnp.exp2((scores - row_max) * FACTOR)
    mixed = lax.dot_general(
        values, exponent.astype(jnp.bfloat16), (((0,), (0,)), ((), ())), preferred_element_type=jnp.float32
    )
    return mixed, jnp.sum(exponent, axis=0, keepdims=True)


def local_kernel(heads, length_ref, q_ref, rk_ref, rv_ref, k_ref, v_ref, sum_ref, stat_ref):
    resident = rk_ref.shape[0] * rk_ref.shape[1]
    position = lax.broadcasted_iota(jnp.int32, (resident, q_ref.shape[0]), 0)
    for h in range(heads):
        part = slice(h * HD, (h + 1) * HD)
        query = q_ref[:, part]
        values = jnp.concatenate([rv_ref[:, :, part].reshape(-1, HD), v_ref[:, part]], axis=0)
        paged = head_scores(query, rk_ref[:, :, part].reshape(-1, HD))
        paged = jnp.where(position < length_ref[0], paged, -jnp.inf)
        scores = jnp.concatenate([paged, head_scores(query, k_ref[:, part])], axis=0)
        row_max = jnp.max(scores, axis=0, keepdims=True)
        mixed, denominator = weigh(scores, row_max, values)
        sum_ref[part] = mixed
        stat_ref[0, 2 * h : 2 * h + 1] = row_max
        stat_ref[0, 2 * h + 1 : 2 * h + 2] = denominator


def arrived_kernel(heads, usable_ref, q_ref, arrived_ref, sum_ref, stat_ref, out_ref):
    for h in range(heads):
        part = slice(h * HD, (h + 1) * HD)
        scores = head_scores(q_ref[:, part], arrived_ref[:, 0, :, part].reshape(-1, HD))
        scores = jnp.where(usable_ref[...] > 0, scores, -jnp.inf)
        local_max = stat_ref[0, 2 * h : 2 * h + 1]
        row_max = jnp.maximum(local_max, jnp.max(scores, axis=0, keepdims=True))
        mixed, denominator = weigh(scores, row_max, arrived_ref[:, 1, :, part].reshape(-1, HD))
        carry = jnp.exp2((local_max - row_max) * FACTOR)
        denominator = denominator + stat_ref[0, 2 * h + 1 : 2 * h + 2] * carry
        mixed = (mixed + sum_ref[part] * carry) / denominator
        out_ref[:, part] = jnp.transpose(mixed).astype(jnp.bfloat16)


def cross_kernel(heads, q_ref, k_ref, v_ref, out_ref):
    for h in range(heads):
        part = slice(h * HD, (h + 1) * HD)
        scores = head_scores(q_ref[:, part], k_ref[:, part])
        mixed, denominator = weigh(scores, jnp.max(scores, axis=0, keepdims=True), v_ref[:, part])
        out_ref[:, part] = jnp.transpose(mixed / denominator).astype(jnp.bfloat16)


def head_group(heads):
    for group in (5, 4, 3, 2):
        if heads % group == 0:
            return group
    return 1


def local_attention(length, query, res_keys, res_values, keys, values):
    tokens, width = query.shape
    group = head_group(width // HD)
    block = group * HD
    steps = width // block
    flat = pl.BlockSpec((tokens, block), lambda h: (0, h))
    paged = pl.BlockSpec(res_keys.shape[:2] + (block,), lambda h: (0, 0, h))
    return pl.pallas_call(
        functools.partial(local_kernel, group),
        out_shape=[
            jax.ShapeDtypeStruct((width, tokens), jnp.float32),
            jax.ShapeDtypeStruct((steps, STAT_ROWS, tokens), jnp.float32),
        ],
        grid=(steps,),
        in_specs=[pl.BlockSpec(memory_space=pltpu.SMEM), flat, paged, paged, flat, flat],
        out_specs=[
            pl.BlockSpec((block, tokens), lambda h: (h, 0)),
            pl.BlockSpec((1, STAT_ROWS, tokens), lambda h: (h, 0, 0)),
        ],
        compiler_params=pltpu.CompilerParams(vmem_limit_bytes=VMEM_LIMIT),
        cost_estimate=COST,
        name="local_attention",
    )(length, query, res_keys, res_values, keys, values)


def arrived_attention(usable, query, arrived, sums, stats):
    tokens, width = query.shape
    steps = stats.shape[0]
    block = width // steps
    flat = pl.BlockSpec((tokens, block), lambda h: (0, h))
    return pl.pallas_call(
        functools.partial(arrived_kernel, block // HD),
        out_shape=jax.ShapeDtypeStruct((tokens, width), query.dtype),
        grid=(steps,),
        in_specs=[
            pl.BlockSpec(usable.shape, lambda h: (0, 0)),
            flat,
            pl.BlockSpec(arrived.shape[:3] + (block,), lambda h: (0, 0, 0, h)),
            pl.BlockSpec((block, tokens), lambda h: (h, 0)),
            pl.BlockSpec((1, STAT_ROWS, tokens), lambda h: (h, 0, 0)),
        ],
        out_specs=flat,
        compiler_params=pltpu.CompilerParams(vmem_limit_bytes=VMEM_LIMIT),
        cost_estimate=COST,
        name="arrived_attention",
    )(usable, query, arrived, sums, stats)


def cross_attention(query, keys, values):
    tokens, width = query.shape
    group = head_group(width // HD)
    block = group * HD
    flat = lambda rows: pl.BlockSpec((rows, block), lambda h: (0, h))
    count = keys.shape[0]
    return pl.pallas_call(
        functools.partial(cross_kernel, group),
        out_shape=jax.ShapeDtypeStruct((tokens, width), query.dtype),
        grid=(width // block,),
        in_specs=[flat(tokens), flat(count), flat(count)],
        out_specs=flat(tokens),
        compiler_params=pltpu.CompilerParams(vmem_limit_bytes=VMEM_LIMIT),
        cost_estimate=COST,
        name="cross_attention",
    )(query, keys, values)


def tp_sum(x):
    if lax.axis_size("tp") == 2:
        return x + lax.ppermute(x, "tp", [(0, 1), (1, 0)])
    return lax.psum(x, "tp")


def after(x, *earlier):
    return lax.optimization_barrier((x,) + earlier)[0]


def swap(x, bits):
    size = lax.axis_size("req")
    return lax.ppermute(x, "req", [(i, i ^ bits) for i in range(size)])


def partial_product(rows, weights):
    return jnp.dot(rows, weights, preferred_element_type=jnp.float32)


def projection_gathered(attended, out_weight):
    width = attended.shape[1]
    weights = lax.all_gather(out_weight, "req", axis=1, tiled=True)
    partial = partial_product(attended, weights).astype(jnp.bfloat16)
    column = lax.axis_index("tp") * width
    if lax.axis_size("tp") == 2:
        other = (lax.axis_size("tp") - 1) * width - column
        own = lax.dynamic_slice_in_dim(partial, column, width, 1)
        sent = lax.dynamic_slice_in_dim(partial, other, width, 1)
        received = lax.ppermute(sent, "tp", [(0, 1), (1, 0)])
        return own.astype(jnp.float32) + received.astype(jnp.float32)
    summed = lax.psum(partial, "tp").astype(jnp.float32)
    return lax.dynamic_slice_in_dim(summed, column, width, 1)


CORE, Y, Z1, Z2 = 1, 2, 4, 8
PIECES = (2, 2, 1)


def planes_weights(out_weight):
    half = out_weight.shape[0] // 2
    core = lax.axis_index("req") % 2
    mine = lax.dynamic_slice_in_dim(out_weight, core * half, half, 0)
    other = lax.dynamic_slice_in_dim(out_weight, (1 - core) * half, half, 0)
    got = swap(other, CORE)
    block = jnp.where(core == 0, jnp.concatenate([mine, got], axis=1), jnp.concatenate([got, mine], axis=1))
    unit = block.shape[1] // sum(PIECES)
    ends = [sum(PIECES[: j + 1]) * unit for j in range(len(PIECES))]
    return block, [lax.slice_in_dim(block, e - p * unit, e, axis=1) for e, p in zip(ends, PIECES)]


def planes_projection(block, pieces, late_0, arrived, attended):
    half = block.shape[0]
    tokens = attended.shape[0]
    me, x = lax.axis_index("req"), lax.axis_index("tp")
    core, y, z_low, z_high = me % 2, (me // 2) % 2, (me // 4) % 2, me // 8
    own_early = x == z_high

    block_y = after(swap(block, Y), attended)
    late = after(late_0, attended)
    rows = jnp.concatenate([attended, swap(attended, Z1)], axis=0)
    rows_mine = jnp.where(core == 0, rows[:, :half], rows[:, half:])
    rows_other = jnp.where(core == 0, rows[:, half:], rows[:, :half])

    def product(w):
        w_other = swap(w, CORE)
        return (partial_product(rows_mine, w) + partial_product(rows_other, w_other)).astype(jnp.bfloat16)

    early = product(block), product(block_y)
    own_parts, near_parts = [], []
    first = 0
    for j, piece in enumerate(pieces):
        size = piece.shape[1]
        if j == 1:
            arrival = swap(after(piece, late_0, attended), Z2)
            late = after(arrival, rows_mine)
        if j > 1:
            arrival = swap(after(piece, arrival), Z2)
            arrival = late = after(arrival, first_sent)
        late_part = product(jnp.concatenate([late, swap(late, Y)], axis=1))
        early_part = jnp.concatenate([e[:, first : first + size] for e in early], axis=1)
        first += size
        kept = jnp.where(own_early, early_part, late_part)
        sent = jnp.where(own_early, late_part, early_part)
        if j == 0:
            first_sent = sent
        received = lax.ppermute(sent, "tp", [(0, 1), (1, 0)])
        total = kept.astype(jnp.float32) + received.astype(jnp.float32)
        own_parts.append(total[:tokens])
        near_parts.append(swap(total[tokens:].astype(jnp.bfloat16), Z1).astype(jnp.float32))

    def ordered(parts):
        this = jnp.concatenate([p[:, : p.shape[1] // 2] for p in parts], axis=1)
        that = jnp.concatenate([p[:, p.shape[1] // 2 :] for p in parts], axis=1)
        return jnp.where(y == 0, jnp.concatenate([this, that], axis=1), jnp.concatenate([that, this], axis=1))

    own, near = ordered(own_parts), ordered(near_parts)
    return jnp.where(z_low == 0, jnp.concatenate([own, near], axis=1), jnp.concatenate([near, own], axis=1))


def shards(
    queries,
    new_keys,
    new_values,
    query_gain,
    key_gain,
    cache_keys,
    cache_values,
    page_table,
    cache_lens,
    mig_pages,
    mig_dest,
    cross_queries,
    text_keys,
    text_values,
    out_weight,
    residual,
    gate,
    shift,
    scale,
):
    tokens, width = queries.shape
    tp, peers = lax.axis_size("tp"), lax.axis_size("req")
    full_width = width * tp
    me = lax.axis_index("req")
    page_len = cache_keys.shape[1]

    packed = pack_pages(mig_dest, mig_pages, cache_keys, cache_values, peers)
    arrived = lax.all_to_all(packed, "req", split_axis=0, concat_axis=0, tiled=True)
    filled = (arrived[:, 0, 0, 0] < jnp.inf).astype(jnp.float32)
    arrived_usable = jnp.broadcast_to(filled[:, None, None], (filled.shape[0], page_len, tokens)).reshape(-1, tokens)

    planes = peers == 16 and tp == 2
    if planes:
        block, pieces = planes_weights(out_weight)
        page_table, cross_queries = after(page_table, block, *pieces), after(cross_queries, block, *pieces)

    query_float = queries.astype(jnp.float32)
    key_float = new_keys.astype(jnp.float32)
    squares = tp_sum(
        jnp.stack([jnp.sum(query_float * query_float, axis=1), jnp.sum(key_float * key_float, axis=1)])
    )
    inverse = lax.rsqrt(squares / full_width + EPS)
    query_normed = (query_float * inverse[0][:, None] * query_gain).astype(jnp.bfloat16)
    key_normed = (key_float * inverse[1][:, None] * key_gain).astype(jnp.bfloat16)

    res_keys, res_values = resident_pages(page_table[0], cache_keys, cache_values)
    sums, stats = local_attention(cache_lens, query_normed, res_keys, res_values, key_normed, new_values)
    cross_out = cross_attention(cross_queries, text_keys, text_values)
    sums = after(sums, cross_out)
    if planes:
        late_0 = swap(after(pieces[0], sums), Z2)
    attended = arrived_attention(arrived_usable, query_normed, arrived, sums, stats)
    if planes:
        projected = planes_projection(block, pieces, late_0, arrived, attended)
    else:
        projected = projection_gathered(attended, out_weight)

    updated = residual.astype(jnp.float32) + gate.astype(jnp.float32) * projected
    stream = updated.astype(jnp.bfloat16)
    local_mean = jnp.mean(updated, axis=1)
    local_square = jnp.sum(jnp.square(updated - local_mean[:, None]), axis=1)
    if tp == 2:
        theirs = lax.ppermute(jnp.stack([local_mean, local_square]), "tp", [(0, 1), (1, 0)])
        row_mean = (local_mean + theirs[0]) * 0.5
        gap = local_mean - theirs[0]
        row_var = (local_square + theirs[1] + gap * gap * (0.5 * width)) / full_width
    else:
        row_mean = lax.psum(local_mean, "tp") / tp
        offset = local_mean - row_mean
        row_var = lax.psum(local_square + width * offset * offset, "tp") / full_width
    normed = (
        (updated - row_mean[:, None]) * lax.rsqrt(row_var + EPS)[:, None] * (1.0 + scale.astype(jnp.float32))
        + shift.astype(jnp.float32)
    ).astype(jnp.bfloat16)
    return (stream, normed, cross_out)


def solution(mesh):
    in_specs = (
        P("req", "tp"),
        P("req", "tp"),
        P("req", "tp"),
        P("tp"),
        P("tp"),
        P("req", None, "tp"),
        P("req", None, "tp"),
        P("req", None),
        P("req"),
        P("req", None),
        P("req", None),
        P("req", "tp"),
        P("req", "tp"),
        P("req", "tp"),
        P("tp", "req"),
        P("req", "tp"),
        P("req", "tp"),
        P("req", "tp"),
        P("req", "tp"),
    )
    out_specs = (P("req", "tp"), P("req", "tp"), P("req", "tp"))
    return jax.shard_map(shards, mesh=mesh, in_specs=in_specs, out_specs=out_specs, check_vma=False)
```

time: 521 us -> 219 us (0.42)
  Pallas kernels: 220 us -> 32.2 us
  waiting for transfers between devices: 166 us -> 95.3 us
  starting transfers between devices: 88.6 us -> 38.2 us
  blocking collectives: 13 us -> 0 us
  matrix products: 9.19 us -> 18.7 us
  local copies, waits for them, and re-layouts: 9.21 us -> 17.2 us
    pallas_call x1, Pallas kernels: 122 us -> 3.66 us  [resident_pages(): pl.pallas_call(resident_kernel, out_shape=[shape, shape], in_specs=[pl.Bl...]
    pallas_call x2 -> x3, Pallas kernels: 94.5 us -> 24.3 us  [the longest x1 11.1 us: local_attention(): pl.pallas_call(functools.partial(local_kernel, group), out_shape=[jax.Sha...]
    ppermute x34 -> x17, waiting for transfers between devices: 129 us -> 59.6 us  [swap(): return lax.ppermute(x, 'req', [(i, i ^ bits) for i in range(size)])]
    ppermute x18 -> x3, starting transfers between devices: 40.7 us -> 3.63 us  [planes_projection(): received = lax.ppermute(sent, 'tp', [(0, 1), (1, 0)])]
    ppermute x18 -> x3, waiting for transfers between devices: 37.4 us -> 8.12 us  [planes_projection(): received = lax.ppermute(sent, 'tp', [(0, 1), (1, 0)])]
    all_to_all x0 -> x1, waiting for transfers between devices: none -> 25.6 us  [shards(): lax.all_to_all(packed, 'req', split_axis=0, concat_axis=0, tiled=True)]
    ppermute x34 -> x17, starting transfers between devices: 44.9 us -> 23.9 us  [swap(): return lax.ppermute(x, 'req', [(i, i ^ bits) for i in range(size)])]
    unnamed x1 -> x0, blocking collectives: 13 us -> none
  transfers between devices with their start and end apart: 54 -> 23, of which waited for: 22 -> 14; matrix products, arithmetic and copies ran while one was open for 3% -> 19% of each run, Pallas kernels for 42% -> 12%
where the time goes in v2:
time: 219 us; the launch traced here: 218 us
  waiting for transfers between devices  95.3 us (44%)
  starting transfers between devices  38.2 us (17%)
  Pallas kernels  32.2 us (15%)
  matrix products  18.7 us (9%)
  local copies, waits for them, and re-layouts  17.2 us (8%)
  other arithmetic  14.3 us (7%)
    ppermute x17, waiting for transfers between devices, swap(): return lax.ppermute(x, 'req', [(i, i ^ bits) for i in range(size)])  59.6 us
    all_to_all x1, waiting for transfers between devices, shards(): lax.all_to_all(packed, 'req', split_axis=0, concat_axis=0, tiled=True)  25.6 us
    ppermute x17, starting transfers between devices, swap(): return lax.ppermute(x, 'req', [(i, i ^ bits) for i in range(size)])  23.9 us
    dot_general x10, matrix products, partial_product(): return jnp.dot(rows, weights, preferred_element_type=jnp.float32)  18.7 us
    pallas_call x1, Pallas kernels, local_attention(): pl.pallas_call(functools.partial(local_kernel, group), out_shape=[jax.Sha...  11.1 us
    ppermute x3, waiting for transfers between devices, planes_projection(): received = lax.ppermute(sent, 'tp', [(0, 1), (1, 0)])  8.12 us
    pallas_call x1, Pallas kernels, arrived_attention(): pl.pallas_call(functools.partial(arrived_kernel, block // HD), out_shape=...  8 us
    unnamed x60, local copies, waits for them, and re-layouts  7.64 us
  transfers between devices with their start and end apart: 23, of which 14 were waited for; matrix products, arithmetic and copies ran while one was open for 19% of the time, Pallas kernels for 12%

profile of v2, /device:TPU:0, one launch (start us, length us, event | category | flops | bytes accessed | tf_op | source)
XLA Modules:
  0.0 217.9 jit_solution(1844140115184507852)
XLA Ops:
  3.8 5.2 %pack_pages.1 = bf16[32,2,8,2560]{3,2,1,0:T(8,128)(2,1)} custom-call(s32[16,1]{1,0:T(8,128)S(1)} %copy.29.dest_ref, s32[1,16]{1,0:T(1,128)S(1)} %copy-done.6, bf16[64,8,2560]{2,1,0:T(8,128)(2,1)S(1)} %copy-done, bf16[64,8,2560]{2,1,0:T(8,128)(2,1)} %values_ref.3), custom_call_target="tpu_custom_call" | custom-call | flops 1 | bytes 1 | tf_op jit(solution)/shard_map/pack_pages/pallas_call | solution.py:66
  9.0 7.5 %all-to-all-start = ((bf16[32,2,8,2560]{3,2,1,0:T(8,128)(2,1)}), bf16[32,2,8,2560]{3,2,1,0:T(8,128)(2,1)}, u32[]{:S(2)}, u32[]{:S(2)}) async-start(bf16[32,2,8,2560]{3,2,1,0:T(8,128)(2,1)} %pack_pages.1), calls=%async_computation | async-start | bytes 5242880 | tf_op jit(solution)/shard_map/all_to_all | solution.py:366
  19.8 2.4 %constant_dynamic-slice_fusion.1 = (bf16[1280,320]{0,1:T(8,128)(2,1)S(1)}, bf16[1280,320]{0,1:T(8,128)(2,1)}) fusion(bf16[2560,320]{0,1:T(8,128)(2,1)} %param.33, s32[]{:T(128)S(6)} %select_n.116, s32[]{:T(128)S(6)} %select_n.117), kind=kLoop, calls=%fused_computation.88 | loop fusion | bytes 3276808 | tf_op jit(solution)/shard_map/dynamic_slice | solution.py:280
  24.9 3.1 %maximum_select_fusion.1 = bf16[1280,640]{0,1:T(8,128)(2,1)} fusion(bf16[1280,320]{0,1:T(8,128)(2,1)} %collective-permute-done.1, bf16[1280,320]{0,1:T(8,128)(2,1)S(1)} %get-tuple-element.37, pred[]{:T(512)S(6)} %eq.23), kind=kLoop, calls=%fused_computation.17 | loop fusion | flops 7372800 | bytes 3276801 | tf_op jit(solution)/shard_map/jit(_where)/select_n | solution.py:283
  34.2 3.7 %resident_pages.1 = (bf16[48,8,2560]{2,1,0:T(8,128)(2,1)S(1)}, bf16[48,8,2560]{2,1,0:T(8,128)(2,1)S(1)}) custom-call(s32[48]{0:T(128)S(1)} %bitcast.29, bf16[64,8,2560]{2,1,0:T(8,128)(2,1)} %keys_ref.3, bf16[64,8,2560]{2,1,0:T(8,128)(2,1)} %values_ref.3), custom_call_target="tpu_custom_call" | custom-call | flops 1 | bytes 1 | tf_op jit(solution)/shard_map/resident_pages/pallas_call | solution.py:99
  38.0 4.2 %cross_attention.1 = bf16[256,2560]{1,0:T(8,128)(2,1)} custom-call(bf16[256,2560]{1,0:T(8,128)(2,1)S(1)} %copy-done.2, bf16[128,2560]{1,0:T(8,128)(2,1)S(1)} %copy-done.4, bf16[128,2560]{1,0:T(8,128)(2,1)S(1)} %copy-done.5), custom_call_target="tpu_custom_call" | custom-call | flops 1 | bytes 1 | tf_op jit(solution)/shard_map/cross_attention/pallas_call | solution.py:227
  42.1 11.1 %local_attention.1 = (f32[2560,256]{1,0:T(8,128)}, f32[4,16,256]{2,1,0:T(8,128)S(1)}) custom-call(s32[1]{0:T(128)S(6)} %copy.65.length_ref, bf16[256,2560]{1,0:T(8,128)(2,1)S(1)} %fusion.2.q_ref, bf16[48,8,2560]{2,1,0:T(8,128)(2,1)S(1)} %get-tuple-element.18.rk_ref, bf16[48,8,2560]{2,1,0:T(8,128)(2,1)} %copy-done.1, bf16[256,2560]{1,0:T(8,128)(2,1)S(1)} %fusion.5.k_ref, ...), custom_call_target="tpu_custom_call" | custom-call | flops 1 | bytes 1 | tf_op jit(solution)/shard_map/local_attention/pallas_call | solution.py:180
  53.2 2.4 %collective-permute-start.6 = (bf16[1280,256]{0,1:T(8,128)(2,1)}, bf16[1280,256]{0,1:T(8,128)(2,1)}, u32[]{:S(2)}, u32[]{:S(2)}) collective-permute-start(bf16[1280,256]{0,1:T(8,128)(2,1)} %get-tuple-element.25), channel_id=1, source_target_pairs={{0,16},{2,18},{4,20},{6,22},{8,24},{10,26},{12,28},{14,30},{16,0},... | collective-permute-start | bytes 1966088 | tf_op jit(solution)/shard_map/ppermute | solution.py:251
  55.6 25.6 %all-to-all-done.arrived_ref = bf16[32,2,8,2560]{3,2,1,0:T(8,128)(2,1)} async-done(((bf16[32,2,8,2560]{3,2,1,0:T(8,128)(2,1)}), bf16[32,2,8,2560]{3,2,1,0:T(8,128)(2,1)}, u32[]{:S(2)}, u32[]{:S(2)}) %all-to-all-start) | async-done | bytes 2621472 | tf_op jit(solution)/shard_map/all_to_all | solution.py:366
  82.6 8.0 %arrived_attention.1 = bf16[256,2560]{1,0:T(8,128)(2,1)S(1)} custom-call(f32[256,256]{1,0:T(8,128)S(1)} %broadcast_in_dim.8.usable_ref, bf16[256,2560]{1,0:T(8,128)(2,1)S(1)} %fusion.2.q_ref, bf16[32,2,8,2560]{3,2,1,0:T(8,128)(2,1)} %all-to-all-done.arrived_ref, f32[2560,256]{1,0:T(8,128)} %get-tuple-element.22.sum_ref, ...), custom_call_target="tpu_custom_call" | custom-call | flops 1 | bytes 1 | tf_op jit(solution)/shard_map/arrived_attention/pallas_call | solution.py:203
  90.6 9.1 %collective-permute-start.2 = (bf16[256,2560]{1,0:T(8,128)(2,1)S(1)}, bf16[256,2560]{1,0:T(8,128)(2,1)}, u32[]{:S(2)}, u32[]{:S(2)}) collective-permute-start(bf16[256,2560]{1,0:T(8,128)(2,1)S(1)} %arrived_attention.1), channel_id=1, source_target_pairs={{0,8},{2,10},{4,12},{6,14},{8,0},{10,2},{12,4},{14,6},{16,24},{18,... | collective-permute-start | bytes 3932168 | tf_op jit(solution)/shard_map/ppermute | solution.py:251
  99.7 5.6 %collective-permute-done.6 = bf16[1280,256]{0,1:T(8,128)(2,1)} collective-permute-done((bf16[1280,256]{0,1:T(8,128)(2,1)}, bf16[1280,256]{0,1:T(8,128)(2,1)}, u32[]{:S(2)}, u32[]{:S(2)}) %collective-permute-start.6) | collective-permute-done | bytes 655392 | tf_op jit(solution)/shard_map/ppermute | solution.py:251
  108.0 13.7 %collective-permute-done.7 = bf16[1280,256]{0,1:T(8,128)(2,1)S(1)} collective-permute-done((bf16[1280,256]{0,1:T(8,128)(2,1)}, bf16[1280,256]{0,1:T(8,128)(2,1)S(1)}, u32[]{:S(2)}, u32[]{:S(2)}) %collective-permute-start.7) | collective-permute-done | bytes 655392 | tf_op jit(solution)/shard_map/ppermute | solution.py:251
  121.8 19.3 %collective-permute-done.10 = bf16[1280,256]{0,1:T(8,128)(2,1)S(1)} collective-permute-done((bf16[1280,256]{0,1:T(8,128)(2,1)S(1)}, bf16[1280,256]{0,1:T(8,128)(2,1)S(1)}, u32[]{:S(2)}, u32[]{:S(2)}) %collective-permute-start.10) | collective-permute-done | bytes 655392 | tf_op jit(solution)/shard_map/ppermute | solution.py:251
  141.2 3.4 %collective-permute-start.14 = (bf16[1280,128]{0,1:T(8,128)(2,1)S(1)}, bf16[1280,128]{0,1:T(8,128)(2,1)S(1)}, u32[]{:S(2)}, u32[]{:S(2)}) collective-permute-start(bf16[1280,128]{0,1:T(8,128)(2,1)S(1)} %copy-done.18), channel_id=1, source_target_pairs={{0,16},{2,18},{4,20},{6,22},{8,24},{10,26},{12,28},{14,30},{16,0},... | collective-permute-start | bytes 983048 | tf_op jit(solution)/shard_map/ppermute | solution.py:251
  144.5 4.5 %collective-permute-done.2 = bf16[256,2560]{1,0:T(8,128)(2,1)} collective-permute-done((bf16[256,2560]{1,0:T(8,128)(2,1)S(1)}, bf16[256,2560]{1,0:T(8,128)(2,1)}, u32[]{:S(2)}, u32[]{:S(2)}) %collective-permute-start.2) | collective-permute-done | bytes 1310752 | tf_op jit(solution)/shard_map/ppermute | solution.py:251
  151.2 3.0 %fusion.22 = f32[512,640]{1,0:T(8,128)S(1)} fusion(bf16[512,1280]{1,0:T(8,128)(2,1)S(1)} %get-tuple-element.34, bf16[1280,640]{0,1:T(8,128)(2,1)} %collective-permute-done.3), kind=kOutput, calls=%fused_computation.96 | convolution fusion | flops 838860800 | bytes 4259840 | tf_op jit(solution)/shard_map/dot_general | solution.py:255
  154.2 2.7 %fusion.8 = bf16[512,640]{1,0:T(8,128)(2,1)S(1)} fusion(f32[512,640]{1,0:T(8,128)S(1)} %fusion.22, bf16[512,1280]{1,0:T(8,128)(2,1)S(1)} %get-tuple-element.33, bf16[1280,640]{0,1:T(8,128)(2,1)} %maximum_select_fusion.1), kind=kOutput, calls=%fused_computation.22 | convolution fusion | flops 839516160 | bytes 4915200 | tf_op jit(solution)/shard_map/dot_general | solution.py:255
  159.1 2.7 %fusion.9 = bf16[512,640]{1,0:T(8,128)(2,1)S(1)} fusion(f32[512,640]{1,0:T(8,128)S(1)} %fusion.23, bf16[512,1280]{1,0:T(8,128)(2,1)S(1)} %get-tuple-element.33, bf16[1280,640]{0,1:T(8,128)(2,1)} %collective-permute-done.4), kind=kOutput, calls=%fused_computation.23 | convolution fusion | flops 839516160 | bytes 4915200 | tf_op jit(solution)/shard_map/dot_general | solution.py:255
  168.7 6.6 %collective-permute-done.15 = bf16[1280,128]{0,1:T(8,128)(2,1)S(1)} collective-permute-done((bf16[1280,128]{0,1:T(8,128)(2,1)S(1)}, bf16[1280,128]{0,1:T(8,128)(2,1)S(1)}, u32[]{:S(2)}, u32[]{:S(2)}) %collective-permute-start.15) | collective-permute-done | bytes 327712 | tf_op jit(solution)/shard_map/ppermute | solution.py:251
  192.7 3.2 %collective-permute-done.20 = bf16[256,256]{1,0:T(8,128)(2,1)S(1)} collective-permute-done((bf16[256,256]{1,0:T(8,128)(2,1)S(1)}, bf16[256,256]{1,0:T(8,128)(2,1)S(1)}, u32[]{:S(2)}, u32[]{:S(2)}) %collective-permute-start.20) | collective-permute-done | bytes 131104 | tf_op jit(solution)/shard_map/ppermute | solution.py:251
  196.0 5.7 %collective-permute-done.13 = bf16[512,512]{1,0:T(8,128)(2,1)S(1)} collective-permute-done((bf16[512,512]{1,0:T(8,128)(2,1)S(1)}, bf16[512,512]{1,0:T(8,128)(2,1)S(1)}, u32[]{:S(2)}, u32[]{:S(2)}) %collective-permute-start.13) | collective-permute-done | bytes 524320 | tf_op jit(solution)/shard_map/ppermute | solution.py:324
  203.9 4.9 %collective-permute-done.19 = bf16[256,512]{1,0:T(8,128)(2,1)S(1)} collective-permute-done((bf16[256,512]{1,0:T(8,128)(2,1)S(1)}, bf16[256,512]{1,0:T(8,128)(2,1)S(1)}, u32[]{:S(2)}, u32[]{:S(2)}) %collective-permute-start.19) | collective-permute-done | bytes 262176 | tf_op jit(solution)/shard_map/ppermute | solution.py:251
  215.3 2.6 %add_convert_fusion = (bf16[256,2560]{1,0:T(8,128)(2,1)}, bf16[256,2560]{1,0:T(8,128)(2,1)}) fusion(f32[2560]{0:T(1024)S(1)} %get-tuple-element.81, f32[2560]{0:T(1024)S(1)} %add_reduce_fusion, f32[256]{0:T(256)S(1)} %get-tuple-element.68, f32[256]{0:T(256)S(1)} %get-tuple-element.67, f32[256,1280]{1,0:T(8,128)S(1)} %get-tuple-element.80, ...), kind=kLoop, calls=%fused_computation.15 | loop fusion | flops 7864320 | bytes 6586369 | tf_op jit(solution)/shard_map/convert_element_type | solution.py:412
  (141 shorter events, 55.8 us)
Async XLA Ops:
  9.0 72.1 %all-to-all-start = ((bf16[32,2,8,2560]{3,2,1,0:T(8,128)(2,1)}), bf16[32,2,8,2560]{3,2,1,0:T(8,128)(2,1)}, u32[]{:S(2)}, u32[]{:S(2)}) async-start(bf16[32,2,8,2560]{3,2,1,0:T(8,128)(2,1)} %pack_pages.1), calls=%async_computation | async-start | bytes 5242880 | tf_op jit(solution)/shard_map/all_to_all | solution.py:366
  18.2 4.7 %collective-permute-start = (f32[2,256]{1,0:T(2,128)S(1)}, f32[2,256]{1,0:T(2,128)S(1)}, u32[]{:S(2)}, u32[]{:S(2)}) collective-permute-start(f32[2,256]{1,0:T(2,128)S(1)} %pad_maximum_fusion.4), channel_id=1, source_target_pairs={{0,1},{1,0},{2,3},{3,2},{4,5},{5,4},{6,7},{7,6},{8,9},{9,8},{10,11... | collective-permute-start | bytes 6152 | tf_op jit(solution)/shard_map/ppermute | solution.py:241
  22.2 2.7 %collective-permute-start.1 = (bf16[1280,320]{0,1:T(8,128)(2,1)}, bf16[1280,320]{0,1:T(8,128)(2,1)}, u32[]{:S(2)}, u32[]{:S(2)}) collective-permute-start(bf16[1280,320]{0,1:T(8,128)(2,1)} %get-tuple-element.38), channel_id=1, source_target_pairs={{0,2},{2,0},{4,6},{6,4},{8,10},{10,8},{12,14},{14,12},{16,18},{18,... | collective-permute-start | bytes 2457608 | tf_op jit(solution)/shard_map/ppermute | solution.py:251
  28.0 78.7 %collective-permute-start.4 = (bf16[1280,640]{0,1:T(8,128)(2,1)}, bf16[1280,640]{0,1:T(8,128)(2,1)}, u32[]{:S(2)}, u32[]{:S(2)}) collective-permute-start(bf16[1280,640]{0,1:T(8,128)(2,1)} %maximum_select_fusion.1), channel_id=1, source_target_pairs={{0,4},{2,6},{4,0},{6,2},{8,12},{10,14},{12,8},{14,10},{16,20},{18,... | collective-permute-start | bytes 4915208 | tf_op jit(solution)/shard_map/ppermute | solution.py:251
  53.2 52.1 %collective-permute-start.6 = (bf16[1280,256]{0,1:T(8,128)(2,1)}, bf16[1280,256]{0,1:T(8,128)(2,1)}, u32[]{:S(2)}, u32[]{:S(2)}) collective-permute-start(bf16[1280,256]{0,1:T(8,128)(2,1)} %get-tuple-element.25), channel_id=1, source_target_pairs={{0,16},{2,18},{4,20},{6,22},{8,24},{10,26},{12,28},{14,30},{16,0},... | collective-permute-start | bytes 1966088 | tf_op jit(solution)/shard_map/ppermute | solution.py:251
  90.6 58.5 %collective-permute-start.2 = (bf16[256,2560]{1,0:T(8,128)(2,1)S(1)}, bf16[256,2560]{1,0:T(8,128)(2,1)}, u32[]{:S(2)}, u32[]{:S(2)}) collective-permute-start(bf16[256,2560]{1,0:T(8,128)(2,1)S(1)} %arrived_attention.1), channel_id=1, source_target_pairs={{0,8},{2,10},{4,12},{6,14},{8,0},{10,2},{12,4},{14,6},{16,24},{18,... | collective-permute-start | bytes 3932168 | tf_op jit(solution)/shard_map/ppermute | solution.py:251
  99.7 51.5 %collective-permute-start.3 = (bf16[1280,640]{0,1:T(8,128)(2,1)}, bf16[1280,640]{0,1:T(8,128)(2,1)}, u32[]{:S(2)}, u32[]{:S(2)}) collective-permute-start(bf16[1280,640]{0,1:T(8,128)(2,1)} %maximum_select_fusion.1), channel_id=1, source_target_pairs={{0,2},{2,0},{4,6},{6,4},{8,10},{10,8},{12,14},{14,12},{16,18},{18,... | collective-permute-start | bytes 4915208 | tf_op jit(solution)/shard_map/ppermute | solution.py:251
  105.3 16.4 %collective-permute-start.7 = (bf16[1280,256]{0,1:T(8,128)(2,1)}, bf16[1280,256]{0,1:T(8,128)(2,1)S(1)}, u32[]{:S(2)}, u32[]{:S(2)}) collective-permute-start(bf16[1280,256]{0,1:T(8,128)(2,1)} %collective-permute-done.6), channel_id=1, source_target_pairs={{0,4},{2,6},{4,0},{6,2},{8,12},{10,14},{12,8},{14,10},{16,20},{18,... | collective-permute-start | bytes 1966088 | tf_op jit(solution)/shard_map/ppermute | solution.py:251
  106.8 34.4 %collective-permute-start.10 = (bf16[1280,256]{0,1:T(8,128)(2,1)S(1)}, bf16[1280,256]{0,1:T(8,128)(2,1)S(1)}, u32[]{:S(2)}, u32[]{:S(2)}) collective-permute-start(bf16[1280,256]{0,1:T(8,128)(2,1)S(1)} %get-tuple-element.27), channel_id=1, source_target_pairs={{0,16},{2,18},{4,20},{6,22},{8,24},{10,26},{12,28},{14,30},{16,0},... | collective-permute-start | bytes 1966088 | tf_op jit(solution)/shard_map/ppermute | solution.py:251
  106.8 34.4 %copy-start.18 = (bf16[1280,128]{0,1:T(8,128)(2,1)S(1)}, bf16[1280,128]{0,1:T(8,128)(2,1)}, u32[]{:S(2)}) copy-start(bf16[1280,128]{0,1:T(8,128)(2,1)} %slice.143) | copy-start | bytes 983044
  106.8 51.1 %collective-permute-start.5 = (bf16[1280,640]{0,1:T(8,128)(2,1)}, bf16[1280,640]{0,1:T(8,128)(2,1)S(1)}, u32[]{:S(2)}, u32[]{:S(2)}) collective-permute-start(bf16[1280,640]{0,1:T(8,128)(2,1)} %collective-permute-done.4), channel_id=1, source_target_pairs={{0,2},{2,0},{4,6},{6,4},{8,10},{10,8},{12,14},{14,12},{16,18},{18,... | collective-permute-start | bytes 4915208 | tf_op jit(solution)/shard_map/ppermute | solution.py:251
  121.7 40.1 %collective-permute-start.8 = (bf16[1280,512]{0,1:T(8,128)(2,1)S(1)}, bf16[1280,512]{0,1:T(8,128)(2,1)S(1)}, u32[]{:S(2)}, u32[]{:S(2)}) collective-permute-start(bf16[1280,512]{0,1:T(8,128)(2,1)S(1)} %constant_dynamic-update-slice_fusion), channel_id=1, source_target_pairs={{0,2},{2,0},{4,6},{6,4},{8,10},{10,8},{12,14},{14,12},{16,18},{18,... | collective-permute-start | bytes 3932168 | tf_op jit(solution)/shard_map/ppermute | solution.py:251
  141.2 24.8 %collective-permute-start.14 = (bf16[1280,128]{0,1:T(8,128)(2,1)S(1)}, bf16[1280,128]{0,1:T(8,128)(2,1)S(1)}, u32[]{:S(2)}, u32[]{:S(2)}) collective-permute-start(bf16[1280,128]{0,1:T(8,128)(2,1)S(1)} %copy-done.18), channel_id=1, source_target_pairs={{0,16},{2,18},{4,20},{6,22},{8,24},{10,26},{12,28},{14,30},{16,0},... | collective-permute-start | bytes 983048 | tf_op jit(solution)/shard_map/ppermute | solution.py:251
  151.1 16.7 %collective-permute-start.11 = (bf16[1280,256]{0,1:T(8,128)(2,1)S(1)}, bf16[1280,256]{0,1:T(8,128)(2,1)S(1)}, u32[]{:S(2)}, u32[]{:S(2)}) collective-permute-start(bf16[1280,256]{0,1:T(8,128)(2,1)S(1)} %copy-done.17), channel_id=1, source_target_pairs={{0,4},{2,6},{4,0},{6,2},{8,12},{10,14},{12,8},{14,10},{16,20},{18,... | collective-permute-start | bytes 1966088 | tf_op jit(solution)/shard_map/ppermute | solution.py:251
  164.5 14.1 %collective-permute-start.9 = (bf16[512,512]{1,0:T(8,128)(2,1)}, bf16[512,512]{1,0:T(8,128)(2,1)}, u32[]{:S(2)}, u32[]{:S(2)}) collective-permute-start(bf16[512,512]{1,0:T(8,128)(2,1)} %get-tuple-element.73), channel_id=1, source_target_pairs={{0,1},{1,0},{2,3},{3,2},{4,5},{5,4},{6,7},{7,6},{8,9},{9,8},{10,11... | collective-permute-start | bytes 1572872 | tf_op jit(solution)/shard_map/ppermute | solution.py:324
  165.9 9.4 %collective-permute-start.15 = (bf16[1280,128]{0,1:T(8,128)(2,1)S(1)}, bf16[1280,128]{0,1:T(8,128)(2,1)S(1)}, u32[]{:S(2)}, u32[]{:S(2)}) collective-permute-start(bf16[1280,128]{0,1:T(8,128)(2,1)S(1)} %collective-permute-done.14), channel_id=1, source_target_pairs={{0,4},{2,6},{4,0},{6,2},{8,12},{10,14},{12,8},{14,10},{16,20},{18,... | collective-permute-start | bytes 983048 | tf_op jit(solution)/shard_map/ppermute | solution.py:251
  168.7 15.1 %collective-permute-start.12 = (bf16[1280,512]{0,1:T(8,128)(2,1)}, bf16[1280,512]{0,1:T(8,128)(2,1)}, u32[]{:S(2)}, u32[]{:S(2)}) collective-permute-start(bf16[1280,512]{0,1:T(8,128)(2,1)} %constant_dynamic-update-slice_fusion.2), channel_id=1, source_target_pairs={{0,2},{2,0},{4,6},{6,4},{8,10},{10,8},{12,14},{14,12},{16,18},{18,... | collective-permute-start | bytes 3932168 | tf_op jit(solution)/shard_map/ppermute | solution.py:251
  175.3 4.7 %collective-permute-start.16 = (bf16[1280,256]{0,1:T(8,128)(2,1)S(1)}, bf16[1280,256]{0,1:T(8,128)(2,1)}, u32[]{:S(2)}, u32[]{:S(2)}) collective-permute-start(bf16[1280,256]{0,1:T(8,128)(2,1)S(1)} %constant_dynamic-update-slice_fusion.4), channel_id=1, source_target_pairs={{0,2},{2,0},{4,6},{6,4},{8,10},{10,8},{12,14},{14,12},{16,18},{18,... | collective-permute-start | bytes 1966088 | tf_op jit(solution)/shard_map/ppermute | solution.py:251
  180.0 8.9 %collective-permute-start.18 = (bf16[256,512]{1,0:T(8,128)(2,1)S(1)}, bf16[256,512]{1,0:T(8,128)(2,1)S(1)}, u32[]{:S(2)}, u32[]{:S(2)}) collective-permute-start(bf16[256,512]{1,0:T(8,128)(2,1)S(1)} %slice.213), channel_id=1, source_target_pairs={{0,8},{2,10},{4,12},{6,14},{8,0},{10,2},{12,4},{14,6},{16,24},{18,... | collective-permute-start | bytes 786440 | tf_op jit(solution)/shard_map/ppermute | solution.py:251
  182.3 8.5 %collective-permute-start.17 = (bf16[512,256]{1,0:T(8,128)(2,1)S(1)}, bf16[512,256]{1,0:T(8,128)(2,1)S(1)}, u32[]{:S(2)}, u32[]{:S(2)}) collective-permute-start(bf16[512,256]{1,0:T(8,128)(2,1)S(1)} %get-tuple-element.77), channel_id=1, source_target_pairs={{0,1},{1,0},{2,3},{3,2},{4,5},{5,4},{6,7},{7,6},{8,9},{9,8},{10,11... | collective-permute-start | bytes 786440 | tf_op jit(solution)/shard_map/ppermute | solution.py:324
  188.3 13.5 %collective-permute-start.13 = (bf16[512,512]{1,0:T(8,128)(2,1)S(1)}, bf16[512,512]{1,0:T(8,128)(2,1)S(1)}, u32[]{:S(2)}, u32[]{:S(2)}) collective-permute-start(bf16[512,512]{1,0:T(8,128)(2,1)S(1)} %get-tuple-element.75), channel_id=1, source_target_pairs={{0,1},{1,0},{2,3},{3,2},{4,5},{5,4},{6,7},{7,6},{8,9},{9,8},{10,11... | collective-permute-start | bytes 1572872 | tf_op jit(solution)/shard_map/ppermute | solution.py:324
  190.9 5.0 %collective-permute-start.20 = (bf16[256,256]{1,0:T(8,128)(2,1)S(1)}, bf16[256,256]{1,0:T(8,128)(2,1)S(1)}, u32[]{:S(2)}, u32[]{:S(2)}) collective-permute-start(bf16[256,256]{1,0:T(8,128)(2,1)S(1)} %slice.214), channel_id=1, source_target_pairs={{0,8},{2,10},{4,12},{6,14},{8,0},{10,2},{12,4},{14,6},{16,24},{18,... | collective-permute-start | bytes 393224 | tf_op jit(solution)/shard_map/ppermute | solution.py:251
  201.9 6.9 %collective-permute-start.19 = (bf16[256,512]{1,0:T(8,128)(2,1)S(1)}, bf16[256,512]{1,0:T(8,128)(2,1)S(1)}, u32[]{:S(2)}, u32[]{:S(2)}) collective-permute-start(bf16[256,512]{1,0:T(8,128)(2,1)S(1)} %slice.212), channel_id=1, source_target_pairs={{0,8},{2,10},{4,12},{6,14},{8,0},{10,2},{12,4},{14,6},{16,24},{18,... | collective-permute-start | bytes 786440 | tf_op jit(solution)/shard_map/ppermute | solution.py:251
  211.7 3.6 %collective-permute-start.21 = (f32[2,256]{1,0:T(2,128)S(1)}, f32[2,256]{1,0:T(2,128)S(1)}, u32[]{:S(2)}, u32[]{:S(2)}) collective-permute-start(f32[2,256]{1,0:T(2,128)S(1)} %pad_maximum_fusion.5), channel_id=1, source_target_pairs={{0,1},{1,0},{2,3},{3,2},{4,5},{5,4},{6,7},{7,6},{8,9},{9,8},{10,11... | collective-permute-start | bytes 6152 | tf_op jit(solution)/shard_map/ppermute | solution.py:401
  (22 other events, 83.3 us)

commit v3 on v2

--- a/solution.py
+++ b/solution.py
@@ -12,6 +12,7 @@
 CAP = 2
 EPS = 1e-06
 VMEM_LIMIT = 48 * 1024 * 1024
+PACK_LIMIT = 60 * 1024 * 1024
 COST = pl.CostEstimate(flops=1, bytes_accessed=1, transcendentals=0)
 
 
@@ -62,7 +63,7 @@
 def pack_pages(dest, pages, cache_keys, cache_values, peers):
     _, page_len, width = cache_keys.shape
     smem = pl.BlockSpec(memory_space=pltpu.SMEM)
-    hbm = pl.BlockSpec(memory_space=pl.ANY)
+    hbm = pl.BlockSpec(memory_space=pltpu.HBM)
     return pl.pallas_call(
         pack_kernel,
         out_shape=jax.ShapeDtypeStruct((peers * CAP, 2, page_len, width), cache_keys.dtype),
@@ -73,7 +74,7 @@
             pltpu.SMEM((peers,), jnp.int32),
             pltpu.SemaphoreType.DMA((peers * CAP * 2,)),
         ],
-        compiler_params=pltpu.CompilerParams(vmem_limit_bytes=VMEM_LIMIT),
+        compiler_params=pltpu.CompilerParams(vmem_limit_bytes=PACK_LIMIT),
         cost_estimate=COST,
         name="pack_pages",
     )(dest, pages, cache_keys, cache_values)
@@ -93,7 +94,7 @@
 
 def resident_pages(table, cache_keys, cache_values):
     pages = table.shape[0]
-    hbm = pl.BlockSpec(memory_space=pl.ANY)
+    hbm = pl.BlockSpec(memory_space=pltpu.HBM)
     vmem = pl.BlockSpec(memory_space=pltpu.VMEM)
     shape = jax.ShapeDtypeStruct((pages,) + cache_keys.shape[1:], cache_keys.dtype)
     return pl.pallas_call(
@@ -102,7 +103,7 @@
         in_specs=[pl.BlockSpec(memory_space=pltpu.SMEM), hbm, hbm],
         out_specs=[vmem, vmem],
         scratch_shapes=[pltpu.SemaphoreType.DMA((pages * 2,))],
-        compiler_params=pltpu.CompilerParams(vmem_limit_bytes=VMEM_LIMIT),
+        compiler_params=pltpu.CompilerParams(vmem_limit_bytes=PACK_LIMIT),
         cost_estimate=COST,
         name="resident_pages",
     )(table, cache_keys, cache_values)
@@ -142,16 +143,20 @@
 
 
 def arrived_kernel(heads, usable_ref, q_ref, arrived_ref, sum_ref, stat_ref, out_ref):
-    for h in range(heads):
-        part = slice(h * HD, (h + 1) * HD)
-        scores = head_scores(q_ref[:, part], arrived_ref[:, 0, :, part].reshape(-1, HD))
-        scores = jnp.where(usable_ref[...] > 0, scores, -jnp.inf)
-        local_max = stat_ref[0, 2 * h : 2 * h + 1]
-        row_max = jnp.maximum(local_max, jnp.max(scores, axis=0, keepdims=True))
-        mixed, denominator = weigh(scores, row_max, arrived_ref[:, 1, :, part].reshape(-1, HD))
-        carry = jnp.exp2((local_max - row_max) * FACTOR)
-        denominator = denominator + stat_ref[0, 2 * h + 1 : 2 * h + 2] * carry
-        mixed = (mixed + sum_ref[part] * carry) / denominator
+    parts = [slice(h * HD, (h + 1) * HD) for h in range(heads)]
+    usable = usable_ref[...] > 0
+    scores = [head_scores(q_ref[:, part], arrived_ref[:, 0, :, part].reshape(-1, HD)) for part in parts]
+    scores = [jnp.where(usable, s, -jnp.inf) for s in scores]
+    local_max = [stat_ref[0, 2 * h : 2 * h + 1] for h in range(heads)]
+    row_max = [jnp.maximum(m, jnp.max(s, axis=0, keepdims=True)) for m, s in zip(local_max, scores)]
+    carry = [jnp.exp2((m - r) * FACTOR) for m, r in zip(local_max, row_max)]
+    weighed = [
+        weigh(s, r, arrived_ref[:, 1, :, part].reshape(-1, HD)) for s, r, part in zip(scores, row_max, parts)
+    ]
+    for h, part in enumerate(parts):
+        mixed, denominator = weighed[h]
+        denominator = denominator + stat_ref[0, 2 * h + 1 : 2 * h + 2] * carry[h]
+        mixed = (mixed + sum_ref[part] * carry[h]) / denominator
         out_ref[:, part] = jnp.transpose(mixed).astype(jnp.bfloat16)
 
 
@@ -286,7 +291,7 @@
     return block, [lax.slice_in_dim(block, e - p * unit, e, axis=1) for e, p in zip(ends, PIECES)]
 
 
-def planes_projection(block, pieces, late_0, arrived, attended):
+def planes_projection(block, block_other, pieces, late_0, arrived, attended):
     half = block.shape[0]
     tokens = attended.shape[0]
     me, x = lax.axis_index("req"), lax.axis_index("tp")
@@ -299,11 +304,11 @@
     rows_mine = jnp.where(core == 0, rows[:, :half], rows[:, half:])
     rows_other = jnp.where(core == 0, rows[:, half:], rows[:, :half])
 
-    def product(w):
-        w_other = swap(w, CORE)
+    def product(w, w_other=None):
+        w_other = swap(w, CORE) if w_other is None else w_other
         return (partial_product(rows_mine, w) + partial_product(rows_other, w_other)).astype(jnp.bfloat16)
 
-    early = product(block), product(block_y)
+    early = product(block, block_other), product(block_y)
     own_parts, near_parts = [], []
     first = 0
     for j, piece in enumerate(pieces):
@@ -315,6 +320,8 @@
             arrival = swap(after(piece, arrival), Z2)
             arrival = late = after(arrival, first_sent)
         late_part = product(jnp.concatenate([late, swap(late, Y)], axis=1))
+        if j == 2:
+            late_part = after(late_part, sent)
         early_part = jnp.concatenate([e[:, first : first + size] for e in early], axis=1)
         first += size
         kept = jnp.where(own_early, early_part, late_part)
@@ -386,10 +393,11 @@
     cross_out = cross_attention(cross_queries, text_keys, text_values)
     sums = after(sums, cross_out)
     if planes:
-        late_0 = swap(after(pieces[0], sums), Z2)
+        block_other = swap(after(block, sums), CORE)
+        late_0 = swap(after(pieces[0], block_other), Z2)
     attended = arrived_attention(arrived_usable, query_normed, arrived, sums, stats)
     if planes:
-        projected = planes_projection(block, pieces, late_0, arrived, attended)
+        projected = planes_projection(block, block_other, pieces, late_0, arrived, attended)
     else:
         projected = projection_gathered(attended, out_weight)
 

time: 219 us -> 215 us (0.982)
  matrix products: 18.7 us -> 14.6 us
  waiting for transfers between devices: 95.3 us -> 98 us
  other arithmetic: 14.3 us -> 12 us
    all_to_all x1, waiting for transfers between devices: 25.6 us -> 18.9 us  [shards(): lax.all_to_all(packed, 'req', split_axis=0, concat_axis=0, tiled=True)]
    ppermute x3, waiting for transfers between devices: 8.12 us -> 13.4 us  [planes_projection(): received = lax.ppermute(sent, 'tp', [(0, 1), (1, 0)])]
    dot_general x10, matrix products: 18.7 us -> 14.6 us  [partial_product(): return jnp.dot(rows, weights, preferred_element_type=jnp.float32)]
    ppermute x17, waiting for transfers between devices: 59.6 us -> 63.7 us  [swap(): return lax.ppermute(x, 'req', [(i, i ^ bits) for i in range(size)])]
    pallas_call x1, Pallas kernels: 8 us -> 5.49 us  [arrived_attention(): pl.pallas_call(functools.partial(arrived_kernel, block // HD), out_shape=...]
    unnamed x60 -> x46, local copies, waits for them, and re-layouts: 7.64 us -> 9.32 us
  transfers between devices with their start and end apart: 23 -> 23, of which waited for: 14 -> 16; matrix products, arithmetic and copies ran while one was open for 19% -> 15% of each run, Pallas kernels for 12% -> 12%
where the time goes in v3:
time: 215 us; the launch traced here: 214 us
  waiting for transfers between devices  98 us (46%)
  starting transfers between devices  39.1 us (18%)
  Pallas kernels  30.9 us (14%)
  local copies, waits for them, and re-layouts  17.5 us (8%)
  matrix products  14.6 us (7%)
  other arithmetic  12 us (6%)
    ppermute x17, waiting for transfers between devices, swap(): return lax.ppermute(x, 'req', [(i, i ^ bits) for i in range(size)])  63.7 us
    ppermute x17, starting transfers between devices, swap(): return lax.ppermute(x, 'req', [(i, i ^ bits) for i in range(size)])  24.8 us
    all_to_all x1, waiting for transfers between devices, shards(): lax.all_to_all(packed, 'req', split_axis=0, concat_axis=0, tiled=True)  18.9 us
    dot_general x10, matrix products, partial_product(): return jnp.dot(rows, weights, preferred_element_type=jnp.float32)  14.6 us
    ppermute x3, waiting for transfers between devices, planes_projection(): received = lax.ppermute(sent, 'tp', [(0, 1), (1, 0)])  13.4 us
    pallas_call x1, Pallas kernels, local_attention(): pl.pallas_call(functools.partial(local_kernel, group), out_shape=[jax.Sha...  11.1 us
    unnamed x46, local copies, waits for them, and re-layouts  9.32 us
    all_to_all x1, starting transfers between devices, shards(): lax.all_to_all(packed, 'req', split_axis=0, concat_axis=0, tiled=True)  7.56 us
  transfers between devices with their start and end apart: 23, of which 16 were waited for; matrix products, arithmetic and copies ran while one was open for 15% of the time, Pallas kernels for 12%

profile of v3, /device:TPU:0, one launch (start us, length us, event | category | flops | bytes accessed | tf_op | source)
XLA Modules:
  0.0 214.0 jit_solution(9579167430356794526)
XLA Ops:
  2.0 4.5 %pack_pages.1 = bf16[32,2,8,2560]{3,2,1,0:T(8,128)(2,1)} custom-call(s32[16,1]{1,0:T(8,128)} %copy.27.dest_ref, s32[1,16]{1,0:T(1,128)} %page_ref.1, bf16[64,8,2560]{2,1,0:T(8,128)(2,1)} %keys_ref.3, bf16[64,8,2560]{2,1,0:T(8,128)(2,1)} %values_ref.3), custom_call_target="tpu_custom_call" | custom-call | flops 1 | bytes 1 | tf_op jit(solution)/shard_map/pack_pages/pallas_call | solution.py:67
  6.4 7.6 %all-to-all-start = ((bf16[32,2,8,2560]{3,2,1,0:T(8,128)(2,1)}), bf16[32,2,8,2560]{3,2,1,0:T(8,128)(2,1)}, u32[]{:S(2)}, u32[]{:S(2)}) async-start(bf16[32,2,8,2560]{3,2,1,0:T(8,128)(2,1)} %pack_pages.1), calls=%async_computation | async-start | bytes 5242880 | tf_op jit(solution)/shard_map/all_to_all | solution.py:373
  22.3 3.2 %maximum_select_fusion.1 = bf16[1280,640]{0,1:T(8,128)(2,1)} fusion(bf16[1280,320]{0,1:T(8,128)(2,1)} %collective-permute-done.1, bf16[1280,320]{0,1:T(8,128)(2,1)S(1)} %get-tuple-element.41, pred[]{:T(512)S(6)} %eq.23), kind=kLoop, calls=%fused_computation.17 | loop fusion | flops 7372800 | bytes 3276801 | tf_op jit(solution)/shard_map/jit(_where)/select_n | solution.py:288
  29.6 5.7 %resident_pages.1 = (bf16[48,8,2560]{2,1,0:T(8,128)(2,1)}, bf16[48,8,2560]{2,1,0:T(8,128)(2,1)}) custom-call(s32[48]{0:T(128)} %bitcast.39, bf16[64,8,2560]{2,1,0:T(8,128)(2,1)} %keys_ref.3, bf16[64,8,2560]{2,1,0:T(8,128)(2,1)} %values_ref.3), custom_call_target="tpu_custom_call" | custom-call | flops 1 | bytes 1 | tf_op jit(solution)/shard_map/resident_pages/pallas_call | solution.py:100
  37.8 4.1 %cross_attention.1 = bf16[256,2560]{1,0:T(8,128)(2,1)} custom-call(bf16[256,2560]{1,0:T(8,128)(2,1)S(1)} %copy-done.1, bf16[128,2560]{1,0:T(8,128)(2,1)S(1)} %copy-done.3, bf16[128,2560]{1,0:T(8,128)(2,1)S(1)} %copy-done.4), custom_call_target="tpu_custom_call" | custom-call | flops 1 | bytes 1 | tf_op jit(solution)/shard_map/cross_attention/pallas_call | solution.py:232
  41.9 11.1 %local_attention.1 = (f32[2560,256]{1,0:T(8,128)}, f32[4,16,256]{2,1,0:T(8,128)S(1)}) custom-call(s32[1]{0:T(128)S(6)} %copy.59.length_ref, bf16[256,2560]{1,0:T(8,128)(2,1)S(1)} %fusion.2.q_ref, bf16[48,8,2560]{2,1,0:T(8,128)(2,1)S(1)} %copy-done, bf16[48,8,2560]{2,1,0:T(8,128)(2,1)} %get-tuple-element.21.rv_ref, bf16[256,2560]{1,0:T(8,128)(2,1)S(1)} %fusion.5.k_ref, ...), custom_call_target="tpu_custom_call" | custom-call | flops 1 | bytes 1 | tf_op jit(solution)/shard_map/local_attention/pallas_call | solution.py:185
  56.8 2.8 %collective-permute-start.6 = (bf16[1280,256]{0,1:T(8,128)(2,1)}, bf16[1280,256]{0,1:T(8,128)(2,1)}, u32[]{:S(2)}, u32[]{:S(2)}) collective-permute-start(bf16[1280,256]{0,1:T(8,128)(2,1)} %get-tuple-element.28), channel_id=1, source_target_pairs={{0,16},{2,18},{4,20},{6,22},{8,24},{10,26},{12,28},{14,30},{16,0},... | collective-permute-start | bytes 1966088 | tf_op jit(solution)/shard_map/ppermute | solution.py:256
  59.6 18.9 %all-to-all-done.arrived_ref = bf16[32,2,8,2560]{3,2,1,0:T(8,128)(2,1)} async-done(((bf16[32,2,8,2560]{3,2,1,0:T(8,128)(2,1)}), bf16[32,2,8,2560]{3,2,1,0:T(8,128)(2,1)}, u32[]{:S(2)}, u32[]{:S(2)}) %all-to-all-start) | async-done | bytes 2621472 | tf_op jit(solution)/shard_map/all_to_all | solution.py:373
  79.9 5.5 %arrived_attention.1 = bf16[256,2560]{1,0:T(8,128)(2,1)S(1)} custom-call(f32[256,256]{1,0:T(8,128)S(1)} %broadcast_in_dim.8.usable_ref, bf16[256,2560]{1,0:T(8,128)(2,1)S(1)} %fusion.2.q_ref, bf16[32,2,8,2560]{3,2,1,0:T(8,128)(2,1)} %all-to-all-done.arrived_ref, f32[2560,256]{1,0:T(8,128)} %get-tuple-element.24.sum_ref, ...), custom_call_target="tpu_custom_call" | custom-call | flops 1 | bytes 1 | tf_op jit(solution)/shard_map/arrived_attention/pallas_call | solution.py:208
  85.4 9.2 %collective-permute-start.2 = (bf16[256,2560]{1,0:T(8,128)(2,1)S(1)}, bf16[256,2560]{1,0:T(8,128)(2,1)S(1)}, u32[]{:S(2)}, u32[]{:S(2)}) collective-permute-start(bf16[256,2560]{1,0:T(8,128)(2,1)S(1)} %arrived_attention.1), channel_id=1, source_target_pairs={{0,8},{2,10},{4,12},{6,14},{8,0},{10,2},{12,4},{14,6},{16,24},{18,... | collective-permute-start | bytes 3932168 | tf_op jit(solution)/shard_map/ppermute | solution.py:256
  94.6 8.1 %collective-permute-done.6 = bf16[1280,256]{0,1:T(8,128)(2,1)} collective-permute-done((bf16[1280,256]{0,1:T(8,128)(2,1)}, bf16[1280,256]{0,1:T(8,128)(2,1)}, u32[]{:S(2)}, u32[]{:S(2)}) %collective-permute-start.6) | collective-permute-done | bytes 655392 | tf_op jit(solution)/shard_map/ppermute | solution.py:256
  105.4 13.9 %collective-permute-done.7 = bf16[1280,256]{0,1:T(8,128)(2,1)} collective-permute-done((bf16[1280,256]{0,1:T(8,128)(2,1)}, bf16[1280,256]{0,1:T(8,128)(2,1)}, u32[]{:S(2)}, u32[]{:S(2)}) %collective-permute-start.7) | collective-permute-done | bytes 655392 | tf_op jit(solution)/shard_map/ppermute | solution.py:256
  120.4 15.6 %collective-permute-done.10 = bf16[1280,256]{0,1:T(8,128)(2,1)} collective-permute-done((bf16[1280,256]{0,1:T(8,128)(2,1)S(1)}, bf16[1280,256]{0,1:T(8,128)(2,1)}, u32[]{:S(2)}, u32[]{:S(2)}) %collective-permute-start.10) | collective-permute-done | bytes 655392 | tf_op jit(solution)/shard_map/ppermute | solution.py:256
  136.0 3.5 %collective-permute-start.14 = (bf16[1280,128]{0,1:T(8,128)(2,1)S(1)}, bf16[1280,128]{0,1:T(8,128)(2,1)S(1)}, u32[]{:S(2)}, u32[]{:S(2)}) collective-permute-start(bf16[1280,128]{0,1:T(8,128)(2,1)S(1)} %copy-done.10), channel_id=1, source_target_pairs={{0,16},{2,18},{4,20},{6,22},{8,24},{10,26},{12,28},{14,30},{16,0},... | collective-permute-start | bytes 983048 | tf_op jit(solution)/shard_map/ppermute | solution.py:256
  139.5 7.0 %collective-permute-done.2 = bf16[256,2560]{1,0:T(8,128)(2,1)S(1)} collective-permute-done((bf16[256,2560]{1,0:T(8,128)(2,1)S(1)}, bf16[256,2560]{1,0:T(8,128)(2,1)S(1)}, u32[]{:S(2)}, u32[]{:S(2)}) %collective-permute-start.2) | collective-permute-done | bytes 1310752 | tf_op jit(solution)/shard_map/ppermute | solution.py:256
  147.3 2.6 %fusion.22 = f32[512,640]{1,0:T(8,128)S(1)} fusion(bf16[512,1280]{1,0:T(8,128)(2,1)S(1)} %get-tuple-element.38, bf16[1280,640]{0,1:T(8,128)(2,1)} %collective-permute-done.3), kind=kOutput, calls=%fused_computation.96 | convolution fusion | flops 838860800 | bytes 4259840 | tf_op jit(solution)/shard_map/dot_general | solution.py:260
  150.0 2.7 %fusion.8 = bf16[512,640]{1,0:T(8,128)(2,1)S(1)} fusion(f32[512,640]{1,0:T(8,128)S(1)} %fusion.22, bf16[512,1280]{1,0:T(8,128)(2,1)S(1)} %get-tuple-element.37, bf16[1280,640]{0,1:T(8,128)(2,1)} %maximum_select_fusion.1), kind=kOutput, calls=%fused_computation.22 | convolution fusion | flops 839516160 | bytes 4915200 | tf_op jit(solution)/shard_map/dot_general | solution.py:260
  155.1 2.7 %fusion.9 = bf16[512,640]{1,0:T(8,128)(2,1)S(1)} fusion(f32[512,640]{1,0:T(8,128)S(1)} %fusion.23, bf16[512,1280]{1,0:T(8,128)(2,1)S(1)} %get-tuple-element.37, bf16[1280,640]{0,1:T(8,128)(2,1)} %collective-permute-done.4), kind=kOutput, calls=%fused_computation.23 | convolution fusion | flops 839516160 | bytes 4915200 | tf_op jit(solution)/shard_map/dot_general | solution.py:260
  165.0 6.2 %collective-permute-done.15 = bf16[1280,128]{0,1:T(8,128)(2,1)S(1)} collective-permute-done((bf16[1280,128]{0,1:T(8,128)(2,1)S(1)}, bf16[1280,128]{0,1:T(8,128)(2,1)S(1)}, u32[]{:S(2)}, u32[]{:S(2)}) %collective-permute-start.15) | collective-permute-done | bytes 327712 | tf_op jit(solution)/shard_map/ppermute | solution.py:256
  181.2 6.5 %collective-permute-done.17 = bf16[512,256]{1,0:T(8,128)(2,1)S(1)} collective-permute-done((bf16[512,256]{1,0:T(8,128)(2,1)}, bf16[512,256]{1,0:T(8,128)(2,1)S(1)}, u32[]{:S(2)}, u32[]{:S(2)}) %collective-permute-start.17) | collective-permute-done | bytes 262176 | tf_op jit(solution)/shard_map/ppermute | solution.py:331
  189.9 2.9 %collective-permute-done.20 = bf16[256,256]{1,0:T(8,128)(2,1)S(1)} collective-permute-done((bf16[256,256]{1,0:T(8,128)(2,1)S(1)}, bf16[256,256]{1,0:T(8,128)(2,1)S(1)}, u32[]{:S(2)}, u32[]{:S(2)}) %collective-permute-start.20) | collective-permute-done | bytes 131104 | tf_op jit(solution)/shard_map/ppermute | solution.py:256
  192.9 4.8 %collective-permute-done.13 = bf16[512,512]{1,0:T(8,128)(2,1)S(1)} collective-permute-done((bf16[512,512]{1,0:T(8,128)(2,1)}, bf16[512,512]{1,0:T(8,128)(2,1)S(1)}, u32[]{:S(2)}, u32[]{:S(2)}) %collective-permute-start.13) | collective-permute-done | bytes 524320 | tf_op jit(solution)/shard_map/ppermute | solution.py:331
  199.3 5.7 %collective-permute-done.19 = bf16[256,512]{1,0:T(8,128)(2,1)S(1)} collective-permute-done((bf16[256,512]{1,0:T(8,128)(2,1)S(1)}, bf16[256,512]{1,0:T(8,128)(2,1)S(1)}, u32[]{:S(2)}, u32[]{:S(2)}) %collective-permute-start.19) | collective-permute-done | bytes 262176 | tf_op jit(solution)/shard_map/ppermute | solution.py:256
  211.5 2.6 %add_convert_fusion = (bf16[256,2560]{1,0:T(8,128)(2,1)}, bf16[256,2560]{1,0:T(8,128)(2,1)}) fusion(f32[2560]{0:T(1024)S(1)} %get-tuple-element.83, f32[2560]{0:T(1024)S(1)} %add_reduce_fusion, f32[256]{0:T(256)S(1)} %get-tuple-element.72, f32[256]{0:T(256)S(1)} %get-tuple-element.71, f32[256,1280]{1,0:T(8,128)S(1)} %get-tuple-element.82, ...), kind=kLoop, calls=%fused_computation.15 | loop fusion | flops 7864320 | bytes 6586369 | tf_op jit(solution)/shard_map/convert_element_type | solution.py:420
  (128 shorter events, 55.1 us)
Async XLA Ops:
  6.4 72.0 %all-to-all-start = ((bf16[32,2,8,2560]{3,2,1,0:T(8,128)(2,1)}), bf16[32,2,8,2560]{3,2,1,0:T(8,128)(2,1)}, u32[]{:S(2)}, u32[]{:S(2)}) async-start(bf16[32,2,8,2560]{3,2,1,0:T(8,128)(2,1)} %pack_pages.1), calls=%async_computation | async-start | bytes 5242880 | tf_op jit(solution)/shard_map/all_to_all | solution.py:373
  15.7 4.7 %collective-permute-start = (f32[2,256]{1,0:T(2,128)S(1)}, f32[2,256]{1,0:T(2,128)S(1)}, u32[]{:S(2)}, u32[]{:S(2)}) collective-permute-start(f32[2,256]{1,0:T(2,128)S(1)} %pad_maximum_fusion.4), channel_id=1, source_target_pairs={{0,1},{1,0},{2,3},{3,2},{4,5},{5,4},{6,7},{7,6},{8,9},{9,8},{10,11... | collective-permute-start | bytes 6152 | tf_op jit(solution)/shard_map/ppermute | solution.py:246
  19.7 2.7 %collective-permute-start.1 = (bf16[1280,320]{0,1:T(8,128)(2,1)}, bf16[1280,320]{0,1:T(8,128)(2,1)}, u32[]{:S(2)}, u32[]{:S(2)}) collective-permute-start(bf16[1280,320]{0,1:T(8,128)(2,1)} %get-tuple-element.42), channel_id=1, source_target_pairs={{0,2},{2,0},{4,6},{6,4},{8,10},{10,8},{12,14},{14,12},{16,18},{18,... | collective-permute-start | bytes 2457608 | tf_op jit(solution)/shard_map/ppermute | solution.py:256
  53.0 3.8 %collective-permute-start.3 = (bf16[1280,640]{0,1:T(8,128)(2,1)}, bf16[1280,640]{0,1:T(8,128)(2,1)}, u32[]{:S(2)}, u32[]{:S(2)}) collective-permute-start(bf16[1280,640]{0,1:T(8,128)(2,1)} %maximum_select_fusion.1), channel_id=1, source_target_pairs={{0,2},{2,0},{4,6},{6,4},{8,10},{10,8},{12,14},{14,12},{16,18},{18,... | collective-permute-start | bytes 4915208 | tf_op jit(solution)/shard_map/ppermute | solution.py:256
  53.2 50.9 %collective-permute-start.4 = (bf16[1280,640]{0,1:T(8,128)(2,1)}, bf16[1280,640]{0,1:T(8,128)(2,1)}, u32[]{:S(2)}, u32[]{:S(2)}) collective-permute-start(bf16[1280,640]{0,1:T(8,128)(2,1)} %maximum_select_fusion.1), channel_id=1, source_target_pairs={{0,4},{2,6},{4,0},{6,2},{8,12},{10,14},{12,8},{14,10},{16,20},{18,... | collective-permute-start | bytes 4915208 | tf_op jit(solution)/shard_map/ppermute | solution.py:256
  56.8 45.9 %collective-permute-start.6 = (bf16[1280,256]{0,1:T(8,128)(2,1)}, bf16[1280,256]{0,1:T(8,128)(2,1)}, u32[]{:S(2)}, u32[]{:S(2)}) collective-permute-start(bf16[1280,256]{0,1:T(8,128)(2,1)} %get-tuple-element.28), channel_id=1, source_target_pairs={{0,16},{2,18},{4,20},{6,22},{8,24},{10,26},{12,28},{14,30},{16,0},... | collective-permute-start | bytes 1966088 | tf_op jit(solution)/shard_map/ppermute | solution.py:256
  85.4 61.1 %collective-permute-start.2 = (bf16[256,2560]{1,0:T(8,128)(2,1)S(1)}, bf16[256,2560]{1,0:T(8,128)(2,1)S(1)}, u32[]{:S(2)}, u32[]{:S(2)}) collective-permute-start(bf16[256,2560]{1,0:T(8,128)(2,1)S(1)} %arrived_attention.1), channel_id=1, source_target_pairs={{0,8},{2,10},{4,12},{6,14},{8,0},{10,2},{12,4},{14,6},{16,24},{18,... | collective-permute-start | bytes 3932168 | tf_op jit(solution)/shard_map/ppermute | solution.py:256
  102.7 16.5 %collective-permute-start.7 = (bf16[1280,256]{0,1:T(8,128)(2,1)}, bf16[1280,256]{0,1:T(8,128)(2,1)}, u32[]{:S(2)}, u32[]{:S(2)}) collective-permute-start(bf16[1280,256]{0,1:T(8,128)(2,1)} %collective-permute-done.6), channel_id=1, source_target_pairs={{0,4},{2,6},{4,0},{6,2},{8,12},{10,14},{12,8},{14,10},{16,20},{18,... | collective-permute-start | bytes 1966088 | tf_op jit(solution)/shard_map/ppermute | solution.py:256
  104.1 31.9 %collective-permute-start.10 = (bf16[1280,256]{0,1:T(8,128)(2,1)S(1)}, bf16[1280,256]{0,1:T(8,128)(2,1)}, u32[]{:S(2)}, u32[]{:S(2)}) collective-permute-start(bf16[1280,256]{0,1:T(8,128)(2,1)S(1)} %copy-done.9), channel_id=1, source_target_pairs={{0,16},{2,18},{4,20},{6,22},{8,24},{10,26},{12,28},{14,30},{16,0},... | collective-permute-start | bytes 1966088 | tf_op jit(solution)/shard_map/ppermute | solution.py:256
  104.1 31.9 %copy-start.10 = (bf16[1280,128]{0,1:T(8,128)(2,1)S(1)}, bf16[1280,128]{0,1:T(8,128)(2,1)}, u32[]{:S(2)}) copy-start(bf16[1280,128]{0,1:T(8,128)(2,1)} %slice.143) | copy-start | bytes 983044
  104.1 49.7 %collective-permute-start.5 = (bf16[1280,640]{0,1:T(8,128)(2,1)}, bf16[1280,640]{0,1:T(8,128)(2,1)S(1)}, u32[]{:S(2)}, u32[]{:S(2)}) collective-permute-start(bf16[1280,640]{0,1:T(8,128)(2,1)} %collective-permute-done.4), channel_id=1, source_target_pairs={{0,2},{2,0},{4,6},{6,4},{8,10},{10,8},{12,14},{14,12},{16,18},{18,... | collective-permute-start | bytes 4915208 | tf_op jit(solution)/shard_map/ppermute | solution.py:256
  120.4 37.4 %collective-permute-start.8 = (bf16[1280,512]{0,1:T(8,128)(2,1)S(1)}, bf16[1280,512]{0,1:T(8,128)(2,1)S(1)}, u32[]{:S(2)}, u32[]{:S(2)}) collective-permute-start(bf16[1280,512]{0,1:T(8,128)(2,1)S(1)} %constant_dynamic-update-slice_fusion), channel_id=1, source_target_pairs={{0,2},{2,0},{4,6},{6,4},{8,10},{10,8},{12,14},{14,12},{16,18},{18,... | collective-permute-start | bytes 3932168 | tf_op jit(solution)/shard_map/ppermute | solution.py:256
  136.0 25.1 %collective-permute-start.14 = (bf16[1280,128]{0,1:T(8,128)(2,1)S(1)}, bf16[1280,128]{0,1:T(8,128)(2,1)S(1)}, u32[]{:S(2)}, u32[]{:S(2)}) collective-permute-start(bf16[1280,128]{0,1:T(8,128)(2,1)S(1)} %copy-done.10), channel_id=1, source_target_pairs={{0,16},{2,18},{4,20},{6,22},{8,24},{10,26},{12,28},{14,30},{16,0},... | collective-permute-start | bytes 983048 | tf_op jit(solution)/shard_map/ppermute | solution.py:256
  147.3 17.6 %collective-permute-start.11 = (bf16[1280,256]{0,1:T(8,128)(2,1)}, bf16[1280,256]{0,1:T(8,128)(2,1)S(1)}, u32[]{:S(2)}, u32[]{:S(2)}) collective-permute-start(bf16[1280,256]{0,1:T(8,128)(2,1)} %collective-permute-done.10), channel_id=1, source_target_pairs={{0,4},{2,6},{4,0},{6,2},{8,12},{10,14},{12,8},{14,10},{16,20},{18,... | collective-permute-start | bytes 1966088 | tf_op jit(solution)/shard_map/ppermute | solution.py:256
  159.6 13.9 %collective-permute-start.9 = (bf16[512,512]{1,0:T(8,128)(2,1)S(1)}, bf16[512,512]{1,0:T(8,128)(2,1)S(1)}, u32[]{:S(2)}, u32[]{:S(2)}) collective-permute-start(bf16[512,512]{1,0:T(8,128)(2,1)S(1)} %get-tuple-element.77), channel_id=1, source_target_pairs={{0,1},{1,0},{2,3},{3,2},{4,5},{5,4},{6,7},{7,6},{8,9},{9,8},{10,11... | collective-permute-start | bytes 1572872 | tf_op jit(solution)/shard_map/ppermute | solution.py:331
  161.1 10.1 %collective-permute-start.15 = (bf16[1280,128]{0,1:T(8,128)(2,1)S(1)}, bf16[1280,128]{0,1:T(8,128)(2,1)S(1)}, u32[]{:S(2)}, u32[]{:S(2)}) collective-permute-start(bf16[1280,128]{0,1:T(8,128)(2,1)S(1)} %collective-permute-done.14), channel_id=1, source_target_pairs={{0,4},{2,6},{4,0},{6,2},{8,12},{10,14},{12,8},{14,10},{16,20},{18,... | collective-permute-start | bytes 983048 | tf_op jit(solution)/shard_map/ppermute | solution.py:256
  164.9 10.0 %collective-permute-start.12 = (bf16[1280,512]{0,1:T(8,128)(2,1)S(1)}, bf16[1280,512]{0,1:T(8,128)(2,1)S(1)}, u32[]{:S(2)}, u32[]{:S(2)}) collective-permute-start(bf16[1280,512]{0,1:T(8,128)(2,1)S(1)} %constant_dynamic-update-slice_fusion.2), channel_id=1, source_target_pairs={{0,2},{2,0},{4,6},{6,4},{8,10},{10,8},{12,14},{14,12},{16,18},{18,... | collective-permute-start | bytes 3932168 | tf_op jit(solution)/shard_map/ppermute | solution.py:256
  171.2 2.5 %collective-permute-start.16 = (bf16[1280,256]{0,1:T(8,128)(2,1)S(1)}, bf16[1280,256]{0,1:T(8,128)(2,1)S(1)}, u32[]{:S(2)}, u32[]{:S(2)}) collective-permute-start(bf16[1280,256]{0,1:T(8,128)(2,1)S(1)} %constant_dynamic-update-slice_fusion.4), channel_id=1, source_target_pairs={{0,2},{2,0},{4,6},{6,4},{8,10},{10,8},{12,14},{14,12},{16,18},{18,... | collective-permute-start | bytes 1966088 | tf_op jit(solution)/shard_map/ppermute | solution.py:256
  173.7 7.4 %collective-permute-start.18 = (bf16[256,512]{1,0:T(8,128)(2,1)S(1)}, bf16[256,512]{1,0:T(8,128)(2,1)S(1)}, u32[]{:S(2)}, u32[]{:S(2)}) collective-permute-start(bf16[256,512]{1,0:T(8,128)(2,1)S(1)} %slice.213), channel_id=1, source_target_pairs={{0,8},{2,10},{4,12},{6,14},{8,0},{10,2},{12,4},{14,6},{16,24},{18,... | collective-permute-start | bytes 786440 | tf_op jit(solution)/shard_map/ppermute | solution.py:256
  178.2 9.4 %collective-permute-start.17 = (bf16[512,256]{1,0:T(8,128)(2,1)}, bf16[512,256]{1,0:T(8,128)(2,1)S(1)}, u32[]{:S(2)}, u32[]{:S(2)}) collective-permute-start(bf16[512,256]{1,0:T(8,128)(2,1)} %broadcast_select_fusion.6), channel_id=1, source_target_pairs={{0,1},{1,0},{2,3},{3,2},{4,5},{5,4},{6,7},{7,6},{8,9},{9,8},{10,11... | collective-permute-start | bytes 786440 | tf_op jit(solution)/shard_map/ppermute | solution.py:331
  179.8 17.8 %collective-permute-start.13 = (bf16[512,512]{1,0:T(8,128)(2,1)}, bf16[512,512]{1,0:T(8,128)(2,1)S(1)}, u32[]{:S(2)}, u32[]{:S(2)}) collective-permute-start(bf16[512,512]{1,0:T(8,128)(2,1)} %get-tuple-element.79), channel_id=1, source_target_pairs={{0,1},{1,0},{2,3},{3,2},{4,5},{5,4},{6,7},{7,6},{8,9},{9,8},{10,11... | collective-permute-start | bytes 1572872 | tf_op jit(solution)/shard_map/ppermute | solution.py:331
  187.8 5.0 %collective-permute-start.20 = (bf16[256,256]{1,0:T(8,128)(2,1)S(1)}, bf16[256,256]{1,0:T(8,128)(2,1)S(1)}, u32[]{:S(2)}, u32[]{:S(2)}) collective-permute-start(bf16[256,256]{1,0:T(8,128)(2,1)S(1)} %slice.214), channel_id=1, source_target_pairs={{0,8},{2,10},{4,12},{6,14},{8,0},{10,2},{12,4},{14,6},{16,24},{18,... | collective-permute-start | bytes 393224 | tf_op jit(solution)/shard_map/ppermute | solution.py:256
  197.9 7.1 %collective-permute-start.19 = (bf16[256,512]{1,0:T(8,128)(2,1)S(1)}, bf16[256,512]{1,0:T(8,128)(2,1)S(1)}, u32[]{:S(2)}, u32[]{:S(2)}) collective-permute-start(bf16[256,512]{1,0:T(8,128)(2,1)S(1)} %slice.212), channel_id=1, source_target_pairs={{0,8},{2,10},{4,12},{6,14},{8,0},{10,2},{12,4},{14,6},{16,24},{18,... | collective-permute-start | bytes 786440 | tf_op jit(solution)/shard_map/ppermute | solution.py:256
  207.8 3.6 %collective-permute-start.21 = (f32[2,256]{1,0:T(2,128)S(1)}, f32[2,256]{1,0:T(2,128)S(1)}, u32[]{:S(2)}, u32[]{:S(2)}) collective-permute-start(f32[2,256]{1,0:T(2,128)S(1)} %pad_maximum_fusion.5), channel_id=1, source_target_pairs={{0,1},{1,0},{2,3},{3,2},{4,5},{5,4},{6,7},{7,6},{8,9},{9,8},{10,11... | collective-permute-start | bytes 6152 | tf_op jit(solution)/shard_map/ppermute | solution.py:409
  (15 other events, 66.9 us)

commit v4 on v3

--- a/solution.py
+++ b/solution.py
@@ -300,7 +300,8 @@
 
     block_y = after(swap(block, Y), attended)
     late = after(late_0, attended)
-    rows = jnp.concatenate([attended, swap(attended, Z1)], axis=0)
+    near = swap(attended, Z1)
+    rows = jnp.concatenate([attended, near], axis=0)
     rows_mine = jnp.where(core == 0, rows[:, :half], rows[:, half:])
     rows_other = jnp.where(core == 0, rows[:, half:], rows[:, :half])
 
@@ -315,7 +316,7 @@
         size = piece.shape[1]
         if j == 1:
             arrival = swap(after(piece, late_0, attended), Z2)
-            late = after(arrival, rows_mine)
+            late = after(arrival, near)
         if j > 1:
             arrival = swap(after(piece, arrival), Z2)
             arrival = late = after(arrival, first_sent)

time: 215 us -> 214 us (level)
  no operation moved by 1% of the time
where the time goes in v4:
time: 214 us; the launch traced here: 213 us
  waiting for transfers between devices  96.2 us (45%)
  starting transfers between devices  39.7 us (19%)
  Pallas kernels  30.9 us (14%)
  local copies, waits for them, and re-layouts  17.5 us (8%)
  matrix products  14.6 us (7%)
  other arithmetic  12 us (6%)
    ppermute x17, waiting for transfers between devices, swap(): return lax.ppermute(x, 'req', [(i, i ^ bits) for i in range(size)])  61.8 us
    ppermute x17, starting transfers between devices, swap(): return lax.ppermute(x, 'req', [(i, i ^ bits) for i in range(size)])  25.3 us
    all_to_all x1, waiting for transfers between devices, shards(): lax.all_to_all(packed, 'req', split_axis=0, concat_axis=0, tiled=True)  18.9 us
    dot_general x10, matrix products, partial_product(): return jnp.dot(rows, weights, preferred_element_type=jnp.float32)  14.6 us
    ppermute x3, waiting for transfers between devices, planes_projection(): received = lax.ppermute(sent, 'tp', [(0, 1), (1, 0)])  13.5 us
    pallas_call x1, Pallas kernels, local_attention(): pl.pallas_call(functools.partial(local_kernel, group), out_shape=[jax.Sha...  11.1 us
    unnamed x46, local copies, waits for them, and re-layouts  9.32 us
    all_to_all x1, starting transfers between devices, shards(): lax.all_to_all(packed, 'req', split_axis=0, concat_axis=0, tiled=True)  7.57 us
  transfers between devices with their start and end apart: 23, of which 16 were waited for; matrix products, arithmetic and copies ran while one was open for 15% of the time, Pallas kernels for 12%

profile of v4, /device:TPU:0, one launch (start us, length us, event | category | flops | bytes accessed | tf_op | source)
XLA Modules:
  0.0 212.7 jit_solution(7686737474366750788)
XLA Ops:
  2.0 4.5 %pack_pages.1 = bf16[32,2,8,2560]{3,2,1,0:T(8,128)(2,1)} custom-call(s32[16,1]{1,0:T(8,128)} %copy.27.dest_ref, s32[1,16]{1,0:T(1,128)} %page_ref.1, bf16[64,8,2560]{2,1,0:T(8,128)(2,1)} %keys_ref.3, bf16[64,8,2560]{2,1,0:T(8,128)(2,1)} %values_ref.3), custom_call_target="tpu_custom_call" | custom-call | flops 1 | bytes 1 | tf_op jit(solution)/shard_map/pack_pages/pallas_call | solution.py:67
  6.4 7.6 %all-to-all-start = ((bf16[32,2,8,2560]{3,2,1,0:T(8,128)(2,1)}), bf16[32,2,8,2560]{3,2,1,0:T(8,128)(2,1)}, u32[]{:S(2)}, u32[]{:S(2)}) async-start(bf16[32,2,8,2560]{3,2,1,0:T(8,128)(2,1)} %pack_pages.1), calls=%async_computation | async-start | bytes 5242880 | tf_op jit(solution)/shard_map/all_to_all | solution.py:374
  22.3 3.2 %maximum_select_fusion.1 = bf16[1280,640]{0,1:T(8,128)(2,1)} fusion(bf16[1280,320]{0,1:T(8,128)(2,1)} %collective-permute-done.1, bf16[1280,320]{0,1:T(8,128)(2,1)S(1)} %get-tuple-element.41, pred[]{:T(512)S(6)} %eq.23), kind=kLoop, calls=%fused_computation.17 | loop fusion | flops 7372800 | bytes 3276801 | tf_op jit(solution)/shard_map/jit(_where)/select_n | solution.py:288
  29.6 5.7 %resident_pages.1 = (bf16[48,8,2560]{2,1,0:T(8,128)(2,1)}, bf16[48,8,2560]{2,1,0:T(8,128)(2,1)}) custom-call(s32[48]{0:T(128)} %bitcast.39, bf16[64,8,2560]{2,1,0:T(8,128)(2,1)} %keys_ref.3, bf16[64,8,2560]{2,1,0:T(8,128)(2,1)} %values_ref.3), custom_call_target="tpu_custom_call" | custom-call | flops 1 | bytes 1 | tf_op jit(solution)/shard_map/resident_pages/pallas_call | solution.py:100
  37.8 4.1 %cross_attention.1 = bf16[256,2560]{1,0:T(8,128)(2,1)} custom-call(bf16[256,2560]{1,0:T(8,128)(2,1)S(1)} %copy-done.1, bf16[128,2560]{1,0:T(8,128)(2,1)S(1)} %copy-done.3, bf16[128,2560]{1,0:T(8,128)(2,1)S(1)} %copy-done.4), custom_call_target="tpu_custom_call" | custom-call | flops 1 | bytes 1 | tf_op jit(solution)/shard_map/cross_attention/pallas_call | solution.py:232
  41.9 11.1 %local_attention.1 = (f32[2560,256]{1,0:T(8,128)}, f32[4,16,256]{2,1,0:T(8,128)S(1)}) custom-call(s32[1]{0:T(128)S(6)} %copy.59.length_ref, bf16[256,2560]{1,0:T(8,128)(2,1)S(1)} %fusion.2.q_ref, bf16[48,8,2560]{2,1,0:T(8,128)(2,1)S(1)} %copy-done, bf16[48,8,2560]{2,1,0:T(8,128)(2,1)} %get-tuple-element.21.rv_ref, bf16[256,2560]{1,0:T(8,128)(2,1)S(1)} %fusion.5.k_ref, ...), custom_call_target="tpu_custom_call" | custom-call | flops 1 | bytes 1 | tf_op jit(solution)/shard_map/local_attention/pallas_call | solution.py:185
  56.8 2.8 %collective-permute-start.6 = (bf16[1280,256]{0,1:T(8,128)(2,1)}, bf16[1280,256]{0,1:T(8,128)(2,1)}, u32[]{:S(2)}, u32[]{:S(2)}) collective-permute-start(bf16[1280,256]{0,1:T(8,128)(2,1)} %get-tuple-element.28), channel_id=1, source_target_pairs={{0,16},{2,18},{4,20},{6,22},{8,24},{10,26},{12,28},{14,30},{16,0},... | collective-permute-start | bytes 1966088 | tf_op jit(solution)/shard_map/ppermute | solution.py:256
  59.6 18.9 %all-to-all-done.arrived_ref = bf16[32,2,8,2560]{3,2,1,0:T(8,128)(2,1)} async-done(((bf16[32,2,8,2560]{3,2,1,0:T(8,128)(2,1)}), bf16[32,2,8,2560]{3,2,1,0:T(8,128)(2,1)}, u32[]{:S(2)}, u32[]{:S(2)}) %all-to-all-start) | async-done | bytes 2621472 | tf_op jit(solution)/shard_map/all_to_all | solution.py:374
  79.9 5.5 %arrived_attention.1 = bf16[256,2560]{1,0:T(8,128)(2,1)S(1)} custom-call(f32[256,256]{1,0:T(8,128)S(1)} %broadcast_in_dim.8.usable_ref, bf16[256,2560]{1,0:T(8,128)(2,1)S(1)} %fusion.2.q_ref, bf16[32,2,8,2560]{3,2,1,0:T(8,128)(2,1)} %all-to-all-done.arrived_ref, f32[2560,256]{1,0:T(8,128)} %get-tuple-element.24.sum_ref, ...), custom_call_target="tpu_custom_call" | custom-call | flops 1 | bytes 1 | tf_op jit(solution)/shard_map/arrived_attention/pallas_call | solution.py:208
  85.4 9.2 %collective-permute-start.2 = (bf16[256,2560]{1,0:T(8,128)(2,1)S(1)}, bf16[256,2560]{1,0:T(8,128)(2,1)S(1)}, u32[]{:S(2)}, u32[]{:S(2)}) collective-permute-start(bf16[256,2560]{1,0:T(8,128)(2,1)S(1)} %arrived_attention.1), channel_id=1, source_target_pairs={{0,8},{2,10},{4,12},{6,14},{8,0},{10,2},{12,4},{14,6},{16,24},{18,... | collective-permute-start | bytes 3932168 | tf_op jit(solution)/shard_map/ppermute | solution.py:256
  94.6 8.1 %collective-permute-done.6 = bf16[1280,256]{0,1:T(8,128)(2,1)} collective-permute-done((bf16[1280,256]{0,1:T(8,128)(2,1)}, bf16[1280,256]{0,1:T(8,128)(2,1)}, u32[]{:S(2)}, u32[]{:S(2)}) %collective-permute-start.6) | collective-permute-done | bytes 655392 | tf_op jit(solution)/shard_map/ppermute | solution.py:256
  105.4 13.9 %collective-permute-done.7 = bf16[1280,256]{0,1:T(8,128)(2,1)} collective-permute-done((bf16[1280,256]{0,1:T(8,128)(2,1)}, bf16[1280,256]{0,1:T(8,128)(2,1)}, u32[]{:S(2)}, u32[]{:S(2)}) %collective-permute-start.7) | collective-permute-done | bytes 655392 | tf_op jit(solution)/shard_map/ppermute | solution.py:256
  120.4 15.6 %collective-permute-done.10 = bf16[1280,256]{0,1:T(8,128)(2,1)} collective-permute-done((bf16[1280,256]{0,1:T(8,128)(2,1)S(1)}, bf16[1280,256]{0,1:T(8,128)(2,1)}, u32[]{:S(2)}, u32[]{:S(2)}) %collective-permute-start.10) | collective-permute-done | bytes 655392 | tf_op jit(solution)/shard_map/ppermute | solution.py:256
  136.0 3.5 %collective-permute-start.14 = (bf16[1280,128]{0,1:T(8,128)(2,1)S(1)}, bf16[1280,128]{0,1:T(8,128)(2,1)S(1)}, u32[]{:S(2)}, u32[]{:S(2)}) collective-permute-start(bf16[1280,128]{0,1:T(8,128)(2,1)S(1)} %copy-done.10), channel_id=1, source_target_pairs={{0,16},{2,18},{4,20},{6,22},{8,24},{10,26},{12,28},{14,30},{16,0},... | collective-permute-start | bytes 983048 | tf_op jit(solution)/shard_map/ppermute | solution.py:256
  139.5 7.0 %collective-permute-done.2 = bf16[256,2560]{1,0:T(8,128)(2,1)S(1)} collective-permute-done((bf16[256,2560]{1,0:T(8,128)(2,1)S(1)}, bf16[256,2560]{1,0:T(8,128)(2,1)S(1)}, u32[]{:S(2)}, u32[]{:S(2)}) %collective-permute-start.2) | collective-permute-done | bytes 1310752 | tf_op jit(solution)/shard_map/ppermute | solution.py:256
  147.3 2.6 %fusion.22 = f32[512,640]{1,0:T(8,128)S(1)} fusion(bf16[512,1280]{1,0:T(8,128)(2,1)S(1)} %get-tuple-element.38, bf16[1280,640]{0,1:T(8,128)(2,1)} %collective-permute-done.3), kind=kOutput, calls=%fused_computation.96 | convolution fusion | flops 838860800 | bytes 4259840 | tf_op jit(solution)/shard_map/dot_general | solution.py:260
  149.9 2.7 %fusion.8 = bf16[512,640]{1,0:T(8,128)(2,1)S(1)} fusion(f32[512,640]{1,0:T(8,128)S(1)} %fusion.22, bf16[512,1280]{1,0:T(8,128)(2,1)S(1)} %get-tuple-element.37, bf16[1280,640]{0,1:T(8,128)(2,1)} %maximum_select_fusion.1), kind=kOutput, calls=%fused_computation.22 | convolution fusion | flops 839516160 | bytes 4915200 | tf_op jit(solution)/shard_map/dot_general | solution.py:260
  155.0 2.7 %fusion.9 = bf16[512,640]{1,0:T(8,128)(2,1)S(1)} fusion(f32[512,640]{1,0:T(8,128)S(1)} %fusion.23, bf16[512,1280]{1,0:T(8,128)(2,1)S(1)} %get-tuple-element.37, bf16[1280,640]{0,1:T(8,128)(2,1)} %collective-permute-done.4), kind=kOutput, calls=%fused_computation.23 | convolution fusion | flops 839516160 | bytes 4915200 | tf_op jit(solution)/shard_map/dot_general | solution.py:260
  163.5 6.9 %collective-permute-done.15 = bf16[1280,128]{0,1:T(8,128)(2,1)S(1)} collective-permute-done((bf16[1280,128]{0,1:T(8,128)(2,1)S(1)}, bf16[1280,128]{0,1:T(8,128)(2,1)S(1)}, u32[]{:S(2)}, u32[]{:S(2)}) %collective-permute-start.15) | collective-permute-done | bytes 327712 | tf_op jit(solution)/shard_map/ppermute | solution.py:256
  170.6 2.8 %collective-permute-done.9 = bf16[512,512]{1,0:T(8,128)(2,1)S(1)} collective-permute-done((bf16[512,512]{1,0:T(8,128)(2,1)S(1)}, bf16[512,512]{1,0:T(8,128)(2,1)S(1)}, u32[]{:S(2)}, u32[]{:S(2)}) %collective-permute-start.9) | collective-permute-done | bytes 524320 | tf_op jit(solution)/shard_map/ppermute | solution.py:332
  181.1 6.5 %collective-permute-done.17 = bf16[512,256]{1,0:T(8,128)(2,1)S(1)} collective-permute-done((bf16[512,256]{1,0:T(8,128)(2,1)}, bf16[512,256]{1,0:T(8,128)(2,1)S(1)}, u32[]{:S(2)}, u32[]{:S(2)}) %collective-permute-start.17) | collective-permute-done | bytes 262176 | tf_op jit(solution)/shard_map/ppermute | solution.py:332
  189.8 2.9 %collective-permute-done.20 = bf16[256,256]{1,0:T(8,128)(2,1)S(1)} collective-permute-done((bf16[256,256]{1,0:T(8,128)(2,1)S(1)}, bf16[256,256]{1,0:T(8,128)(2,1)S(1)}, u32[]{:S(2)}, u32[]{:S(2)}) %collective-permute-start.20) | collective-permute-done | bytes 131104 | tf_op jit(solution)/shard_map/ppermute | solution.py:256
  192.8 4.2 %collective-permute-done.13 = bf16[512,512]{1,0:T(8,128)(2,1)S(1)} collective-permute-done((bf16[512,512]{1,0:T(8,128)(2,1)}, bf16[512,512]{1,0:T(8,128)(2,1)S(1)}, u32[]{:S(2)}, u32[]{:S(2)}) %collective-permute-start.13) | collective-permute-done | bytes 524320 | tf_op jit(solution)/shard_map/ppermute | solution.py:332
  199.2 4.5 %collective-permute-done.19 = bf16[256,512]{1,0:T(8,128)(2,1)S(1)} collective-permute-done((bf16[256,512]{1,0:T(8,128)(2,1)S(1)}, bf16[256,512]{1,0:T(8,128)(2,1)S(1)}, u32[]{:S(2)}, u32[]{:S(2)}) %collective-permute-start.19) | collective-permute-done | bytes 262176 | tf_op jit(solution)/shard_map/ppermute | solution.py:256
  (128 shorter events, 54.5 us)
Async XLA Ops:
  6.4 72.0 %all-to-all-start = ((bf16[32,2,8,2560]{3,2,1,0:T(8,128)(2,1)}), bf16[32,2,8,2560]{3,2,1,0:T(8,128)(2,1)}, u32[]{:S(2)}, u32[]{:S(2)}) async-start(bf16[32,2,8,2560]{3,2,1,0:T(8,128)(2,1)} %pack_pages.1), calls=%async_computation | async-start | bytes 5242880 | tf_op jit(solution)/shard_map/all_to_all | solution.py:374
  15.7 4.7 %collective-permute-start = (f32[2,256]{1,0:T(2,128)S(1)}, f32[2,256]{1,0:T(2,128)S(1)}, u32[]{:S(2)}, u32[]{:S(2)}) collective-permute-start(f32[2,256]{1,0:T(2,128)S(1)} %pad_maximum_fusion.4), channel_id=1, source_target_pairs={{0,1},{1,0},{2,3},{3,2},{4,5},{5,4},{6,7},{7,6},{8,9},{9,8},{10,11... | collective-permute-start | bytes 6152 | tf_op jit(solution)/shard_map/ppermute | solution.py:246
  19.7 2.7 %collective-permute-start.1 = (bf16[1280,320]{0,1:T(8,128)(2,1)}, bf16[1280,320]{0,1:T(8,128)(2,1)}, u32[]{:S(2)}, u32[]{:S(2)}) collective-permute-start(bf16[1280,320]{0,1:T(8,128)(2,1)} %get-tuple-element.42), channel_id=1, source_target_pairs={{0,2},{2,0},{4,6},{6,4},{8,10},{10,8},{12,14},{14,12},{16,18},{18,... | collective-permute-start | bytes 2457608 | tf_op jit(solution)/shard_map/ppermute | solution.py:256
  53.0 3.8 %collective-permute-start.3 = (bf16[1280,640]{0,1:T(8,128)(2,1)}, bf16[1280,640]{0,1:T(8,128)(2,1)}, u32[]{:S(2)}, u32[]{:S(2)}) collective-permute-start(bf16[1280,640]{0,1:T(8,128)(2,1)} %maximum_select_fusion.1), channel_id=1, source_target_pairs={{0,2},{2,0},{4,6},{6,4},{8,10},{10,8},{12,14},{14,12},{16,18},{18,... | collective-permute-start | bytes 4915208 | tf_op jit(solution)/shard_map/ppermute | solution.py:256
  53.2 50.9 %collective-permute-start.4 = (bf16[1280,640]{0,1:T(8,128)(2,1)}, bf16[1280,640]{0,1:T(8,128)(2,1)}, u32[]{:S(2)}, u32[]{:S(2)}) collective-permute-start(bf16[1280,640]{0,1:T(8,128)(2,1)} %maximum_select_fusion.1), channel_id=1, source_target_pairs={{0,4},{2,6},{4,0},{6,2},{8,12},{10,14},{12,8},{14,10},{16,20},{18,... | collective-permute-start | bytes 4915208 | tf_op jit(solution)/shard_map/ppermute | solution.py:256
  56.8 45.9 %collective-permute-start.6 = (bf16[1280,256]{0,1:T(8,128)(2,1)}, bf16[1280,256]{0,1:T(8,128)(2,1)}, u32[]{:S(2)}, u32[]{:S(2)}) collective-permute-start(bf16[1280,256]{0,1:T(8,128)(2,1)} %get-tuple-element.28), channel_id=1, source_target_pairs={{0,16},{2,18},{4,20},{6,22},{8,24},{10,26},{12,28},{14,30},{16,0},... | collective-permute-start | bytes 1966088 | tf_op jit(solution)/shard_map/ppermute | solution.py:256
  85.4 61.1 %collective-permute-start.2 = (bf16[256,2560]{1,0:T(8,128)(2,1)S(1)}, bf16[256,2560]{1,0:T(8,128)(2,1)S(1)}, u32[]{:S(2)}, u32[]{:S(2)}) collective-permute-start(bf16[256,2560]{1,0:T(8,128)(2,1)S(1)} %arrived_attention.1), channel_id=1, source_target_pairs={{0,8},{2,10},{4,12},{6,14},{8,0},{10,2},{12,4},{14,6},{16,24},{18,... | collective-permute-start | bytes 3932168 | tf_op jit(solution)/shard_map/ppermute | solution.py:256
  102.7 16.5 %collective-permute-start.7 = (bf16[1280,256]{0,1:T(8,128)(2,1)}, bf16[1280,256]{0,1:T(8,128)(2,1)}, u32[]{:S(2)}, u32[]{:S(2)}) collective-permute-start(bf16[1280,256]{0,1:T(8,128)(2,1)} %collective-permute-done.6), channel_id=1, source_target_pairs={{0,4},{2,6},{4,0},{6,2},{8,12},{10,14},{12,8},{14,10},{16,20},{18,... | collective-permute-start | bytes 1966088 | tf_op jit(solution)/shard_map/ppermute | solution.py:256
  104.1 31.9 %collective-permute-start.10 = (bf16[1280,256]{0,1:T(8,128)(2,1)S(1)}, bf16[1280,256]{0,1:T(8,128)(2,1)}, u32[]{:S(2)}, u32[]{:S(2)}) collective-permute-start(bf16[1280,256]{0,1:T(8,128)(2,1)S(1)} %copy-done.9), channel_id=1, source_target_pairs={{0,16},{2,18},{4,20},{6,22},{8,24},{10,26},{12,28},{14,30},{16,0},... | collective-permute-start | bytes 1966088 | tf_op jit(solution)/shard_map/ppermute | solution.py:256
  104.1 31.9 %copy-start.10 = (bf16[1280,128]{0,1:T(8,128)(2,1)S(1)}, bf16[1280,128]{0,1:T(8,128)(2,1)}, u32[]{:S(2)}) copy-start(bf16[1280,128]{0,1:T(8,128)(2,1)} %slice.143) | copy-start | bytes 983044
  104.1 49.6 %collective-permute-start.5 = (bf16[1280,640]{0,1:T(8,128)(2,1)}, bf16[1280,640]{0,1:T(8,128)(2,1)S(1)}, u32[]{:S(2)}, u32[]{:S(2)}) collective-permute-start(bf16[1280,640]{0,1:T(8,128)(2,1)} %collective-permute-done.4), channel_id=1, source_target_pairs={{0,2},{2,0},{4,6},{6,4},{8,10},{10,8},{12,14},{14,12},{16,18},{18,... | collective-permute-start | bytes 4915208 | tf_op jit(solution)/shard_map/ppermute | solution.py:256
  120.4 37.4 %collective-permute-start.8 = (bf16[1280,512]{0,1:T(8,128)(2,1)S(1)}, bf16[1280,512]{0,1:T(8,128)(2,1)S(1)}, u32[]{:S(2)}, u32[]{:S(2)}) collective-permute-start(bf16[1280,512]{0,1:T(8,128)(2,1)S(1)} %constant_dynamic-update-slice_fusion), channel_id=1, source_target_pairs={{0,2},{2,0},{4,6},{6,4},{8,10},{10,8},{12,14},{14,12},{16,18},{18,... | collective-permute-start | bytes 3932168 | tf_op jit(solution)/shard_map/ppermute | solution.py:256
  136.0 25.0 %collective-permute-start.14 = (bf16[1280,128]{0,1:T(8,128)(2,1)S(1)}, bf16[1280,128]{0,1:T(8,128)(2,1)S(1)}, u32[]{:S(2)}, u32[]{:S(2)}) collective-permute-start(bf16[1280,128]{0,1:T(8,128)(2,1)S(1)} %copy-done.10), channel_id=1, source_target_pairs={{0,16},{2,18},{4,20},{6,22},{8,24},{10,26},{12,28},{14,30},{16,0},... | collective-permute-start | bytes 983048 | tf_op jit(solution)/shard_map/ppermute | solution.py:256
  146.5 16.9 %collective-permute-start.11 = (bf16[1280,256]{0,1:T(8,128)(2,1)}, bf16[1280,256]{0,1:T(8,128)(2,1)S(1)}, u32[]{:S(2)}, u32[]{:S(2)}) collective-permute-start(bf16[1280,256]{0,1:T(8,128)(2,1)} %collective-permute-done.10), channel_id=1, source_target_pairs={{0,4},{2,6},{4,0},{6,2},{8,12},{10,14},{12,8},{14,10},{16,20},{18,... | collective-permute-start | bytes 1966088 | tf_op jit(solution)/shard_map/ppermute | solution.py:256
  159.5 13.9 %collective-permute-start.9 = (bf16[512,512]{1,0:T(8,128)(2,1)S(1)}, bf16[512,512]{1,0:T(8,128)(2,1)S(1)}, u32[]{:S(2)}, u32[]{:S(2)}) collective-permute-start(bf16[512,512]{1,0:T(8,128)(2,1)S(1)} %get-tuple-element.77), channel_id=1, source_target_pairs={{0,1},{1,0},{2,3},{3,2},{4,5},{5,4},{6,7},{7,6},{8,9},{9,8},{10,11... | collective-permute-start | bytes 1572872 | tf_op jit(solution)/shard_map/ppermute | solution.py:332
  161.0 9.4 %collective-permute-start.15 = (bf16[1280,128]{0,1:T(8,128)(2,1)S(1)}, bf16[1280,128]{0,1:T(8,128)(2,1)S(1)}, u32[]{:S(2)}, u32[]{:S(2)}) collective-permute-start(bf16[1280,128]{0,1:T(8,128)(2,1)S(1)} %collective-permute-done.14), channel_id=1, source_target_pairs={{0,4},{2,6},{4,0},{6,2},{8,12},{10,14},{12,8},{14,10},{16,20},{18,... | collective-permute-start | bytes 983048 | tf_op jit(solution)/shard_map/ppermute | solution.py:256
  163.4 11.4 %collective-permute-start.12 = (bf16[1280,512]{0,1:T(8,128)(2,1)S(1)}, bf16[1280,512]{0,1:T(8,128)(2,1)S(1)}, u32[]{:S(2)}, u32[]{:S(2)}) collective-permute-start(bf16[1280,512]{0,1:T(8,128)(2,1)S(1)} %constant_dynamic-update-slice_fusion.2), channel_id=1, source_target_pairs={{0,2},{2,0},{4,6},{6,4},{8,10},{10,8},{12,14},{14,12},{16,18},{18,... | collective-permute-start | bytes 3932168 | tf_op jit(solution)/shard_map/ppermute | solution.py:256
  170.4 3.3 %collective-permute-start.16 = (bf16[1280,256]{0,1:T(8,128)(2,1)S(1)}, bf16[1280,256]{0,1:T(8,128)(2,1)S(1)}, u32[]{:S(2)}, u32[]{:S(2)}) collective-permute-start(bf16[1280,256]{0,1:T(8,128)(2,1)S(1)} %constant_dynamic-update-slice_fusion.4), channel_id=1, source_target_pairs={{0,2},{2,0},{4,6},{6,4},{8,10},{10,8},{12,14},{14,12},{16,18},{18,... | collective-permute-start | bytes 1966088 | tf_op jit(solution)/shard_map/ppermute | solution.py:256
  173.6 7.4 %collective-permute-start.18 = (bf16[256,512]{1,0:T(8,128)(2,1)S(1)}, bf16[256,512]{1,0:T(8,128)(2,1)S(1)}, u32[]{:S(2)}, u32[]{:S(2)}) collective-permute-start(bf16[256,512]{1,0:T(8,128)(2,1)S(1)} %slice.213), channel_id=1, source_target_pairs={{0,8},{2,10},{4,12},{6,14},{8,0},{10,2},{12,4},{14,6},{16,24},{18,... | collective-permute-start | bytes 786440 | tf_op jit(solution)/shard_map/ppermute | solution.py:256
  178.2 9.5 %collective-permute-start.17 = (bf16[512,256]{1,0:T(8,128)(2,1)}, bf16[512,256]{1,0:T(8,128)(2,1)S(1)}, u32[]{:S(2)}, u32[]{:S(2)}) collective-permute-start(bf16[512,256]{1,0:T(8,128)(2,1)} %broadcast_select_fusion.6), channel_id=1, source_target_pairs={{0,1},{1,0},{2,3},{3,2},{4,5},{5,4},{6,7},{7,6},{8,9},{9,8},{10,11... | collective-permute-start | bytes 786440 | tf_op jit(solution)/shard_map/ppermute | solution.py:332
  179.8 17.2 %collective-permute-start.13 = (bf16[512,512]{1,0:T(8,128)(2,1)}, bf16[512,512]{1,0:T(8,128)(2,1)S(1)}, u32[]{:S(2)}, u32[]{:S(2)}) collective-permute-start(bf16[512,512]{1,0:T(8,128)(2,1)} %get-tuple-element.79), channel_id=1, source_target_pairs={{0,1},{1,0},{2,3},{3,2},{4,5},{5,4},{6,7},{7,6},{8,9},{9,8},{10,11... | collective-permute-start | bytes 1572872 | tf_op jit(solution)/shard_map/ppermute | solution.py:332
  187.7 5.0 %collective-permute-start.20 = (bf16[256,256]{1,0:T(8,128)(2,1)S(1)}, bf16[256,256]{1,0:T(8,128)(2,1)S(1)}, u32[]{:S(2)}, u32[]{:S(2)}) collective-permute-start(bf16[256,256]{1,0:T(8,128)(2,1)S(1)} %slice.214), channel_id=1, source_target_pairs={{0,8},{2,10},{4,12},{6,14},{8,0},{10,2},{12,4},{14,6},{16,24},{18,... | collective-permute-start | bytes 393224 | tf_op jit(solution)/shard_map/ppermute | solution.py:256
  197.2 6.5 %collective-permute-start.19 = (bf16[256,512]{1,0:T(8,128)(2,1)S(1)}, bf16[256,512]{1,0:T(8,128)(2,1)S(1)}, u32[]{:S(2)}, u32[]{:S(2)}) collective-permute-start(bf16[256,512]{1,0:T(8,128)(2,1)S(1)} %slice.212), channel_id=1, source_target_pairs={{0,8},{2,10},{4,12},{6,14},{8,0},{10,2},{12,4},{14,6},{16,24},{18,... | collective-permute-start | bytes 786440 | tf_op jit(solution)/shard_map/ppermute | solution.py:256
  206.5 3.6 %collective-permute-start.21 = (f32[2,256]{1,0:T(2,128)S(1)}, f32[2,256]{1,0:T(2,128)S(1)}, u32[]{:S(2)}, u32[]{:S(2)}) collective-permute-start(f32[2,256]{1,0:T(2,128)S(1)} %pad_maximum_fusion.5), channel_id=1, source_target_pairs={{0,1},{1,0},{2,3},{3,2},{4,5},{5,4},{6,7},{7,6},{8,9},{9,8},{10,11... | collective-permute-start | bytes 6152 | tf_op jit(solution)/shard_map/ppermute | solution.py:410
  (15 other events, 67.0 us)

commit v5 on v4

--- a/solution.py
+++ b/solution.py
@@ -329,10 +329,17 @@
         sent = jnp.where(own_early, late_part, early_part)
         if j == 0:
             first_sent = sent
-        received = lax.ppermute(sent, "tp", [(0, 1), (1, 0)])
-        total = kept.astype(jnp.float32) + received.astype(jnp.float32)
-        own_parts.append(total[:tokens])
-        near_parts.append(swap(total[tokens:].astype(jnp.bfloat16), Z1).astype(jnp.float32))
+        if j == 1:
+            near_sum, own_sum = [
+                kept[part].astype(jnp.float32)
+                + lax.ppermute(sent[part], "tp", [(0, 1), (1, 0)]).astype(jnp.float32)
+                for part in (slice(tokens, None), slice(0, tokens))
+            ]
+        else:
+            total = kept.astype(jnp.float32) + lax.ppermute(sent, "tp", [(0, 1), (1, 0)]).astype(jnp.float32)
+            own_sum, near_sum = total[:tokens], total[tokens:]
+        own_parts.append(own_sum)
+        near_parts.append(swap(near_sum.astype(jnp.bfloat16), Z1).astype(jnp.float32))
 
     def ordered(parts):
         this = jnp.concatenate([p[:, : p.shape[1] // 2] for p in parts], axis=1)

time: 214 us -> 227 us (1.061)
  waiting for transfers between devices: 96.2 us -> 101 us
  local copies, waits for them, and re-layouts: 17.5 us -> 22 us
  matrix products: 14.6 us -> 18.1 us
    dot_general x10, matrix products: 14.6 us -> 18.1 us  [partial_product(): return jnp.dot(rows, weights, preferred_element_type=jnp.float32)]
    slice x4, local copies, waits for them, and re-layouts: 0.09 us -> 3.52 us  [planes_projection(): e[:, first:first + size]]
    ppermute x3 -> x4, waiting for transfers between devices: 13.5 us -> 16.4 us  [the longest x2 8.49 us: planes_projection(): lax.ppermute(sent, 'tp', [(0, 1), (1, 0)]).astype(jnp.float32)]
    ppermute x17, starting transfers between devices: 25.3 us -> 22.3 us  [swap(): return lax.ppermute(x, 'req', [(i, i ^ bits) for i in range(size)])]
    ppermute x3 -> x4, starting transfers between devices: 3.62 us -> 5.18 us  [the longest x2 3.09 us: planes_projection(): lax.ppermute(sent, 'tp', [(0, 1), (1, 0)]).astype(jnp.float32)]
    unnamed x46 -> x60, local copies, waits for them, and re-layouts: 9.32 us -> 10.6 us
  transfers between devices with their start and end apart: 23 -> 24, of which waited for: 16 -> 15; matrix products, arithmetic and copies ran while one was open for 15% -> 17% of each run, Pallas kernels for 12% -> 12%
where the time goes in v5:
time: 227 us; the launch traced here: 226 us
  waiting for transfers between devices  101 us (44%)
  starting transfers between devices  38.2 us (17%)
  Pallas kernels  30.8 us (14%)
  local copies, waits for them, and re-layouts  22 us (10%)
  matrix products  18.1 us (8%)
  other arithmetic  13.1 us (6%)
    ppermute x17, waiting for transfers between devices, swap(): return lax.ppermute(x, 'req', [(i, i ^ bits) for i in range(size)])  64 us
    ppermute x17, starting transfers between devices, swap(): return lax.ppermute(x, 'req', [(i, i ^ bits) for i in range(size)])  22.3 us
    all_to_all x1, waiting for transfers between devices, shards(): lax.all_to_all(packed, 'req', split_axis=0, concat_axis=0, tiled=True)  18.9 us
    dot_general x10, matrix products, partial_product(): return jnp.dot(rows, weights, preferred_element_type=jnp.float32)  18.1 us
    pallas_call x1, Pallas kernels, local_attention(): pl.pallas_call(functools.partial(local_kernel, group), out_shape=[jax.Sha...  11 us
    unnamed x60, local copies, waits for them, and re-layouts  10.6 us
    ppermute x2, waiting for transfers between devices, planes_projection(): lax.ppermute(sent, 'tp', [(0, 1), (1, 0)]).astype(jnp.float32)  8.49 us
    ppermute x2, waiting for transfers between devices, planes_projection(): lax.ppermute(sent[part], 'tp', [(0, 1), (1, 0)]).astype(jnp.float32)  7.96 us
  transfers between devices with their start and end apart: 24, of which 15 were waited for; matrix products, arithmetic and copies ran while one was open for 17% of the time, Pallas kernels for 12%

profile of v5, /device:TPU:0, one launch (start us, length us, event | category | flops | bytes accessed | tf_op | source)
XLA Modules:
  0.0 225.5 jit_solution(10294150775182018083)
XLA Ops:
  2.0 4.4 %pack_pages.1 = bf16[32,2,8,2560]{3,2,1,0:T(8,128)(2,1)} custom-call(s32[16,1]{1,0:T(8,128)} %copy.27.dest_ref, s32[1,16]{1,0:T(1,128)} %page_ref.1, bf16[64,8,2560]{2,1,0:T(8,128)(2,1)} %keys_ref.3, bf16[64,8,2560]{2,1,0:T(8,128)(2,1)} %values_ref.3), custom_call_target="tpu_custom_call" | custom-call | flops 1 | bytes 1 | tf_op jit(solution)/shard_map/pack_pages/pallas_call | solution.py:67
  6.4 7.6 %all-to-all-start = ((bf16[32,2,8,2560]{3,2,1,0:T(8,128)(2,1)}), bf16[32,2,8,2560]{3,2,1,0:T(8,128)(2,1)}, u32[]{:S(2)}, u32[]{:S(2)}) async-start(bf16[32,2,8,2560]{3,2,1,0:T(8,128)(2,1)} %pack_pages.1), calls=%async_computation | async-start | bytes 5242880 | tf_op jit(solution)/shard_map/all_to_all | solution.py:381
  22.3 3.2 %maximum_select_fusion.1 = bf16[1280,640]{0,1:T(8,128)(2,1)} fusion(bf16[1280,320]{0,1:T(8,128)(2,1)} %collective-permute-done.1, bf16[1280,320]{0,1:T(8,128)(2,1)S(1)} %get-tuple-element.41, pred[]{:T(512)S(6)} %eq.23), kind=kLoop, calls=%fused_computation.17 | loop fusion | flops 7372800 | bytes 3276801 | tf_op jit(solution)/shard_map/jit(_where)/select_n | solution.py:288
  29.7 5.7 %resident_pages.1 = (bf16[48,8,2560]{2,1,0:T(8,128)(2,1)}, bf16[48,8,2560]{2,1,0:T(8,128)(2,1)}) custom-call(s32[48]{0:T(128)} %bitcast.39, bf16[64,8,2560]{2,1,0:T(8,128)(2,1)} %keys_ref.3, bf16[64,8,2560]{2,1,0:T(8,128)(2,1)} %values_ref.3), custom_call_target="tpu_custom_call" | custom-call | flops 1 | bytes 1 | tf_op jit(solution)/shard_map/resident_pages/pallas_call | solution.py:100
  37.8 4.1 %cross_attention.1 = bf16[256,2560]{1,0:T(8,128)(2,1)} custom-call(bf16[256,2560]{1,0:T(8,128)(2,1)S(1)} %copy-done.1, bf16[128,2560]{1,0:T(8,128)(2,1)S(1)} %copy-done.3, bf16[128,2560]{1,0:T(8,128)(2,1)S(1)} %copy-done.4), custom_call_target="tpu_custom_call" | custom-call | flops 1 | bytes 1 | tf_op jit(solution)/shard_map/cross_attention/pallas_call | solution.py:232
  41.9 11.0 %local_attention.1 = (f32[2560,256]{1,0:T(8,128)}, f32[4,16,256]{2,1,0:T(8,128)S(1)}) custom-call(s32[1]{0:T(128)S(6)} %copy.59.length_ref, bf16[256,2560]{1,0:T(8,128)(2,1)S(1)} %fusion.2.q_ref, bf16[48,8,2560]{2,1,0:T(8,128)(2,1)S(1)} %copy-done, bf16[48,8,2560]{2,1,0:T(8,128)(2,1)} %get-tuple-element.21.rv_ref, bf16[256,2560]{1,0:T(8,128)(2,1)S(1)} %fusion.5.k_ref, ...), custom_call_target="tpu_custom_call" | custom-call | flops 1 | bytes 1 | tf_op jit(solution)/shard_map/local_attention/pallas_call | solution.py:185
  56.8 2.8 %collective-permute-start.6 = (bf16[1280,256]{0,1:T(8,128)(2,1)}, bf16[1280,256]{0,1:T(8,128)(2,1)}, u32[]{:S(2)}, u32[]{:S(2)}) collective-permute-start(bf16[1280,256]{0,1:T(8,128)(2,1)} %get-tuple-element.28), channel_id=1, source_target_pairs={{0,16},{2,18},{4,20},{6,22},{8,24},{10,26},{12,28},{14,30},{16,0},... | collective-permute-start | bytes 1966088 | tf_op jit(solution)/shard_map/ppermute | solution.py:256
  59.6 18.9 %all-to-all-done.arrived_ref = bf16[32,2,8,2560]{3,2,1,0:T(8,128)(2,1)} async-done(((bf16[32,2,8,2560]{3,2,1,0:T(8,128)(2,1)}), bf16[32,2,8,2560]{3,2,1,0:T(8,128)(2,1)}, u32[]{:S(2)}, u32[]{:S(2)}) %all-to-all-start) | async-done | bytes 2621472 | tf_op jit(solution)/shard_map/all_to_all | solution.py:381
  79.9 5.5 %arrived_attention.1 = bf16[256,2560]{1,0:T(8,128)(2,1)S(1)} custom-call(f32[256,256]{1,0:T(8,128)S(1)} %broadcast_in_dim.8.usable_ref, bf16[256,2560]{1,0:T(8,128)(2,1)S(1)} %fusion.2.q_ref, bf16[32,2,8,2560]{3,2,1,0:T(8,128)(2,1)} %all-to-all-done.arrived_ref, f32[2560,256]{1,0:T(8,128)} %get-tuple-element.24.sum_ref, ...), custom_call_target="tpu_custom_call" | custom-call | flops 1 | bytes 1 | tf_op jit(solution)/shard_map/arrived_attention/pallas_call | solution.py:208
  85.4 9.2 %collective-permute-start.2 = (bf16[256,2560]{1,0:T(8,128)(2,1)S(1)}, bf16[256,2560]{1,0:T(8,128)(2,1)}, u32[]{:S(2)}, u32[]{:S(2)}) collective-permute-start(bf16[256,2560]{1,0:T(8,128)(2,1)S(1)} %arrived_attention.1), channel_id=1, source_target_pairs={{0,8},{2,10},{4,12},{6,14},{8,0},{10,2},{12,4},{14,6},{16,24},{18,... | collective-permute-start | bytes 3932168 | tf_op jit(solution)/shard_map/ppermute | solution.py:256
  94.6 8.1 %collective-permute-done.6 = bf16[1280,256]{0,1:T(8,128)(2,1)} collective-permute-done((bf16[1280,256]{0,1:T(8,128)(2,1)}, bf16[1280,256]{0,1:T(8,128)(2,1)}, u32[]{:S(2)}, u32[]{:S(2)}) %collective-permute-start.6) | collective-permute-done | bytes 655392 | tf_op jit(solution)/shard_map/ppermute | solution.py:256
  105.4 13.7 %collective-permute-done.7 = bf16[1280,256]{0,1:T(8,128)(2,1)S(1)} collective-permute-done((bf16[1280,256]{0,1:T(8,128)(2,1)}, bf16[1280,256]{0,1:T(8,128)(2,1)S(1)}, u32[]{:S(2)}, u32[]{:S(2)}) %collective-permute-start.7) | collective-permute-done | bytes 655392 | tf_op jit(solution)/shard_map/ppermute | solution.py:256
  119.2 16.8 %collective-permute-done.10 = bf16[1280,256]{0,1:T(8,128)(2,1)} collective-permute-done((bf16[1280,256]{0,1:T(8,128)(2,1)S(1)}, bf16[1280,256]{0,1:T(8,128)(2,1)}, u32[]{:S(2)}, u32[]{:S(2)}) %collective-permute-start.10) | collective-permute-done | bytes 655392 | tf_op jit(solution)/shard_map/ppermute | solution.py:256
  136.0 3.5 %collective-permute-start.14 = (bf16[1280,128]{0,1:T(8,128)(2,1)S(1)}, bf16[1280,128]{0,1:T(8,128)(2,1)S(1)}, u32[]{:S(2)}, u32[]{:S(2)}) collective-permute-start(bf16[1280,128]{0,1:T(8,128)(2,1)S(1)} %copy-done.14), channel_id=1, source_target_pairs={{0,16},{2,18},{4,20},{6,22},{8,24},{10,26},{12,28},{14,30},{16,0},... | collective-permute-start | bytes 983048 | tf_op jit(solution)/shard_map/ppermute | solution.py:256
  139.5 7.1 %collective-permute-done.2 = bf16[256,2560]{1,0:T(8,128)(2,1)} collective-permute-done((bf16[256,2560]{1,0:T(8,128)(2,1)S(1)}, bf16[256,2560]{1,0:T(8,128)(2,1)}, u32[]{:S(2)}, u32[]{:S(2)}) %collective-permute-start.2) | collective-permute-done | bytes 1310752 | tf_op jit(solution)/shard_map/ppermute | solution.py:256
  148.6 3.1 %fusion.23 = f32[512,640]{1,0:T(8,128)S(1)} fusion(bf16[512,1280]{1,0:T(8,128)(2,1)S(1)} %get-tuple-element.38, bf16[1280,640]{0,1:T(8,128)(2,1)} %collective-permute-done.3), kind=kOutput, calls=%fused_computation.98 | convolution fusion | flops 838860800 | bytes 4259840 | tf_op jit(solution)/shard_map/dot_general | solution.py:260
  158.4 2.7 %fusion.9 = bf16[512,640]{1,0:T(8,128)(2,1)S(1)} fusion(f32[512,640]{1,0:T(8,128)S(1)} %fusion.24, bf16[512,1280]{1,0:T(8,128)(2,1)S(1)} %get-tuple-element.37, bf16[1280,640]{0,1:T(8,128)(2,1)} %collective-permute-done.4), kind=kOutput, calls=%fused_computation.23 | convolution fusion | flops 839516160 | bytes 4915200 | tf_op jit(solution)/shard_map/dot_general | solution.py:260
  168.2 6.4 %collective-permute-done.15 = bf16[1280,128]{0,1:T(8,128)(2,1)S(1)} collective-permute-done((bf16[1280,128]{0,1:T(8,128)(2,1)S(1)}, bf16[1280,128]{0,1:T(8,128)(2,1)S(1)}, u32[]{:S(2)}, u32[]{:S(2)}) %collective-permute-start.15) | collective-permute-done | bytes 327712 | tf_op jit(solution)/shard_map/ppermute | solution.py:256
  174.7 2.9 %collective-permute-done.9 = bf16[512,512]{1,0:T(8,128)(2,1)S(1)} collective-permute-done((bf16[512,512]{1,0:T(8,128)(2,1)S(1)}, bf16[512,512]{1,0:T(8,128)(2,1)S(1)}, u32[]{:S(2)}, u32[]{:S(2)}) %collective-permute-start.9) | collective-permute-done | bytes 524320 | tf_op jit(solution)/shard_map/ppermute | solution.py:339
  180.9 4.3 %collective-permute-done.18 = bf16[256,512]{1,0:T(8,128)(2,1)S(1)} collective-permute-done((bf16[256,512]{1,0:T(8,128)(2,1)S(1)}, bf16[256,512]{1,0:T(8,128)(2,1)S(1)}, u32[]{:S(2)}, u32[]{:S(2)}) %collective-permute-start.18) | collective-permute-done | bytes 262176 | tf_op jit(solution)/shard_map/ppermute | solution.py:256
  195.8 5.6 %collective-permute-done.17 = bf16[512,256]{1,0:T(8,128)(2,1)S(1)} collective-permute-done((bf16[512,256]{1,0:T(8,128)(2,1)S(1)}, bf16[512,256]{1,0:T(8,128)(2,1)S(1)}, u32[]{:S(2)}, u32[]{:S(2)}) %collective-permute-start.17) | collective-permute-done | bytes 262176 | tf_op jit(solution)/shard_map/ppermute | solution.py:339
  201.9 5.1 %collective-permute-done.13 = bf16[256,512]{1,0:T(8,128)(2,1)S(1)} collective-permute-done((bf16[256,512]{1,0:T(8,128)(2,1)S(1)}, bf16[256,512]{1,0:T(8,128)(2,1)S(1)}, u32[]{:S(2)}, u32[]{:S(2)}) %collective-permute-start.13) | collective-permute-done | bytes 262176 | tf_op jit(solution)/shard_map/ppermute | solution.py:335
  207.1 2.8 %collective-permute-done.19 = bf16[256,512]{1,0:T(8,128)(2,1)S(1)} collective-permute-done((bf16[256,512]{1,0:T(8,128)(2,1)S(1)}, bf16[256,512]{1,0:T(8,128)(2,1)S(1)}, u32[]{:S(2)}, u32[]{:S(2)}) %collective-permute-start.19) | collective-permute-done | bytes 262176 | tf_op jit(solution)/shard_map/ppermute | solution.py:335
  210.9 5.6 %collective-permute-done.20 = bf16[256,512]{1,0:T(8,128)(2,1)S(1)} collective-permute-done((bf16[256,512]{1,0:T(8,128)(2,1)S(1)}, bf16[256,512]{1,0:T(8,128)(2,1)S(1)}, u32[]{:S(2)}, u32[]{:S(2)}) %collective-permute-start.20) | collective-permute-done | bytes 262176 | tf_op jit(solution)/shard_map/ppermute | solution.py:256
  (144 shorter events, 63.4 us)
Async XLA Ops:
  6.4 72.0 %all-to-all-start = ((bf16[32,2,8,2560]{3,2,1,0:T(8,128)(2,1)}), bf16[32,2,8,2560]{3,2,1,0:T(8,128)(2,1)}, u32[]{:S(2)}, u32[]{:S(2)}) async-start(bf16[32,2,8,2560]{3,2,1,0:T(8,128)(2,1)} %pack_pages.1), calls=%async_computation | async-start | bytes 5242880 | tf_op jit(solution)/shard_map/all_to_all | solution.py:381
  15.7 4.7 %collective-permute-start = (f32[2,256]{1,0:T(2,128)S(1)}, f32[2,256]{1,0:T(2,128)S(1)}, u32[]{:S(2)}, u32[]{:S(2)}) collective-permute-start(f32[2,256]{1,0:T(2,128)S(1)} %pad_maximum_fusion.4), channel_id=1, source_target_pairs={{0,1},{1,0},{2,3},{3,2},{4,5},{5,4},{6,7},{7,6},{8,9},{9,8},{10,11... | collective-permute-start | bytes 6152 | tf_op jit(solution)/shard_map/ppermute | solution.py:246
  19.6 2.7 %collective-permute-start.1 = (bf16[1280,320]{0,1:T(8,128)(2,1)}, bf16[1280,320]{0,1:T(8,128)(2,1)}, u32[]{:S(2)}, u32[]{:S(2)}) collective-permute-start(bf16[1280,320]{0,1:T(8,128)(2,1)} %get-tuple-element.42), channel_id=1, source_target_pairs={{0,2},{2,0},{4,6},{6,4},{8,10},{10,8},{12,14},{14,12},{16,18},{18,... | collective-permute-start | bytes 2457608 | tf_op jit(solution)/shard_map/ppermute | solution.py:256
  52.9 3.8 %collective-permute-start.3 = (bf16[1280,640]{0,1:T(8,128)(2,1)}, bf16[1280,640]{0,1:T(8,128)(2,1)}, u32[]{:S(2)}, u32[]{:S(2)}) collective-permute-start(bf16[1280,640]{0,1:T(8,128)(2,1)} %maximum_select_fusion.1), channel_id=1, source_target_pairs={{0,2},{2,0},{4,6},{6,4},{8,10},{10,8},{12,14},{14,12},{16,18},{18,... | collective-permute-start | bytes 4915208 | tf_op jit(solution)/shard_map/ppermute | solution.py:256
  53.2 50.9 %collective-permute-start.4 = (bf16[1280,640]{0,1:T(8,128)(2,1)}, bf16[1280,640]{0,1:T(8,128)(2,1)}, u32[]{:S(2)}, u32[]{:S(2)}) collective-permute-start(bf16[1280,640]{0,1:T(8,128)(2,1)} %maximum_select_fusion.1), channel_id=1, source_target_pairs={{0,4},{2,6},{4,0},{6,2},{8,12},{10,14},{12,8},{14,10},{16,20},{18,... | collective-permute-start | bytes 4915208 | tf_op jit(solution)/shard_map/ppermute | solution.py:256
  56.8 45.9 %collective-permute-start.6 = (bf16[1280,256]{0,1:T(8,128)(2,1)}, bf16[1280,256]{0,1:T(8,128)(2,1)}, u32[]{:S(2)}, u32[]{:S(2)}) collective-permute-start(bf16[1280,256]{0,1:T(8,128)(2,1)} %get-tuple-element.28), channel_id=1, source_target_pairs={{0,16},{2,18},{4,20},{6,22},{8,24},{10,26},{12,28},{14,30},{16,0},... | collective-permute-start | bytes 1966088 | tf_op jit(solution)/shard_map/ppermute | solution.py:256
  85.4 61.2 %collective-permute-start.2 = (bf16[256,2560]{1,0:T(8,128)(2,1)S(1)}, bf16[256,2560]{1,0:T(8,128)(2,1)}, u32[]{:S(2)}, u32[]{:S(2)}) collective-permute-start(bf16[256,2560]{1,0:T(8,128)(2,1)S(1)} %arrived_attention.1), channel_id=1, source_target_pairs={{0,8},{2,10},{4,12},{6,14},{8,0},{10,2},{12,4},{14,6},{16,24},{18,... | collective-permute-start | bytes 3932168 | tf_op jit(solution)/shard_map/ppermute | solution.py:256
  102.7 16.4 %collective-permute-start.7 = (bf16[1280,256]{0,1:T(8,128)(2,1)}, bf16[1280,256]{0,1:T(8,128)(2,1)S(1)}, u32[]{:S(2)}, u32[]{:S(2)}) collective-permute-start(bf16[1280,256]{0,1:T(8,128)(2,1)} %collective-permute-done.6), channel_id=1, source_target_pairs={{0,4},{2,6},{4,0},{6,2},{8,12},{10,14},{12,8},{14,10},{16,20},{18,... | collective-permute-start | bytes 1966088 | tf_op jit(solution)/shard_map/ppermute | solution.py:256
  104.1 31.9 %collective-permute-start.10 = (bf16[1280,256]{0,1:T(8,128)(2,1)S(1)}, bf16[1280,256]{0,1:T(8,128)(2,1)}, u32[]{:S(2)}, u32[]{:S(2)}) collective-permute-start(bf16[1280,256]{0,1:T(8,128)(2,1)S(1)} %copy-done.11), channel_id=1, source_target_pairs={{0,16},{2,18},{4,20},{6,22},{8,24},{10,26},{12,28},{14,30},{16,0},... | collective-permute-start | bytes 1966088 | tf_op jit(solution)/shard_map/ppermute | solution.py:256
  104.1 53.0 %collective-permute-start.5 = (bf16[1280,640]{0,1:T(8,128)(2,1)}, bf16[1280,640]{0,1:T(8,128)(2,1)S(1)}, u32[]{:S(2)}, u32[]{:S(2)}) collective-permute-start(bf16[1280,640]{0,1:T(8,128)(2,1)} %collective-permute-done.4), channel_id=1, source_target_pairs={{0,2},{2,0},{4,6},{6,4},{8,10},{10,8},{12,14},{14,12},{16,18},{18,... | collective-permute-start | bytes 4915208 | tf_op jit(solution)/shard_map/ppermute | solution.py:256
  119.2 42.7 %collective-permute-start.8 = (bf16[1280,512]{0,1:T(8,128)(2,1)S(1)}, bf16[1280,512]{0,1:T(8,128)(2,1)S(1)}, u32[]{:S(2)}, u32[]{:S(2)}) collective-permute-start(bf16[1280,512]{0,1:T(8,128)(2,1)S(1)} %constant_dynamic-update-slice_fusion), channel_id=1, source_target_pairs={{0,2},{2,0},{4,6},{6,4},{8,10},{10,8},{12,14},{14,12},{16,18},{18,... | collective-permute-start | bytes 3932168 | tf_op jit(solution)/shard_map/ppermute | solution.py:256
  136.0 29.2 %collective-permute-start.14 = (bf16[1280,128]{0,1:T(8,128)(2,1)S(1)}, bf16[1280,128]{0,1:T(8,128)(2,1)S(1)}, u32[]{:S(2)}, u32[]{:S(2)}) collective-permute-start(bf16[1280,128]{0,1:T(8,128)(2,1)S(1)} %copy-done.14), channel_id=1, source_target_pairs={{0,16},{2,18},{4,20},{6,22},{8,24},{10,26},{12,28},{14,30},{16,0},... | collective-permute-start | bytes 983048 | tf_op jit(solution)/shard_map/ppermute | solution.py:256
  146.6 20.6 %collective-permute-start.11 = (bf16[1280,256]{0,1:T(8,128)(2,1)}, bf16[1280,256]{0,1:T(8,128)(2,1)S(1)}, u32[]{:S(2)}, u32[]{:S(2)}) collective-permute-start(bf16[1280,256]{0,1:T(8,128)(2,1)} %collective-permute-done.10), channel_id=1, source_target_pairs={{0,4},{2,6},{4,0},{6,2},{8,12},{10,14},{12,8},{14,10},{16,20},{18,... | collective-permute-start | bytes 1966088 | tf_op jit(solution)/shard_map/ppermute | solution.py:256
  163.6 13.9 %collective-permute-start.9 = (bf16[512,512]{1,0:T(8,128)(2,1)S(1)}, bf16[512,512]{1,0:T(8,128)(2,1)S(1)}, u32[]{:S(2)}, u32[]{:S(2)}) collective-permute-start(bf16[512,512]{1,0:T(8,128)(2,1)S(1)} %get-tuple-element.83), channel_id=1, source_target_pairs={{0,1},{1,0},{2,3},{3,2},{4,5},{5,4},{6,7},{7,6},{8,9},{9,8},{10,11... | collective-permute-start | bytes 1572872 | tf_op jit(solution)/shard_map/ppermute | solution.py:339
  165.2 9.4 %collective-permute-start.15 = (bf16[1280,128]{0,1:T(8,128)(2,1)S(1)}, bf16[1280,128]{0,1:T(8,128)(2,1)S(1)}, u32[]{:S(2)}, u32[]{:S(2)}) collective-permute-start(bf16[1280,128]{0,1:T(8,128)(2,1)S(1)} %collective-permute-done.14), channel_id=1, source_target_pairs={{0,4},{2,6},{4,0},{6,2},{8,12},{10,14},{12,8},{14,10},{16,20},{18,... | collective-permute-start | bytes 983048 | tf_op jit(solution)/shard_map/ppermute | solution.py:256
  168.1 19.4 %collective-permute-start.12 = (bf16[1280,512]{0,1:T(8,128)(2,1)}, bf16[1280,512]{0,1:T(8,128)(2,1)}, u32[]{:S(2)}, u32[]{:S(2)}) collective-permute-start(bf16[1280,512]{0,1:T(8,128)(2,1)} %constant_dynamic-update-slice_fusion.2), channel_id=1, source_target_pairs={{0,2},{2,0},{4,6},{6,4},{8,10},{10,8},{12,14},{14,12},{16,18},{18,... | collective-permute-start | bytes 3932168 | tf_op jit(solution)/shard_map/ppermute | solution.py:256
  174.6 10.7 %collective-permute-start.16 = (bf16[1280,256]{0,1:T(8,128)(2,1)S(1)}, bf16[1280,256]{0,1:T(8,128)(2,1)}, u32[]{:S(2)}, u32[]{:S(2)}) collective-permute-start(bf16[1280,256]{0,1:T(8,128)(2,1)S(1)} %constant_dynamic-update-slice_fusion.4), channel_id=1, source_target_pairs={{0,2},{2,0},{4,6},{6,4},{8,10},{10,8},{12,14},{14,12},{16,18},{18,... | collective-permute-start | bytes 1966088 | tf_op jit(solution)/shard_map/ppermute | solution.py:256
  177.8 7.4 %collective-permute-start.18 = (bf16[256,512]{1,0:T(8,128)(2,1)S(1)}, bf16[256,512]{1,0:T(8,128)(2,1)S(1)}, u32[]{:S(2)}, u32[]{:S(2)}) collective-permute-start(bf16[256,512]{1,0:T(8,128)(2,1)S(1)} %slice.224), channel_id=1, source_target_pairs={{0,8},{2,10},{4,12},{6,14},{8,0},{10,2},{12,4},{14,6},{16,24},{18,... | collective-permute-start | bytes 786440 | tf_op jit(solution)/shard_map/ppermute | solution.py:256
  192.1 9.3 %collective-permute-start.17 = (bf16[512,256]{1,0:T(8,128)(2,1)S(1)}, bf16[512,256]{1,0:T(8,128)(2,1)S(1)}, u32[]{:S(2)}, u32[]{:S(2)}) collective-permute-start(bf16[512,256]{1,0:T(8,128)(2,1)S(1)} %broadcast_select_fusion.7), channel_id=1, source_target_pairs={{0,1},{1,0},{2,3},{3,2},{4,5},{5,4},{6,7},{7,6},{8,9},{9,8},{10,11... | collective-permute-start | bytes 786440 | tf_op jit(solution)/shard_map/ppermute | solution.py:339
  193.7 13.3 %collective-permute-start.13 = (bf16[256,512]{1,0:T(8,128)(2,1)S(1)}, bf16[256,512]{1,0:T(8,128)(2,1)S(1)}, u32[]{:S(2)}, u32[]{:S(2)}) collective-permute-start(bf16[256,512]{1,0:T(8,128)(2,1)S(1)} %get-tuple-element.64), channel_id=1, source_target_pairs={{0,1},{1,0},{2,3},{3,2},{4,5},{5,4},{6,7},{7,6},{8,9},{9,8},{10,11... | collective-permute-start | bytes 786440 | tf_op jit(solution)/shard_map/ppermute | solution.py:335
  194.3 15.6 %collective-permute-start.19 = (bf16[256,512]{1,0:T(8,128)(2,1)S(1)}, bf16[256,512]{1,0:T(8,128)(2,1)S(1)}, u32[]{:S(2)}, u32[]{:S(2)}) collective-permute-start(bf16[256,512]{1,0:T(8,128)(2,1)S(1)} %get-tuple-element.63), channel_id=1, source_target_pairs={{0,1},{1,0},{2,3},{3,2},{4,5},{5,4},{6,7},{7,6},{8,9},{9,8},{10,11... | collective-permute-start | bytes 786440 | tf_op jit(solution)/shard_map/ppermute | solution.py:335
  201.6 9.3 %collective-permute-start.21 = (bf16[256,256]{1,0:T(8,128)(2,1)S(1)}, bf16[256,256]{1,0:T(8,128)(2,1)S(1)}, u32[]{:S(2)}, u32[]{:S(2)}) collective-permute-start(bf16[256,256]{1,0:T(8,128)(2,1)S(1)} %slice.225), channel_id=1, source_target_pairs={{0,8},{2,10},{4,12},{6,14},{8,0},{10,2},{12,4},{14,6},{16,24},{18,... | collective-permute-start | bytes 393224 | tf_op jit(solution)/shard_map/ppermute | solution.py:256
  210.0 6.4 %collective-permute-start.20 = (bf16[256,512]{1,0:T(8,128)(2,1)S(1)}, bf16[256,512]{1,0:T(8,128)(2,1)S(1)}, u32[]{:S(2)}, u32[]{:S(2)}) collective-permute-start(bf16[256,512]{1,0:T(8,128)(2,1)S(1)} %get-tuple-element.61), channel_id=1, source_target_pairs={{0,8},{2,10},{4,12},{6,14},{8,0},{10,2},{12,4},{14,6},{16,24},{18,... | collective-permute-start | bytes 786440 | tf_op jit(solution)/shard_map/ppermute | solution.py:256
  219.3 3.6 %collective-permute-start.22 = (f32[2,256]{1,0:T(2,128)S(1)}, f32[2,256]{1,0:T(2,128)S(1)}, u32[]{:S(2)}, u32[]{:S(2)}) collective-permute-start(f32[2,256]{1,0:T(2,128)S(1)} %pad_maximum_fusion.5), channel_id=1, source_target_pairs={{0,1},{1,0},{2,3},{3,2},{4,5},{5,4},{6,7},{7,6},{8,9},{9,8},{10,11... | collective-permute-start | bytes 6152 | tf_op jit(solution)/shard_map/ppermute | solution.py:417
  (23 other events, 126.5 us)
